TPU v7x, 128 devices: a whole 4x4x4 slice. The times are simulated.
128 devices in a mesh: dp: 8 (over y, x_lo), chan: 16 (over x_hi, z, core).
Axes of the slice: x: 4 (x_hi: 2, x_lo: 2; x = x_hi * 2 + x_lo), y: 4, z: 4, core: 2. Of those that a mesh axis runs over, the one named last changes fastest.
Arguments:
- tokens: int32 [2, 128], P(None, 'dp'), may hold values from 0 to 511
- parents: int32 [2, 128], replicated, may hold values from 0 to 127, as said below
- embed_table: bfloat16 [512, 8192], P(None, 'chan'), may hold values from -5 to 5
- norm_gain: float32 [2, 8192], P(None, 'chan'), may hold values from 0.1 to 1.9
- weight_in: bfloat16 [2, 16, 8, 3, 64, 8192], P(None, None, 'dp', None, None, 'chan'), may hold values from -0.0625 to 0.0625
- weight_out: bfloat16 [2, 16, 8, 64, 8192], P(None, None, 'dp', None, 'chan'), may hold values from -0.0625 to 0.0625
- fir_filters: float32 [512, 128], P('chan'), may hold values from -0.6 to 0.6
- mode_poles: float32 [16, 8192], P(None, 'chan'), may hold values from 0.3 to 0.99
- residues: float32 [16, 8192], P(None, 'chan'), may hold values from -1.5 to 1.5
- fir_cache: bfloat16 [128, 127, 8192], P('dp', None, 'chan'), may hold values from -6 to 6
- modal_state: float32 [128, 16, 8192], P('dp', None, 'chan'), may hold values from -12 to 12
Outputs:
- hidden_out: bfloat16 [2, 128, 8192], P(None, 'dp', 'chan')
- fir_next: bfloat16 [128, 127, 8192], P('dp', None, 'chan')
- state_next: float32 [128, 16, 8192], P('dp', None, 'chan')
Inputs may be any that keep to these rules, and one draw needn't show every extreme that they name: `parents`: beams 2 * 16 * q to 2 * 16 * q + 2 * 16 - 1 form request q; at every step each beam's parent is a beam of its own request.
All inputs are finite; a program needn't handle non-finite values.
Results may differ from a plain program's by a relative error of at most 0.02.
Values may be sent and summed in bfloat16 or wider, within the bound.
No kernel may reach another device: no remote copies, remote signals or barrier semaphores. Data moves between devices by JAX's collectives and lax.ppermute only.
A program may use at most 128 MiB of HBM per device.

v0:
```python
import jax
import jax.numpy as jnp
from jax import lax
from jax.sharding import PartitionSpec as P

D = 8192
GROUP = 16
STEPS = 2


EPSILON = 1e-05


def partner(value, axis, apart):
    mask = 2**apart
    pairs = [(source, source ^ mask) for source in range(lax.axis_size(axis))]
    return lax.ppermute(value, axis, pairs)


def select_rows(wanted, own_rows, partner_rows, own_start, partner_start):
    count_rows = own_rows.shape[0]
    slot_ids = jnp.arange(count_rows, dtype=jnp.int32)
    mask_own = (wanted[:, None] == own_start + slot_ids[None, :]).astype(own_rows.dtype)
    mask_partner = (wanted[:, None] == partner_start + slot_ids[None, :]).astype(own_rows.dtype)
    flat_own = own_rows.reshape(count_rows, -1)
    flat_partner = partner_rows.reshape(count_rows, -1)
    picked = jnp.dot(
        mask_own, flat_own, preferred_element_type=jnp.float32, precision=lax.Precision.HIGHEST
    )
    picked = picked + jnp.dot(
        mask_partner,
        flat_partner,
        preferred_element_type=jnp.float32,
        precision=lax.Precision.HIGHEST,
    )
    return picked.reshape((wanted.shape[0],) + own_rows.shape[1:]).astype(own_rows.dtype)


def norm_rows(hidden_in, gain_row):
    values = hidden_in.astype(jnp.float32)
    local_sums = jnp.sum(values * values, axis=1)
    totals = lax.psum(local_sums, "chan")
    scaled = values * lax.rsqrt(totals[:, None] / D + EPSILON) * gain_row[None, :]
    return scaled.astype(jnp.bfloat16)


def project(rows_in, weight_block, kind_count):
    all_rows = lax.all_gather(rows_in, "dp", axis=0, tiled=True)
    flat_weight = weight_block.reshape(weight_block.shape[0], -1, weight_block.shape[-1])
    whole_terms = jnp.einsum(
        "bc,jnc->jbn", all_rows, flat_weight, preferred_element_type=jnp.float32
    )
    totals = lax.psum(whole_terms, "chan")
    own_block = lax.dynamic_index_in_dim(totals, lax.axis_index("chan"), 0, keepdims=False)
    rounded = own_block.astype(jnp.bfloat16).reshape(all_rows.shape[0], kind_count, -1)
    return lax.all_to_all(rounded, "dp", split_axis=0, concat_axis=2, tiled=True)


def fir_mix(tap_rows, cache_rows, product_kv):
    filtered = tap_rows[0][None, :] * product_kv.astype(jnp.float32)
    filtered = filtered + jnp.sum(cache_rows.astype(jnp.float32) * tap_rows[1:][None], axis=1)
    updated = jnp.concatenate([product_kv[:, None, :], cache_rows[:, :-1]], axis=1)
    return (filtered, updated)


def modal_mix(mode_poles, residues, state_rows, product_kv):
    updated = mode_poles[None] * state_rows + product_kv.astype(jnp.float32)[:, None, :]
    return (jnp.sum(residues[None] * updated, axis=1), updated)


def hyena_block(hidden_in, gain_row, weight_in_block, weight_out_block, mixing):
    normed = norm_rows(hidden_in, gain_row)
    features = project(normed, weight_in_block, 3)
    product_kv = (features[:, 1].astype(jnp.float32) * features[:, 2].astype(jnp.float32)).astype(
        jnp.bfloat16
    )
    filtered, memory = mixing(product_kv)
    gated_rows = (features[:, 0].astype(jnp.float32) * filtered).astype(jnp.bfloat16)
    outward = project(gated_rows, weight_out_block, 1)[:, 0]
    return (
        (hidden_in.astype(jnp.float32) + outward.astype(jnp.float32)).astype(jnp.bfloat16),
        memory,
    )


def local(
    tokens,
    parents,
    embed_table,
    norm_gain,
    weight_in,
    weight_out,
    fir_filters,
    mode_poles,
    residues,
    fir_cache,
    modal_state,
):
    beam_dev = fir_cache.shape[0]
    group_index = lax.axis_index("dp")
    own_start = group_index * beam_dev
    partner_start = jnp.bitwise_xor(group_index, 1) * beam_dev
    tap_rows = jnp.repeat(fir_filters, GROUP, axis=0).T
    vocab_ids = jnp.arange(embed_table.shape[0], dtype=jnp.int32)
    local_parents = lax.dynamic_slice_in_dim(parents, own_start, beam_dev, 1)
    cache_now = fir_cache
    state_now = modal_state
    outputs = []
    for step_index in range(STEPS):
        partner_cache = partner(cache_now, "dp", 0)
        partner_state = partner(state_now, "dp", 0)
        wanted = local_parents[step_index]
        cache_now = select_rows(wanted, cache_now, partner_cache, own_start, partner_start)
        state_now = select_rows(wanted, state_now, partner_state, own_start, partner_start)
        onehot = (tokens[step_index][:, None] == vocab_ids[None, :]).astype(jnp.bfloat16)
        hidden_now = jnp.dot(onehot, embed_table, preferred_element_type=jnp.float32).astype(
            jnp.bfloat16
        )

        def finite_part(product_kv, cache_rows=cache_now):
            return fir_mix(tap_rows, cache_rows, product_kv)

        hidden_now, cache_now = hyena_block(
            hidden_now, norm_gain[0], weight_in[0], weight_out[0], finite_part
        )

        def modal_part(product_kv, state_rows=state_now):
            return modal_mix(mode_poles, residues, state_rows, product_kv)

        hidden_now, state_now = hyena_block(
            hidden_now, norm_gain[1], weight_in[1], weight_out[1], modal_part
        )
        outputs.append(hidden_now)
    return (jnp.stack(outputs), cache_now, state_now)


def solution(mesh):
    return jax.shard_map(
        local,
        mesh=mesh,
        in_specs=(
            P(None, "dp"),
            P(),
            P(None, "chan"),
            P(None, "chan"),
            P(None, None, "dp", None, None, "chan"),
            P(None, None, "dp", None, "chan"),
            P("chan", None),
            P(None, "chan"),
            P(None, "chan"),
            P("dp", None, "chan"),
            P("dp", None, "chan"),
        ),
        out_specs=(P(None, "dp", "chan"), P("dp", None, "chan"), P("dp", None, "chan")),
        check_vma=False,
    )
```

profile of v0, /device:TPU:1, one launch (start us, length us, event | category | flops | bytes accessed | tf_op | source)
XLA Modules:
  0.0 837.5 jit_solution(11023228450754467506)
XLA Ops:
  0.6 2.1 collective-permute-start
  5.5 73.1 %all-reduce.5 = (f32[16]{0:T(128)S(1)}, f32[16]{0:T(128)S(1)}) all-reduce(f32[16]{0:T(128)S(1)} %get-tuple-element.48, f32[16]{0:T(128)S(1)} %get-tuple-element.50), channel_id=1, replica_groups=mesh['dp'=8,'chan'=16] {'chan'}, use_global_device_ids=true, to_apply=%region_1.0 | all-reduce | flops 32 | bytes 256 | tf_op jit(solution)/shard_map/psum | solution.py:42
  78.7 22.4 %all_gather.28 = bf16[128,512]{1,0:T(8,128)(2,1)S(1)} all-gather(bf16[16,512]{1,0:T(8,128)(2,1)S(1)} %get-tuple-element.42), channel_id=1, replica_groups=mesh['dp'=8,'chan'=16] {'dp'}, dimensions={0}, use_global_device_ids=true | all-gather | bytes 147456 | tf_op jit(solution)/shard_map/all_gather | solution.py:48
  101.2 21.9 %all_gather.24 = bf16[128,512]{1,0:T(8,128)(2,1)S(1)} all-gather(bf16[16,512]{1,0:T(8,128)(2,1)S(1)} %get-tuple-element.43), channel_id=1, replica_groups=mesh['dp'=8,'chan'=16] {'dp'}, dimensions={0}, use_global_device_ids=true | all-gather | bytes 147456 | tf_op jit(solution)/shard_map/all_gather | solution.py:48
  123.1 3.5 fusion.74
  126.6 2.2 convolution_bitcast_fusion.1
  128.7 2.1 convolution_bitcast_fusion.3
  130.8 87.8 %all-reduce.10 = (bf16[16,128,192]{1,2,0:T(8,128)(2,1)}, bf16[16,128,192]{1,2,0:T(8,128)(2,1)}) all-reduce(f32[16,128,192]{1,2,0:T(8,128)} %convolution_bitcast_fusion.3, f32[16,128,192]{1,2,0:T(8,128)} %convolution_bitcast_fusion.1), channel_id=1, replica_groups=mesh['dp'=8,'chan'=16] {'chan'}, use_global_device_ids=true, to_apply=%region_2.0 | all-reduce | flops 786432 | bytes 4718592 | tf_op jit(solution)/shard_map/psum | solution.py:53
  220.3 3.7 all-to-all-start
  224.0 3.1 copy.108
  227.7 4.3 fusion.55
  232.4 1.9 copy.109
  235.1 2.1 fusion
  237.2 3.3 convert_element_type.321
  240.5 2.5 pad_maximum_fusion
  243.0 2.5 copy.95
  248.6 5.1 all-to-all-start.4
  259.7 40.1 %all-to-all-done.4 = bf16[8,2,1536]{2,1,0:T(2,128)(2,1)} async-done(((bf16[8,2,1536]{2,1,0:T(2,128)(2,1)}), bf16[8,2,1536]{2,1,0:T(2,128)(2,1)}, u32[]{:S(2)}, u32[]{:S(2)}) %all-to-all-start.4) | async-done | bytes 49184 | tf_op jit(solution)/shard_map/all_to_all | solution.py:56
  300.9 1.5 copy.112
  307.0 1.7 copy.110
  308.7 2.1 fusion.1
  310.8 3.3 convert_element_type.361
  314.1 3.3 multiply_reduce_fusion
  317.4 21.9 %all_gather.29 = bf16[128,512]{1,0:T(8,128)(2,1)S(1)} all-gather(bf16[16,512]{1,0:T(8,128)(2,1)S(1)} %get-tuple-element.33), channel_id=1, replica_groups=mesh['dp'=8,'chan'=16] {'dp'}, dimensions={0}, use_global_device_ids=true | all-gather | bytes 147456 | tf_op jit(solution)/shard_map/all_gather | solution.py:48
  339.4 22.3 %all_gather.25 = bf16[128,512]{1,0:T(8,128)(2,1)S(1)} all-gather(bf16[16,512]{1,0:T(8,128)(2,1)S(1)} %get-tuple-element.41), channel_id=1, replica_groups=mesh['dp'=8,'chan'=16] {'dp'}, dimensions={0}, use_global_device_ids=true | all-gather | bytes 147456 | tf_op jit(solution)/shard_map/all_gather | solution.py:48
  364.1 92.6 %all-reduce.11 = (bf16[16,128,64]{1,2,0:T(8,128)(2,1)}, bf16[16,128,64]{1,2,0:T(8,128)(2,1)}) all-reduce(f32[16,128,64]{1,2,0:T(8,128)} %convolution_bitcast_fusion.7, f32[16,128,64]{1,2,0:T(8,128)} %convolution_bitcast_fusion.5), channel_id=1, replica_groups=mesh['dp'=8,'chan'=16] {'chan'}, use_global_device_ids=true, to_apply=%region_4.5 | all-reduce | flops 262144 | bytes 1572864 | tf_op jit(solution)/shard_map/psum | solution.py:53
  459.5 3.3 all-to-all-start.5
  465.1 2.7 all-to-all-done.5
  467.8 3.3 all-to-all-start.1
  471.5 4.6 all-to-all-done.1
  476.5 41.1 %all-reduce.2 = (f32[16]{0:T(128)S(1)}, f32[16]{0:T(128)S(1)}) all-reduce(f32[16]{0:T(128)S(1)} %get-tuple-element.31, f32[16]{0:T(128)S(1)} %get-tuple-element.29), channel_id=1, replica_groups=mesh['dp'=8,'chan'=16] {'chan'}, use_global_device_ids=true, to_apply=%region_6.7 | all-reduce | flops 32 | bytes 256 | tf_op jit(solution)/shard_map/psum | solution.py:42
  517.7 22.3 %all_gather.30 = bf16[128,512]{1,0:T(8,128)(2,1)S(1)} all-gather(bf16[16,512]{1,0:T(8,128)(2,1)S(1)} %get-tuple-element.39), channel_id=1, replica_groups=mesh['dp'=8,'chan'=16] {'dp'}, dimensions={0}, use_global_device_ids=true | all-gather | bytes 147456 | tf_op jit(solution)/shard_map/all_gather | solution.py:48
  540.0 22.2 %all_gather.26 = bf16[128,512]{1,0:T(8,128)(2,1)S(1)} all-gather(bf16[16,512]{1,0:T(8,128)(2,1)S(1)} %get-tuple-element.40), channel_id=1, replica_groups=mesh['dp'=8,'chan'=16] {'dp'}, dimensions={0}, use_global_device_ids=true | all-gather | bytes 147456 | tf_op jit(solution)/shard_map/all_gather | solution.py:48
  562.1 2.1 convolution_bitcast_fusion.2
  564.3 2.1 convolution_bitcast_fusion
  566.4 87.7 %all-reduce.12 = (bf16[16,128,192]{1,2,0:T(8,128)(2,1)}, bf16[16,128,192]{1,2,0:T(8,128)(2,1)}) all-reduce(f32[16,128,192]{1,2,0:T(8,128)} %convolution_bitcast_fusion.2, f32[16,128,192]{1,2,0:T(8,128)} %convolution_bitcast_fusion), channel_id=1, replica_groups=mesh['dp'=8,'chan'=16] {'chan'}, use_global_device_ids=true, to_apply=%region_7.8 | all-reduce | flops 786432 | bytes 4718592 | tf_op jit(solution)/shard_map/psum | solution.py:53
  656.0 3.6 all-to-all-start.2
  661.2 3.2 all-to-all-done.2
  664.4 3.3 all-to-all-start.6
  671.2 2.5 copy.107
  675.2 2.1 collective-permute-done.3
  679.3 22.7 %all_gather.27 = bf16[128,512]{1,0:T(8,128)(2,1)S(1)} all-gather(bf16[16,512]{1,0:T(8,128)(2,1)S(1)} %fusion.30), channel_id=1, replica_groups=mesh['dp'=8,'chan'=16] {'dp'}, dimensions={0}, use_global_device_ids=true | all-gather | bytes 147456 | tf_op jit(solution)/shard_map/all_gather | solution.py:48
  701.9 22.0 %all_gather.31 = bf16[128,512]{1,0:T(8,128)(2,1)S(1)} all-gather(bf16[16,512]{1,0:T(8,128)(2,1)S(1)} %fusion.26), channel_id=1, replica_groups=mesh['dp'=8,'chan'=16] {'dp'}, dimensions={0}, use_global_device_ids=true | all-gather | bytes 147456 | tf_op jit(solution)/shard_map/all_gather | solution.py:48
  725.6 91.3 %all-reduce.13 = (bf16[16,128,64]{1,2,0:T(8,128)(2,1)S(1)}, bf16[16,128,64]{1,2,0:T(8,128)(2,1)S(1)}) all-reduce(f32[16,128,64]{1,2,0:T(8,128)S(1)} %convolution_bitcast_fusion.4, f32[16,128,64]{1,2,0:T(8,128)} %convolution_bitcast_fusion.6), channel_id=1, replica_groups=mesh['dp'=8,'chan'=16] {'chan'}, use_global_device_ids=true, to_apply=%region_19.20 | all-reduce | flops 262144 | bytes 1572864 | tf_op jit(solution)/shard_map/psum | solution.py:53
  818.5 4.8 all-to-all-start.3
  824.8 3.5 all-to-all-done.3
  828.3 3.3 all-to-all-start.7
  831.9 4.7 all-to-all-done.7
  (185 shorter events, 45.5 us)
Async XLA Ops:
  0.6 4.2 copy-start
  0.6 231.7 %collective-permute-start = (bf16[16,127,512]{2,0,1:T(8,128)(2,1)}, bf16[16,127,512]{2,0,1:T(8,128)(2,1)}, u32[]{:S(2)}, u32[]{:S(2)}) collective-permute-start(bf16[16,127,512]{2,0,1:T(8,128)(2,1)} %param.20), channel_id=1, source_target_pairs={{0,16},{16,0},{32,48},{48,32},{64,80},{80,64},{96,112},{112,96},{1... | collective-permute-start | bytes 6242312 | tf_op jit(solution)/shard_map/ppermute | solution.py:17
  5.2 96.0 %copy-start.17 = (f32[16,512]{1,0:T(8,128)}, f32[16,512]{1,0:T(8,128)S(1)}, u32[]{:S(2)}) copy-start(f32[16,512]{1,0:T(8,128)S(1)} %get-tuple-element.51) | copy-start | bytes 98308
  5.5 95.6 %copy-start.15 = (f32[16,512]{1,0:T(8,128)}, f32[16,512]{1,0:T(8,128)S(1)}, u32[]{:S(2)}) copy-start(f32[16,512]{1,0:T(8,128)S(1)} %get-tuple-element.49) | copy-start | bytes 98308
  220.3 11.6 %all-to-all-start = ((bf16[8,2,1536]{2,1,0:T(2,128)(2,1)}), bf16[8,2,1536]{2,1,0:T(2,128)(2,1)S(1)}, u32[]{:S(2)}, u32[]{:S(2)}) async-start(bf16[8,2,1536]{2,1,0:T(2,128)(2,1)} %reshape.211), calls=%async_computation | async-start | bytes 98304 | tf_op jit(solution)/shard_map/all_to_all | solution.py:56
  224.0 3.1 copy-start.30
  227.1 28.0 %copy-start.28 = (s32[16]{0:T(128)}, s32[16]{0:T(128)S(1)}, u32[]{:S(2)}) copy-start(s32[16]{0:T(128)S(1)} %iota_add_fusion.1) | copy-start | bytes 196
  227.7 27.4 %copy-start.22 = (s32[16]{0:T(128)}, s32[16]{0:T(128)S(1)}, u32[]{:S(2)}) copy-start(s32[16]{0:T(128)S(1)} %get-tuple-element.45) | copy-start | bytes 196
  232.0 2.3 copy-start.25
  232.3 2.0 copy-start.11
  232.3 2.8 copy-start.5
  243.0 4.8 copy-start.3
  245.4 10.9 %copy-start.21 = (f32[32,128]{1,0:T(8,128)S(1)}, f32[32,128]{1,0:T(8,128)}, u32[]{:S(2)}) copy-start(f32[32,128]{1,0:T(8,128)} %param.17) | copy-start | bytes 49156
  245.4 12.5 %copy-start.13 = (f32[16,512]{1,0:T(8,128)S(1)}, f32[16,512]{1,0:T(8,128)}, u32[]{:S(2)}) copy-start(f32[16,512]{1,0:T(8,128)} %param.18) | copy-start | bytes 98308
  245.4 61.5 %collective-permute-start.2 = (bf16[16,127,512]{2,0,1:T(8,128)(2,1)}, bf16[16,127,512]{2,0,1:T(8,128)(2,1)}, u32[]{:S(2)}, u32[]{:S(2)}) collective-permute-start(bf16[16,127,512]{2,0,1:T(8,128)(2,1)} %copy.95), channel_id=1, source_target_pairs={{0,16},{16,0},{32,48},{48,32},{64,80},{80,64},{96,112},{112,96},{1... | collective-permute-start | bytes 6242312 | tf_op jit(solution)/shard_map/ppermute | solution.py:17
  246.9 54.0 %collective-permute-start.1 = (f32[16,16,512]{2,1,0:T(8,128)}, f32[16,16,512]{2,1,0:T(8,128)}, u32[]{:S(2)}, u32[]{:S(2)}) collective-permute-start(f32[16,16,512]{2,1,0:T(8,128)} %param.21), channel_id=1, source_target_pairs={{0,16},{16,0},{32,48},{48,32},{64,80},{80,64},{96,112},{112,96},{1... | collective-permute-start | bytes 1572872 | tf_op jit(solution)/shard_map/ppermute | solution.py:17
  248.6 51.1 %all-to-all-start.4 = ((bf16[8,2,1536]{2,1,0:T(2,128)(2,1)}), bf16[8,2,1536]{2,1,0:T(2,128)(2,1)}, u32[]{:S(2)}, u32[]{:S(2)}) async-start(bf16[8,2,1536]{2,1,0:T(2,128)(2,1)} %reshape.217), calls=%async_computation.4 | async-start | bytes 98304 | tf_op jit(solution)/shard_map/all_to_all | solution.py:56
  300.9 4.1 copy-start.4
  303.9 1.1 copy-start.9
  305.0 1.2 copy-start.23
  305.0 1.2 copy-start.29
  306.9 1.7 copy-start.26
  314.1 3.3 copy-start.12
  314.1 3.3 copy-start.24
  314.1 47.6 %copy-start.6 = (bf16[2,16,1,64,512]{4,3,2,1,0:T(8,128)(2,1)S(1)}, bf16[2,16,1,64,512]{4,3,2,1,0:T(8,128)(2,1)}, u32[]{:S(2)}) copy-start(bf16[2,16,1,64,512]{4,3,2,1,0:T(8,128)(2,1)} %param.16) | copy-start | bytes 6291460
  362.8 108.6 %copy-start.18 = (f32[16,512]{1,0:T(8,128)S(1)}, f32[16,512]{1,0:T(8,128)}, u32[]{:S(2)}) copy-start(f32[16,512]{1,0:T(8,128)} %copy-done.17) | copy-start | bytes 98308
  362.9 113.6 %copy-start.16 = (f32[16,512]{1,0:T(8,128)S(1)}, f32[16,512]{1,0:T(8,128)}, u32[]{:S(2)}) copy-start(f32[16,512]{1,0:T(8,128)} %copy-done.15) | copy-start | bytes 98308
  362.9 154.8 %copy-start.27 = (f32[1,512]{1,0:T(1,128)S(1)}, f32[1,512]{1,0:T(1,128)}, u32[]{:S(2)}) copy-start(f32[1,512]{1,0:T(1,128)} %get-tuple-element.37) | copy-start | bytes 6148
  459.5 8.3 all-to-all-start.5
  467.8 8.3 all-to-all-start.1
  566.4 101.7 %copy-start.8 = (f32[2,8,16,512]{3,2,1,0:T(8,128)S(1)}, f32[2,8,16,512]{3,2,1,0:T(8,128)}, u32[]{:S(2)}) copy-start(f32[2,8,16,512]{3,2,1,0:T(8,128)} %copy.113) | copy-start | bytes 1572868
  566.4 101.7 %copy-start.14 = (f32[16,512]{1,0:T(8,128)S(1)}, f32[16,512]{1,0:T(8,128)}, u32[]{:S(2)}) copy-start(f32[16,512]{1,0:T(8,128)} %param.18) | copy-start | bytes 98308
  654.1 16.2 %copy-start.2 = (bf16[16,127,512]{2,1,0:T(8,128)(2,1)S(1)}, bf16[16,127,512]{2,1,0:T(8,128)(2,1)}, u32[]{:S(2)}) copy-start(bf16[16,127,512]{2,1,0:T(8,128)(2,1)} %convert_element_type.361) | copy-start | bytes 6242308
  656.0 8.4 %all-to-all-start.2 = ((bf16[8,2,1536]{2,1,0:T(2,128)(2,1)}), bf16[8,2,1536]{2,1,0:T(2,128)(2,1)S(1)}, u32[]{:S(2)}, u32[]{:S(2)}) async-start(bf16[8,2,1536]{2,1,0:T(2,128)(2,1)} %reshape.215), calls=%async_computation.2 | async-start | bytes 98304 | tf_op jit(solution)/shard_map/all_to_all | solution.py:56
  664.4 9.3 %all-to-all-start.6 = ((bf16[8,2,1536]{2,1,0:T(2,128)(2,1)}), bf16[8,2,1536]{2,1,0:T(2,128)(2,1)S(1)}, u32[]{:S(2)}, u32[]{:S(2)}) async-start(bf16[8,2,1536]{2,1,0:T(2,128)(2,1)} %reshape.221), calls=%async_computation.6 | async-start | bytes 98304 | tf_op jit(solution)/shard_map/all_to_all | solution.py:56
  669.0 8.2 collective-permute-start.3
  673.7 1.0 copy-start.10
  673.7 1.0 copy-start.19
  675.1 3.1 copy-start.20
  677.5 46.4 %copy-start.7 = (bf16[2,16,1,64,512]{4,3,2,1,0:T(8,128)(2,1)S(1)}, bf16[2,16,1,64,512]{4,3,2,1,0:T(8,128)(2,1)}, u32[]{:S(2)}) copy-start(bf16[2,16,1,64,512]{4,3,2,1,0:T(8,128)(2,1)} %param.16) | copy-start | bytes 6291460
  723.9 113.6 %copy-start.1 = (bf16[512,512]{1,0:T(8,128)(2,1)S(1)}, bf16[512,512]{1,0:T(8,128)(2,1)}, u32[]{:S(2)}) copy-start(bf16[512,512]{1,0:T(8,128)(2,1)} %param.13) | copy-start | bytes 1572868
  818.5 9.8 %all-to-all-start.3 = ((bf16[8,2,512]{2,1,0:T(2,128)(2,1)}), bf16[8,2,512]{2,1,0:T(2,128)(2,1)S(1)}, u32[]{:S(2)}, u32[]{:S(2)}) async-start(bf16[8,2,512]{2,1,0:T(2,128)(2,1)} %reshape.225), calls=%async_computation.3 | async-start | bytes 32768 | tf_op jit(solution)/shard_map/all_to_all | solution.py:56
  828.3 8.3 all-to-all-start.7
where the time goes:
time: 847 us; the launch traced here: 838 us
  blocking collectives  651 us (77%)
  waiting for transfers between devices  61 us (7%)
  local copies, waits for them, and re-layouts  50.2 us (6%)
  starting transfers between devices  35.5 us (4%)
  matrix products  25.9 us (3%)
  other arithmetic  12.4 us (1%)
    psum x4, blocking collectives, project(): totals = lax.psum(whole_terms, 'chan')  359 us
    all_gather x8, blocking collectives, project(): all_rows = lax.all_gather(rows_in, 'dp', axis=0, tiled=True)  178 us
    psum x2, blocking collectives, norm_rows(): totals = lax.psum(local_sums, 'chan')  114 us
    all_to_all x8, waiting for transfers between devices, project(): lax.all_to_all(rounded, 'dp', split_axis=0, concat_axis=2, tiled=True)  58.9 us
    all_to_all x8, starting transfers between devices, project(): lax.all_to_all(rounded, 'dp', split_axis=0, concat_axis=2, tiled=True)  30.5 us
    unnamed x91, local copies, waits for them, and re-layouts  18.4 us
  transfers between devices with their start and end apart: 12, of which 7 were waited for; matrix products, arithmetic and copies ran while one was open for 6% of the time, Pallas kernels for 0%

commit v1 on v0

v1 whole, which is shorter than its diff:
```python
import jax
import jax.numpy as jnp
from jax import lax
from jax.experimental import pallas as pl
from jax.experimental.pallas import tpu as pltpu
from jax.sharding import Mesh, PartitionSpec as P

D = 8192
EPSILON = 1e-05
BF = jnp.bfloat16
F32 = jnp.float32
I32 = jnp.int32
HIGH = lax.Precision.HIGHEST
DP = ("y", "xl")
CHAN = ("xh", "z", "c")
XZ = ("xh", "z")
VMEM = pl.BlockSpec(memory_space=pltpu.VMEM)
SMEM = pl.BlockSpec(memory_space=pltpu.SMEM)
ANY = pl.BlockSpec(memory_space=pl.ANY)
LIMIT = 24 * 1024 * 1024
EXTRA = 16


def params(**kw):
    return pltpu.CompilerParams(vmem_limit_bytes=LIMIT, **kw)


def swap(value, axis):
    return lax.ppermute(value, axis, [(0, 1), (1, 0)])


def exchange(value, axes):
    return lax.all_to_all(value, axes, 0, 0, tiled=True)


def sums_kernel(filt_ref, poles_ref, res_ref, state_ref, cache_ref, out_ref, tap_a, tap_b, rows):
    step = pl.program_id(0)

    @pl.when(step == 0)
    def _():
        group = lax.broadcasted_iota(I32, (32, 512), 1) // 16
        spread = (group == lax.broadcasted_iota(I32, (32, 512), 0)).astype(F32)
        taps = lax.dot_general(
            filt_ref[...], spread, (((0,), (0,)), ((), ())),
            preferred_element_type=F32, precision=HIGH,
        )
        place = lax.broadcasted_iota(I32, (128, 512), 0)
        tap_a[...] = pltpu.roll(taps, 127, 0)
        tap_b[...] = jnp.where(place < 126, pltpu.roll(taps, 126, 0), 0.0)
        rows[64:128, :] = jnp.zeros((64, 512), F32)
        rows[64:66, :] = taps[0:2, :]
        poles = poles_ref[...]
        once = res_ref[...] * poles
        twice = once * poles
        rows[66:67, :] = jnp.sum(res_ref[...], axis=0, keepdims=True)
        rows[67:68, :] = jnp.sum(once, axis=0, keepdims=True)
        for b in range(16):
            state = state_ref[b]
            rows[32 + b : 33 + b, :] = jnp.sum(state * once, axis=0, keepdims=True)
            rows[48 + b : 49 + b, :] = jnp.sum(state * twice, axis=0, keepdims=True)

    for s in range(4):
        @pl.when(step == s)
        def _(s=s):
            for k in range(4):
                b = 4 * s + k
                past = cache_ref[k].astype(F32)
                rows[b : b + 1, :] = jnp.sum(past * tap_a[0:127, :], axis=0, keepdims=True)
                rows[16 + b : 17 + b, :] = jnp.sum(past * tap_b[0:127, :], axis=0, keepdims=True)

    @pl.when(step == 3)
    def _():
        out_ref[...] = rows[...].T


def make_sums(filters, poles, residues, state, cache):
    whole = lambda *shape: pl.BlockSpec(shape, lambda s: (0,) * len(shape))
    return pl.pallas_call(
        sums_kernel,
        grid=(4,),
        in_specs=[
            whole(32, 128), whole(16, 512), whole(16, 512), whole(16, 16, 512),
            pl.BlockSpec((4, 127, 512), lambda s: (s, 0, 0)),
        ],
        out_specs=whole(512, 128),
        out_shape=jax.ShapeDtypeStruct((512, 128), F32),
        scratch_shapes=[pltpu.VMEM((128, 512), F32)] * 3,
        compiler_params=params(),
        name="state_sums",
    )(filters, poles, residues, state, cache)


def write_squares(x_own, x_oth, squares):
    total = jnp.sum(x_own * x_own, axis=0, keepdims=True)
    total = total + jnp.sum(x_oth * x_oth, axis=0, keepdims=True)
    high = total.astype(BF).astype(F32)
    low = total - high
    place = lax.broadcasted_iota(I32, (EXTRA, 128), 0)
    squares[...] = jnp.where(place == 0, high, jnp.where(place == 1, low, 0.0)).astype(BF)


def product_in(w_own, w_oth, scaled, squares, out_ref):
    acc = jnp.dot(w_own[0], scaled[0], preferred_element_type=F32)
    acc = acc + jnp.dot(w_oth[0], scaled[1], preferred_element_type=F32)
    out_ref[0, 0:384, :] = acc.astype(BF)
    out_ref[0, 384:400, :] = squares[...]


def embed_kernel(tok_ref, e_own, e_oth, g_own, g_oth, w_own, w_oth, out_ref, x_ref, scaled, squares):
    @pl.when(pl.program_id(0) == 0)
    def _():
        vocab = lax.broadcasted_iota(I32, (512, 128), 0)
        onehot = (vocab == tok_ref[0:1, :]).astype(BF)
        halves = []
        for k, (table, gain) in enumerate(((e_own, g_own), (e_oth, g_oth))):
            x = lax.dot_general(
                table[...], onehot, (((0,), (0,)), ((), ())), preferred_element_type=F32
            )
            x_ref[k] = x.astype(BF)
            scaled[k] = (x * gain[:, 0:1]).astype(BF)
            halves.append(x)
        write_squares(halves[0], halves[1], squares)

    product_in(w_own, w_oth, scaled, squares, out_ref)


W_IN_SPECS = lambda block: [pl.BlockSpec((1, 384, 512), lambda g: (block, g, 0))] * 2
IN_SCRATCH = [pltpu.VMEM((2, 512, 128), BF), pltpu.VMEM((EXTRA, 128), BF)]
COST_IN = pl.CostEstimate(flops=2 * 3072 * 1024 * 128, bytes_accessed=7 << 20, transcendentals=0)
COST_OUT = pl.CostEstimate(flops=2 * 1024 * 1024 * 128, bytes_accessed=5 << 19, transcendentals=0)


def project_embed(tok, e_own, e_oth, g_own, g_oth, w_own, w_oth):
    whole = lambda *shape: pl.BlockSpec(shape, lambda g: (0,) * len(shape))
    return pl.pallas_call(
        embed_kernel,
        grid=(8,),
        in_specs=[
            whole(1, 128), whole(512, 512), whole(512, 512), whole(512, 8), whole(512, 8),
            *W_IN_SPECS(0),
        ],
        out_specs=[pl.BlockSpec((1, 400, 128), lambda g: (g, 0, 0)), whole(2, 512, 128)],
        out_shape=[
            jax.ShapeDtypeStruct((8, 400, 128), BF),
            jax.ShapeDtypeStruct((2, 512, 128), BF),
        ],
        scratch_shapes=IN_SCRATCH,
        compiler_params=params(),
        cost_estimate=COST_IN,
        name="embed_project",
    )(tok, e_own, e_oth, g_own, g_oth, w_own, w_oth)


def gather_rows(c, a_ref, k):
    start = pl.multiple_of((c ^ k) * 64, 64)
    return jnp.concatenate([a_ref[i, pl.ds(start, 64), :] for i in range(8)], axis=0)


def in_kernel(c_ref, a_ref, g_own, g_oth, w_own, w_oth, out_ref, scaled, squares):
    @pl.when(pl.program_id(0) == 0)
    def _():
        halves = []
        for k, gain in enumerate((g_own, g_oth)):
            x = gather_rows(c_ref[0], a_ref, k).astype(F32)
            scaled[k] = (x * gain[:, 1:2]).astype(BF)
            halves.append(x)
        write_squares(halves[0], halves[1], squares)

    product_in(w_own, w_oth, scaled, squares, out_ref)


def project_in(where, rows, g_own, g_oth, w_own, w_oth):
    whole = lambda *shape: pl.BlockSpec(shape, lambda g: (0,) * len(shape))
    return pl.pallas_call(
        in_kernel,
        grid=(8,),
        in_specs=[SMEM, whole(8, 128, 128), whole(512, 8), whole(512, 8), *W_IN_SPECS(1)],
        out_specs=pl.BlockSpec((1, 400, 128), lambda g: (g, 0, 0)),
        out_shape=jax.ShapeDtypeStruct((8, 400, 128), BF),
        scratch_shapes=IN_SCRATCH,
        compiler_params=params(),
        cost_estimate=COST_IN,
        name="norm_project",
    )(where, rows, g_own, g_oth, w_own, w_oth)


def mix_kernel(block, c_ref, r_ref, t_own, t_oth, idx_ref, gated_ref, kv_ref):
    c = c_ref[0]
    total = r_ref[0].astype(F32)
    for g in range(1, 8):
        total = total + r_ref[g].astype(F32)
    squares = total[384:385, :] + total[385:386, :]
    feats = (total[0:384, :] * lax.rsqrt(squares / D + EPSILON)).astype(BF).astype(F32)
    kind = lambda m: jnp.concatenate(
        [feats[64 * m : 64 * m + 64, :], feats[192 + 64 * m : 256 + 64 * m, :]], axis=0
    )
    kv = (kind(1) * kind(2)).astype(BF)
    square = lax.broadcasted_iota(I32, (128, 128), 0)
    earlier = (square == idx_ref[2:3, :]).astype(BF)
    onward = (square == idx_ref[3:4, :]).astype(BF)
    kv_before = jnp.dot(kv, earlier, preferred_element_type=F32)
    kv_ref[...] = jnp.dot(kv, onward, preferred_element_type=F32).T.astype(BF)
    parts, first, second = [], [], []
    for k in range(2):
        own = c == k
        acc = jnp.zeros((64, 128), F32)
        for q in range(4):
            sums = jnp.where(own, t_own[q], t_oth[q])
            pick = (square + 128 * q == idx_ref[block : block + 1, :]).astype(F32)
            acc = acc + jnp.dot(sums, pick, preferred_element_type=F32, precision=HIGH)
            if q == 0:
                first.append(sums[:, 64 + 2 * block : 65 + 2 * block])
                second.append(sums[:, 65 + 2 * block : 66 + 2 * block])
        parts.append(acc)
    first, second = jnp.concatenate(first, axis=0), jnp.concatenate(second, axis=0)
    filtered = first * kv.astype(F32) + second * kv_before + jnp.concatenate(parts, axis=0)
    gated = (kind(0) * filtered).astype(BF)
    for i in range(8):
        gated_ref[i] = gated


def mix(block, where, received, t_own, t_oth, idx):
    return pl.pallas_call(
        lambda *refs: mix_kernel(block, *refs),
        in_specs=[SMEM, VMEM, VMEM, VMEM, VMEM],
        out_specs=[VMEM, VMEM],
        out_shape=[
            jax.ShapeDtypeStruct((8, 128, 128), BF),
            jax.ShapeDtypeStruct((128, 128), BF),
        ],
        compiler_params=params(),
        name="mix",
    )(where, received, t_own, t_oth, idx)


def out_kernel(c_ref, a_ref, w_own, w_oth, out_ref, rows):
    @pl.when(pl.program_id(0) == 0)
    def _():
        for k in range(2):
            rows[k] = gather_rows(c_ref[0], a_ref, k)

    acc = jnp.dot(w_own[0], rows[0], preferred_element_type=F32)
    acc = acc + jnp.dot(w_oth[0], rows[1], preferred_element_type=F32)
    for k in range(2):
        out_ref[k] = acc[128 * k : 128 * k + 128, :].astype(BF)


def project_out(block, where, rows, w_own, w_oth):
    whole = lambda *shape: pl.BlockSpec(shape, lambda g: (0,) * len(shape))
    return pl.pallas_call(
        out_kernel,
        grid=(4,),
        in_specs=[SMEM, whole(8, 128, 128)]
        + [pl.BlockSpec((1, 256, 512), lambda g: (block, g, 0))] * 2,
        out_specs=pl.BlockSpec((2, 128, 128), lambda g: (g, 0, 0)),
        out_shape=jax.ShapeDtypeStruct((8, 128, 128), BF),
        scratch_shapes=[pltpu.VMEM((2, 512, 128), BF)],
        compiler_params=params(),
        cost_estimate=COST_OUT,
        name="project_out",
    )(where, rows, w_own, w_oth)


def add_up(r_ref):
    total = r_ref[0].astype(F32)
    for g in range(1, 8):
        total = total + r_ref[g].astype(F32)
    return total.astype(BF).astype(F32)


def residual_kernel(c_ref, r_ref, x_ref, out_ref):
    outward = add_up(r_ref)
    start = pl.multiple_of(c_ref[1] * 64, 64)
    before = jnp.concatenate(
        [x_ref[c_ref[0] ^ k, pl.ds(start, 64), :] for k in range(2)], axis=0
    )
    hidden = (before.astype(F32) + outward).astype(BF)
    for i in range(8):
        out_ref[i] = hidden


def residual(where, received, embedded):
    return pl.pallas_call(
        residual_kernel,
        in_specs=[SMEM, VMEM, VMEM],
        out_specs=VMEM,
        out_shape=jax.ShapeDtypeStruct((8, 128, 128), BF),
        compiler_params=params(),
        name="residual",
    )(where, received, embedded)


def last_kernel(c_ref, r_ref, h_ref, kv0_ref, kv1_ref, keep_ref, send_ref):
    hidden = (h_ref[0].astype(F32) + add_up(r_ref)).astype(BF).astype(F32).T
    first = c_ref[0] == 0
    for k, rows in enumerate((hidden, kv0_ref[...].astype(F32), kv1_ref[...].astype(F32))):
        low, high = rows[:, 0:64], rows[:, 64:128]
        keep_ref[k] = jnp.where(first, low, high).astype(BF)
        send_ref[k] = jnp.where(first, high, low).astype(BF)


def last(where, received, hidden, kv0, kv1):
    whole = lambda *shape: pl.BlockSpec(shape, lambda g: (0,) * len(shape))
    return pl.pallas_call(
        last_kernel,
        grid=(1,),
        in_specs=[
            SMEM, whole(8, 128, 128), pl.BlockSpec((1, 128, 128), lambda g: (0, 0, 0)),
            whole(128, 128), whole(128, 128),
        ],
        out_specs=[whole(3, 128, 64)] * 2,
        out_shape=[jax.ShapeDtypeStruct((3, 128, 64), BF)] * 2,
        compiler_params=params(),
        name="last",
    )(where, received, hidden, kv0, kv1)


def arrange_kernel(c_ref, keep_ref, got_ref, out_ref):
    first = c_ref[0] == 0
    for k in range(3):
        keep, got = keep_ref[k].astype(F32), got_ref[k].astype(F32)
        for half in range(2):
            rows = jnp.where(first == (half == 0), keep, got).astype(BF)
            for q in range(4):
                out_ref[4 * half + q, 32 * k : 32 * k + 32, :] = rows[32 * q : 32 * q + 32, :]


def arrange(where, keep, got):
    return pl.pallas_call(
        arrange_kernel,
        in_specs=[SMEM, VMEM, VMEM],
        out_specs=VMEM,
        out_shape=jax.ShapeDtypeStruct((8, 96, 64), BF),
        compiler_params=params(),
        name="arrange",
    )(where, keep, got)


def reorder_kernel(pick_ref, own_ref, oth_ref, out_ref, held, ready, sem_in, sem_out):
    for b in range(16):
        row = pick_ref[0, b]

        @pl.when(pick_ref[1, b] == 1)
        def _():
            pltpu.make_async_copy(own_ref.at[row], held.at[b], sem_in.at[b]).start()

        @pl.when(pick_ref[1, b] == 0)
        def _():
            pltpu.make_async_copy(oth_ref.at[row], held.at[b], sem_in.at[b]).start()

    for b in range(16):
        pltpu.make_async_copy(own_ref.at[0], held.at[b], sem_in.at[b]).wait()
        past = held[b].astype(F32)
        moved = jnp.concatenate([past[0:2, :], past[0:125, :]], axis=0)
        ready[b] = moved.astype(BF)
        pltpu.make_async_copy(ready.at[b], out_ref.at[b], sem_out.at[b]).start()
    for b in range(16):
        pltpu.make_async_copy(ready.at[b], out_ref.at[b], sem_out.at[b]).wait()


def reorder(pick, own, oth):
    return pl.pallas_call(
        reorder_kernel,
        in_specs=[SMEM, ANY, ANY],
        out_specs=ANY,
        out_shape=jax.ShapeDtypeStruct((16, 127, 512), BF),
        scratch_shapes=[
            pltpu.VMEM((16, 127, 512), BF),
            pltpu.VMEM((16, 127, 512), BF),
            pltpu.SemaphoreType.DMA((16,)),
            pltpu.SemaphoreType.DMA((16,)),
        ],
        compiler_params=params(),
        cost_estimate=pl.CostEstimate(flops=0, bytes_accessed=4 << 20, transcendentals=0),
        name="reorder",
    )(pick, own, oth)


def final_kernel(pick_ref, r_ref, poles_ref, own_ref, oth_ref, fir_ref, hid_ref, fir_out, state_ref):
    wide = lambda start: jnp.concatenate(
        [r_ref[i, start : start + 16, :].astype(F32) for i in range(8)], axis=1
    )
    for t in range(2):
        hid_ref[t] = wide(16 * t).astype(BF)
    before, now = wide(32), wide(48)
    place = lax.broadcasted_iota(I32, (16, 512), 0)
    for b in range(16):
        old = fir_ref[b].astype(F32)
        fresh = jnp.where(place == 0, now[b : b + 1, :], before[b : b + 1, :])
        fir_out[b] = jnp.where(place < 2, fresh, old).astype(BF)
    before, now = wide(64), wide(80)
    poles = poles_ref[...]
    for b in range(16):
        row = pick_ref[0, b]
        old = jnp.where(pick_ref[1, b] == 1, own_ref[row], oth_ref[row])
        state_ref[b] = poles * (poles * old + before[b : b + 1, :]) + now[b : b + 1, :]


def final(pick, received, poles, own, oth, fir):
    whole = lambda *shape: pl.BlockSpec(shape, lambda g: (0,) * len(shape))
    return pl.pallas_call(
        final_kernel,
        grid=(1,),
        in_specs=[
            SMEM, whole(8, 96, 64), whole(16, 512), whole(16, 16, 512), whole(16, 16, 512),
            whole(16, 16, 512),
        ],
        out_specs=[whole(2, 16, 512), whole(16, 16, 512), whole(16, 16, 512)],
        out_shape=[
            jax.ShapeDtypeStruct((2, 16, 512), BF),
            jax.ShapeDtypeStruct((16, 127, 512), BF),
            jax.ShapeDtypeStruct((16, 16, 512), F32),
        ],
        input_output_aliases={5: 1},
        compiler_params=params(),
        name="final",
    )(pick, received, poles, own, oth, fir)


def indices(parents, dp, c):
    beams = jnp.arange(128, dtype=I32)
    composed = jnp.sum(
        jnp.where(parents[1][None, :] == beams[:, None], parents[0][:, None], 0), axis=0
    )
    chosen = jnp.stack([parents[0], parents[1], composed])
    mine = lax.dynamic_slice_in_dim(composed, dp * 16, 16, 0)
    pick = jnp.stack([mine % 16, (mine // 16 == dp).astype(I32)])
    half = lax.dynamic_slice_in_dim(chosen, c * 64, 64, 1) - c * 64
    p0, p1, pp = half[0].reshape(4, 16), half[1].reshape(4, 16), half[2].reshape(4, 16)
    sums_row = lambda beam, kind: beam // 16 * 128 + kind * 16 + beam % 16
    column = lambda beam, t: beam // 16 * 32 + t * 16 + beam % 16
    both = lambda a, b: jnp.stack([a, b], axis=1).reshape(128)
    here = jnp.arange(64, dtype=I32).reshape(4, 16)
    rows = [
        both(sums_row(p0, 0), sums_row(pp, 1)),
        both(sums_row(p0, 2), sums_row(pp, 3)),
        both(jnp.full_like(p1, -1), column(p1, 0)),
        both(column(p1, 0), column(here, 1)),
    ]
    return jnp.stack(rows + [rows[0]] * 4), pick


def local(
    tokens, parents, embed_table, norm_gain, weight_in, weight_out, fir_filters, mode_poles,
    residues, fir_cache, modal_state,
):
    dp = lax.axis_index(DP).astype(I32)
    c = lax.axis_index("c").astype(I32)
    where = jnp.stack([c, dp])
    w_in = weight_in.reshape(2, 3072, 512)
    w_out = weight_out.reshape(2, 1024, 512)

    slot = (jnp.arange(4, dtype=I32) == dp % 4).astype(I32)
    row = (slot[:, None] * tokens.reshape(1, 32)).reshape(1, 128)
    got = exchange(jnp.broadcast_to(row[None], (8, 1, 128)), DP)
    tok = jnp.sum(lax.dynamic_slice_in_dim(got, c * 4, 4, 0), axis=0)

    gains = jnp.concatenate([norm_gain, jnp.zeros((6, 512), F32)], axis=0)
    e_oth = swap(embed_table, "c")
    g_own = gains.T
    g_oth = swap(g_own, "c")
    w_in_oth = swap(w_in, "c")
    w_out_oth = swap(w_out, "c")
    cache_oth = swap(fir_cache, "xl")
    state_oth = swap(modal_state, "xl")
    idx, pick = indices(parents, dp, c)

    sums = make_sums(fir_filters, mode_poles, residues, modal_state, fir_cache)
    sums = exchange(sums.reshape(8, 64, 128), DP)
    t_own = lax.dynamic_slice_in_dim(sums, c * 4, 4, 0)
    t_oth = swap(lax.dynamic_slice_in_dim(sums, 4 - c * 4, 4, 0), "c")

    partial, embedded = project_embed(tok, embed_table, e_oth, g_own, g_oth, w_in, w_in_oth)
    gated, kv0 = mix(0, where, exchange(partial, XZ), t_own, t_oth, idx)
    partial = project_out(0, where, exchange(gated, DP), w_out, w_out_oth)
    hidden = residual(where, exchange(partial, XZ), embedded)
    partial = project_in(where, exchange(hidden, DP), g_own, g_oth, w_in, w_in_oth)
    gated, kv1 = mix(1, where, exchange(partial, XZ), t_own, t_oth, idx)
    partial = project_out(1, where, exchange(gated, DP), w_out, w_out_oth)
    keep, send = last(where, exchange(partial, XZ), hidden, kv0, kv1)
    moved = exchange(arrange(where, keep, swap(send, "c")), DP)
    fir_before = reorder(pick, fir_cache, cache_oth)
    return final(pick, moved, mode_poles, modal_state, state_oth, fir_before)


def solution(mesh):
    fine = Mesh(mesh.devices.reshape(4, 2, 2, 4, 2), ("y", "xl", "xh", "z", "c"))
    return jax.shard_map(
        local,
        mesh=fine,
        in_specs=(
            P(None, DP),
            P(),
            P(None, CHAN),
            P(None, CHAN),
            P(None, None, DP, None, None, CHAN),
            P(None, None, DP, None, CHAN),
            P(CHAN, None),
            P(None, CHAN),
            P(None, CHAN),
            P(DP, None, CHAN),
            P(DP, None, CHAN),
        ),
        out_specs=(P(None, DP, CHAN), P(DP, None, CHAN), P(DP, None, CHAN)),
        check_vma=False,
    )
```

time: 847 us -> 207 us (0.24)
  blocking collectives: 651 us -> 77.8 us
  waiting for transfers between devices: 61 us -> 21.5 us
  Pallas kernels: 0 us -> 35.8 us
  matrix products: 25.9 us -> 0 us
  local copies, waits for them, and re-layouts: 50.2 us -> 26.1 us
  other arithmetic: 12.4 us -> 1.31 us
    psum x6 -> x0, blocking collectives: 474 us -> none  [the longest x4 359 us: project(): totals = lax.psum(whole_terms, 'chan')]
    all_gather x8 -> x0, blocking collectives: 178 us -> none  [project(): all_rows = lax.all_gather(rows_in, 'dp', axis=0, tiled=True)]
    all_to_all x0 -> x4, blocking collectives: none -> 77.8 us  [exchange(): return lax.all_to_all(value, axes, 0, 0, tiled=True)]
    all_to_all x8 -> x6, waiting for transfers between devices: 58.9 us -> 19.9 us  [exchange(): return lax.all_to_all(value, axes, 0, 0, tiled=True)]
    pallas_call x0 -> x12, Pallas kernels: none -> 35.8 us  [the longest x1 7.2 us: reorder(): pl.pallas_call(reorder_kernel, in_specs=[SMEM, ANY, ANY], out_specs=ANY,...]
    dot_general x18 -> x0, matrix products: 25.9 us -> none  [the longest x8 12.7 us: project(): jnp.einsum('bc,jnc->jbn', all_rows, flat_weight, preferred_element_type=j...]
    convert_element_type x25 -> x0, local copies, waits for them, and re-layouts: 13 us -> none  [the longest x2 6.59 us: select_rows(): picked.reshape((wanted.shape[0],) + own_rows.shape[1:])]
    unnamed x91 -> x38, local copies, waits for them, and re-layouts: 18.4 us -> 15.2 us
  transfers between devices with their start and end apart: 12 -> 14, of which waited for: 7 -> 5; matrix products, arithmetic and copies ran while one was open for 6% -> 6% of each run, Pallas kernels for 0% -> 16%
where the time goes in v1:
time: 207 us; the launch traced here: 205 us
  blocking collectives  77.8 us (38%)
  starting transfers between devices  42 us (20%)
  Pallas kernels  35.8 us (17%)
  local copies, waits for them, and re-layouts  26.1 us (13%)
  waiting for transfers between devices  21.5 us (10%)
    all_to_all x4, blocking collectives, exchange(): return lax.all_to_all(value, axes, 0, 0, tiled=True)  77.8 us
    all_to_all x6, starting transfers between devices, exchange(): return lax.all_to_all(value, axes, 0, 0, tiled=True)  29 us
    all_to_all x6, waiting for transfers between devices, exchange(): return lax.all_to_all(value, axes, 0, 0, tiled=True)  19.9 us
    unnamed x38, local copies, waits for them, and re-layouts  15.2 us
    ppermute x8, starting transfers between devices, swap(): return lax.ppermute(value, axis, [(0, 1), (1, 0)])  13.1 us
    pallas_call x1, Pallas kernels, reorder(): pl.pallas_call(reorder_kernel, in_specs=[SMEM, ANY, ANY], out_specs=ANY,...  7.2 us
    pallas_call x2, Pallas kernels, project_out(): pl.pallas_call(out_kernel, grid=(4,), in_specs=[SMEM, whole(8, 128, 128)]...  6.78 us
    pallas_call x1, Pallas kernels, project_embed(): pl.pallas_call(embed_kernel, grid=(8,), in_specs=[whole(1, 128), whole(51...  6.56 us
  transfers between devices with their start and end apart: 14, of which 5 were waited for; matrix products, arithmetic and copies ran while one was open for 6% of the time, Pallas kernels for 16%

profile of v1, /device:TPU:1, one launch (start us, length us, event | category | flops | bytes accessed | tf_op | source)
XLA Modules:
  0.0 205.5 jit_solution(84872690300728523)
XLA Ops:
  0.6 1.5 collective-permute-start.2
  2.1 0.8 mul.91
  3.7 5.2 %all-to-all-start = ((s32[8,1,128]{2,1,0:T(1,128)}), s32[8,1,128]{2,1,0:T(1,128)S(1)}, u32[]{:S(2)}, u32[]{:S(2)}) async-start(s32[8,1,128]{2,1,0:T(1,128)} %broadcast_in_dim.25), calls=%async_computation | async-start | bytes 8192 | tf_op jit(solution)/shard_map/all_to_all | solution.py:33
  8.9 0.8 copy.47
  10.6 0.8 slice_bitcast_fusion.1
  11.5 0.7 pad_add_fusion.3
  12.4 2.7 %copy.48.cache_ref.own_ref = bf16[16,127,512]{2,1,0:T(8,128)(2,1)S(1)} copy(bf16[16,127,512]{2,0,1:T(8,128)(2,1)} %param.20) | data formatting | bytes 4161536 | tf_op args[9]
  15.2 2.5 %state_sums.1 = f32[512,128]{1,0:T(8,128)} custom-call(f32[32,128]{1,0:T(8,128)S(1)} %copy-done.16, f32[16,512]{1,0:T(8,128)S(1)} %copy-done.14, f32[16,512]{1,0:T(8,128)S(1)} %copy-done.15, f32[16,16,512]{2,1,0:T(8,128)S(1)} %copy-done.5, bf16[16,127,512]{2,1,0:T(8,128)(2,1)S(1)} %copy.48.cache_ref.own_ref), custom_call_target="tpu_custom_call" | custom-call | tf_op jit(solution)/shard_map/state_sums/pallas_call | solution.py:78
  17.7 1.4 copy-done.2
  19.2 5.4 %all-to-all-start.2 = ((f32[8,64,128]{2,1,0:T(8,128)}), f32[8,64,128]{2,1,0:T(8,128)S(1)}, u32[]{:S(2)}, u32[]{:S(2)}) async-start(f32[8,64,128]{2,1,0:T(8,128)} %bitcast.10), calls=%async_computation.2 | async-start | bytes 524288 | tf_op jit(solution)/shard_map/all_to_all | solution.py:33
  24.8 2.8 %copy-done = bf16[2,16,1,3,64,512]{5,4,3,2,1,0:T(8,128)(2,1)S(1)} copy-done((bf16[2,16,1,3,64,512]{5,4,3,2,1,0:T(8,128)(2,1)S(1)}, bf16[2,16,1,3,64,512]{5,4,3,2,1,0:T(8,128)(2,1)}, u32[]{:S(2)}) %copy-start) | copy-done | bytes 6291480
  27.5 6.6 %embed_project.1 = (bf16[8,400,128]{2,1,0:T(8,128)(2,1)S(1)}, bf16[2,512,128]{2,1,0:T(8,128)(2,1)S(1)}) custom-call(s32[1,128]{1,0:T(1,128)S(1)} %bitcast.25, bf16[512,512]{1,0:T(8,128)(2,1)S(1)} %copy-done.10, bf16[512,512]{1,0:T(8,128)(2,1)S(1)} %collective-permute-done.e_oth, f32[512,8]{1,0:T(8,128)S(1)} %pad_bitcast_fusion.g_own, ...), custom_call_target="tpu_custom_call" | custom-call | flops 805306368 | bytes 7340032 | tf_op jit(solution)/shard_map/embed_project/pallas_call | solution.py:135
  34.1 0.7 copy-done.7
  34.8 0.9 copy-done.9
  35.7 0.7 copy-done.12
  36.4 0.7 copy-done.17
  37.1 7.3 %all-to-all-start.1 = ((bf16[8,400,128]{2,1,0:T(8,128)(2,1)}), bf16[8,400,128]{2,1,0:T(8,128)(2,1)S(1)}, u32[]{:S(2)}, u32[]{:S(2)}) async-start(bf16[8,400,128]{2,1,0:T(8,128)(2,1)} %copy-done.9), calls=%async_computation.1 | async-start | bytes 1638400 | tf_op jit(solution)/shard_map/all_to_all | solution.py:33
  44.6 1.7 constant_dynamic-slice_fusion
  46.2 0.6 collective-permute-start.3
  47.4 0.7 collective-permute-done.3.refs_3_
  48.1 8.5 %all-to-all-done.1.refs_1_ = bf16[8,400,128]{2,1,0:T(8,128)(2,1)S(1)} async-done(((bf16[8,400,128]{2,1,0:T(8,128)(2,1)}), bf16[8,400,128]{2,1,0:T(8,128)(2,1)S(1)}, u32[]{:S(2)}, u32[]{:S(2)}) %all-to-all-start.1) | async-done | bytes 819232 | tf_op jit(solution)/shard_map/all_to_all | solution.py:33
  56.6 1.2 mix.2
  57.8 0.7 copy-done.11
  58.4 4.2 %all-to-all-start.3 = ((bf16[8,128,128]{2,1,0:T(8,128)(2,1)}), bf16[8,128,128]{2,1,0:T(8,128)(2,1)S(1)}, u32[]{:S(2)}, u32[]{:S(2)}) async-start(bf16[8,128,128]{2,1,0:T(8,128)(2,1)} %copy-done.11), calls=%async_computation.3 | async-start | bytes 524288 | tf_op jit(solution)/shard_map/all_to_all | solution.py:33
  62.7 1.5 collective-permute-start.7
  64.1 4.7 %all-to-all-done.3.a_ref = bf16[8,128,128]{2,1,0:T(8,128)(2,1)S(1)} async-done(((bf16[8,128,128]{2,1,0:T(8,128)(2,1)}), bf16[8,128,128]{2,1,0:T(8,128)(2,1)S(1)}, u32[]{:S(2)}, u32[]{:S(2)}) %all-to-all-start.3) | async-done | bytes 262176 | tf_op jit(solution)/shard_map/all_to_all | solution.py:33
  68.8 2.9 %project_out.2 = bf16[8,128,128]{2,1,0:T(8,128)(2,1)S(1)} custom-call(s32[2]{0:T(128)S(1)} %pad_add_fusion.5.refs_0_.c_ref, bf16[8,128,128]{2,1,0:T(8,128)(2,1)S(1)} %all-to-all-done.3.a_ref, bf16[2,1024,512]{2,1,0:T(8,128)(2,1)S(1)} %bitcast.23, bf16[2,1024,512]{2,1,0:T(8,128)(2,1)} %collective-permute-done.4.w_oth), custom_call_target="tpu_custom_call" | custom-call | flops 268435456 | bytes 2621440 | tf_op jit(solution)/shard_map/project_out/pallas_call | solution.py:250
  71.7 46.2 %all_to_all.50.r_ref = bf16[8,128,128]{2,1,0:T(8,128)(2,1)S(1)} all-to-all(bf16[8,128,128]{2,1,0:T(8,128)(2,1)S(1)} %project_out.2), channel_id=1, replica_groups=mesh['y'=4,'xl'=2,'xh'=2,'z'=4,'c'=2] {'xh','z'}, dimensions={0} | all-to-all | bytes 524288 | tf_op jit(solution)/shard_map/all_to_all | solution.py:33
  117.9 0.9 copy-done.13
  119.4 9.8 %all_to_all.51.a_ref = bf16[8,128,128]{2,1,0:T(8,128)(2,1)S(1)} all-to-all(bf16[8,128,128]{2,1,0:T(8,128)(2,1)S(1)} %residual.1.h_ref), channel_id=1, replica_groups=mesh['y'=4,'xl'=2,'xh'=2,'z'=4,'c'=2] {'y','xl'}, dimensions={0} | all-to-all | bytes 524288 | tf_op jit(solution)/shard_map/all_to_all | solution.py:33
  129.3 2.8 %copy-done.1 = bf16[2,16,1,3,64,512]{5,4,3,2,1,0:T(8,128)(2,1)S(1)} copy-done((bf16[2,16,1,3,64,512]{5,4,3,2,1,0:T(8,128)(2,1)S(1)}, bf16[2,16,1,3,64,512]{5,4,3,2,1,0:T(8,128)(2,1)}, u32[]{:S(2)}) %copy-start.1) | copy-done | bytes 6291480
  132.1 6.2 %norm_project.1 = bf16[8,400,128]{2,1,0:T(8,128)(2,1)S(1)} custom-call(s32[2]{0:T(128)S(1)} %pad_add_fusion.5.refs_0_.c_ref, bf16[8,128,128]{2,1,0:T(8,128)(2,1)S(1)} %all_to_all.51.a_ref, f32[512,8]{1,0:T(8,128)S(1)} %pad_bitcast_fusion.g_own, f32[512,8]{1,0:T(8,128)S(1)} %copy-done.8, bf16[2,3072,512]{2,1,0:T(8,128)(2,1)S(1)} %bitcast.21, ...), custom_call_target="tpu_custom_call" | custom-call | flops 805306368 | bytes 7340032 | tf_op jit(solution)/shard_map/norm_project/pallas_call | solution.py:174
  138.3 13.2 %all_to_all.52.refs_1_ = bf16[8,400,128]{2,1,0:T(8,128)(2,1)S(1)} all-to-all(bf16[8,400,128]{2,1,0:T(8,128)(2,1)S(1)} %norm_project.1), channel_id=1, replica_groups=mesh['y'=4,'xl'=2,'xh'=2,'z'=4,'c'=2] {'xh','z'}, dimensions={0} | all-to-all | bytes 1638400 | tf_op jit(solution)/shard_map/all_to_all | solution.py:33
  151.6 1.2 mix.3
  152.7 8.5 %all_to_all.53.a_ref = bf16[8,128,128]{2,1,0:T(8,128)(2,1)S(1)} all-to-all(bf16[8,128,128]{2,1,0:T(8,128)(2,1)S(1)} %get-tuple-element.14), channel_id=1, replica_groups=mesh['y'=4,'xl'=2,'xh'=2,'z'=4,'c'=2] {'y','xl'}, dimensions={0} | all-to-all | bytes 524288 | tf_op jit(solution)/shard_map/all_to_all | solution.py:33
  161.3 3.9 %project_out.3 = bf16[8,128,128]{2,1,0:T(8,128)(2,1)} custom-call(s32[2]{0:T(128)S(1)} %pad_add_fusion.5.refs_0_.c_ref, bf16[8,128,128]{2,1,0:T(8,128)(2,1)S(1)} %all_to_all.53.a_ref, bf16[2,1024,512]{2,1,0:T(8,128)(2,1)S(1)} %bitcast.24, bf16[2,1024,512]{2,1,0:T(8,128)(2,1)} %collective-permute-done.4.w_oth), custom_call_target="tpu_custom_call" | custom-call | flops 268435456 | bytes 2621440 | tf_op jit(solution)/shard_map/project_out/pallas_call | solution.py:250
  165.2 3.4 %all-to-all-start.8 = ((bf16[8,128,128]{2,1,0:T(8,128)(2,1)}), bf16[8,128,128]{2,1,0:T(8,128)(2,1)S(1)}, u32[]{:S(2)}, u32[]{:S(2)}) async-start(bf16[8,128,128]{2,1,0:T(8,128)(2,1)} %project_out.3), calls=%async_computation.8 | async-start | bytes 524288 | tf_op jit(solution)/shard_map/all_to_all | solution.py:33
  168.6 0.7 collective-permute-start.6
  169.3 6.8 %all-to-all-done.8.r_ref = bf16[8,128,128]{2,1,0:T(8,128)(2,1)S(1)} async-done(((bf16[8,128,128]{2,1,0:T(8,128)(2,1)}), bf16[8,128,128]{2,1,0:T(8,128)(2,1)S(1)}, u32[]{:S(2)}, u32[]{:S(2)}) %all-to-all-start.8) | async-done | bytes 262176 | tf_op jit(solution)/shard_map/all_to_all | solution.py:33
  176.1 0.9 last.1
  177.0 7.9 %collective-permute-start.5 = (bf16[3,128,64]{2,1,0:T(8,128)(2,1)S(1)}, bf16[3,128,64]{2,1,0:T(8,128)(2,1)S(1)}, u32[]{:S(2)}, u32[]{:S(2)}) collective-permute-start(bf16[3,128,64]{2,1,0:T(8,128)(2,1)S(1)} %get-tuple-element.18), channel_id=1, source_target_pairs={{0,1},{1,0},{2,3},{3,2},{4,5},{5,4},{6,7},{7,6},{8,9},{9,8},{10,11... | collective-permute-start | bytes 147464 | tf_op jit(solution)/shard_map/ppermute | solution.py:29
  185.0 0.9 collective-permute-done.5.got_ref
  186.4 0.8 copy.53
  187.2 3.4 %all-to-all-start.9 = ((bf16[8,96,64]{1,2,0:T(8,128)(2,1)}), bf16[8,96,64]{1,2,0:T(8,128)(2,1)S(1)}, u32[]{:S(2)}, u32[]{:S(2)}) async-start(bf16[8,96,64]{1,2,0:T(8,128)(2,1)} %copy.53), calls=%async_computation.9 | async-start | bytes 262144 | tf_op jit(solution)/shard_map/all_to_all | solution.py:33
  190.6 2.9 %copy.55.oth_ref = bf16[16,127,512]{2,1,0:T(8,128)(2,1)S(1)} copy(bf16[16,127,512]{2,0,1:T(8,128)(2,1)} %collective-permute-done.7) | data formatting | bytes 4161536 | tf_op jit(solution)/shard_map/ppermute | solution.py:29
  193.5 7.2 %reorder.1.fir_ref = bf16[16,127,512]{2,1,0:T(8,128)(2,1)S(1)} custom-call(s32[2,16]{1,0:T(2,128)S(1)} %pad_add_fusion.4.pick_ref, bf16[16,127,512]{2,1,0:T(8,128)(2,1)S(1)} %copy-done.3, bf16[16,127,512]{2,1,0:T(8,128)(2,1)S(1)} %copy.55.oth_ref), custom_call_target="tpu_custom_call" | custom-call | bytes 4194304 | tf_op jit(solution)/shard_map/reorder/pallas_call | solution.py:362
  200.9 2.1 %final.1 = (bf16[2,16,512]{2,1,0:T(8,128)(2,1)}, bf16[16,127,512]{2,1,0:T(8,128)(2,1)S(1)}, f32[16,16,512]{2,1,0:T(8,128)}) custom-call(s32[2,16]{1,0:T(2,128)S(1)} %pad_add_fusion.4.pick_ref, bf16[8,96,64]{2,1,0:T(8,128)(2,1)S(1)} %copy.56.r_ref, f32[16,512]{1,0:T(8,128)S(1)} %copy-done.14, ...), custom_call_target="tpu_custom_call", output_to_operand_aliasing={{1}: (5, {})} | custom-call | tf_op jit(solution)/shard_map/final/pallas_call | solution.py:401
  203.0 2.5 %copy.57 = bf16[16,127,512]{2,0,1:T(8,128)(2,1)} copy(bf16[16,127,512]{2,1,0:T(8,128)(2,1)S(1)} %get-tuple-element.29) | data formatting | bytes 4161536 | tf_op jit(solution)/shard_map/final/pallas_call | solution.py:401
  (73 shorter events, 4.3 us)
Async XLA Ops:
  0.6 24.1 %collective-permute-start.2 = (bf16[2,3072,512]{2,1,0:T(8,128)(2,1)}, bf16[2,3072,512]{2,1,0:T(8,128)(2,1)}, u32[]{:S(2)}, u32[]{:S(2)}) collective-permute-start(bf16[2,3072,512]{2,1,0:T(8,128)(2,1)} %bitcast.19), channel_id=1, source_target_pairs={{0,1},{1,0},{2,3},{3,2},{4,5},{5,4},{6,7},{7,6},{8,9},{9,8},{10,11... | collective-permute-start | bytes 18874376 | tf_op jit(solution)/shard_map/ppermute | solution.py:29
  3.7 15.5 %all-to-all-start = ((s32[8,1,128]{2,1,0:T(1,128)}), s32[8,1,128]{2,1,0:T(1,128)S(1)}, u32[]{:S(2)}, u32[]{:S(2)}) async-start(s32[8,1,128]{2,1,0:T(1,128)} %broadcast_in_dim.25), calls=%async_computation | async-start | bytes 8192 | tf_op jit(solution)/shard_map/all_to_all | solution.py:33
  9.7 15.0 %collective-permute-start.1 = (f32[512,8]{1,0:T(8,128)S(1)}, f32[512,8]{1,0:T(8,128)S(1)}, u32[]{:S(2)}, u32[]{:S(2)}) collective-permute-start(f32[512,8]{1,0:T(8,128)S(1)} %pad_bitcast_fusion.g_own), channel_id=1, source_target_pairs={{0,1},{1,0},{2,3},{3,2},{4,5},{5,4},{6,7},{7,6},{8,9},{9,8},{10,11... | collective-permute-start | bytes 49160 | tf_op jit(solution)/shard_map/ppermute | solution.py:29
  10.1 14.6 %collective-permute-start = (bf16[512,512]{1,0:T(8,128)(2,1)}, bf16[512,512]{1,0:T(8,128)(2,1)S(1)}, u32[]{:S(2)}, u32[]{:S(2)}) collective-permute-start(bf16[512,512]{1,0:T(8,128)(2,1)} %e_own.1), channel_id=1, source_target_pairs={{0,1},{1,0},{2,3},{3,2},{4,5},{5,4},{6,7},{7,6},{8,9},{9,8},{10,11... | collective-permute-start | bytes 1572872 | tf_op jit(solution)/shard_map/ppermute | solution.py:29
  10.3 53.8 %collective-permute-start.4 = (bf16[2,1024,512]{2,1,0:T(8,128)(2,1)}, bf16[2,1024,512]{2,1,0:T(8,128)(2,1)}, u32[]{:S(2)}, u32[]{:S(2)}) collective-permute-start(bf16[2,1024,512]{2,1,0:T(8,128)(2,1)} %bitcast.22), channel_id=1, source_target_pairs={{0,1},{1,0},{2,3},{3,2},{4,5},{5,4},{6,7},{7,6},{8,9},{9,8},{10,11... | collective-permute-start | bytes 6291464 | tf_op jit(solution)/shard_map/ppermute | solution.py:29
  11.5 3.7 %copy-start.5 = (f32[16,16,512]{2,1,0:T(8,128)S(1)}, f32[16,16,512]{2,1,0:T(8,128)}, u32[]{:S(2)}) copy-start(f32[16,16,512]{2,1,0:T(8,128)} %own_ref.2) | copy-start | bytes 1572868
  11.5 3.7 %copy-start.14 = (f32[16,512]{1,0:T(8,128)S(1)}, f32[16,512]{1,0:T(8,128)}, u32[]{:S(2)}) copy-start(f32[16,512]{1,0:T(8,128)} %poles_ref.3) | copy-start | bytes 98308
  11.5 3.7 %copy-start.15 = (f32[16,512]{1,0:T(8,128)S(1)}, f32[16,512]{1,0:T(8,128)}, u32[]{:S(2)}) copy-start(f32[16,512]{1,0:T(8,128)} %res_ref.1) | copy-start | bytes 98308
  11.5 3.7 %copy-start.16 = (f32[32,128]{1,0:T(8,128)S(1)}, f32[32,128]{1,0:T(8,128)}, u32[]{:S(2)}) copy-start(f32[32,128]{1,0:T(8,128)} %filt_ref.1) | copy-start | bytes 49156
  15.2 9.5 %copy-start.10 = (bf16[512,512]{1,0:T(8,128)(2,1)S(1)}, bf16[512,512]{1,0:T(8,128)(2,1)}, u32[]{:S(2)}) copy-start(bf16[512,512]{1,0:T(8,128)(2,1)} %e_own.1) | copy-start | bytes 1572868
  17.7 1.4 copy-start.2
  19.2 17.3 %all-to-all-start.2 = ((f32[8,64,128]{2,1,0:T(8,128)}), f32[8,64,128]{2,1,0:T(8,128)S(1)}, u32[]{:S(2)}, u32[]{:S(2)}) async-start(f32[8,64,128]{2,1,0:T(8,128)} %bitcast.10), calls=%async_computation.2 | async-start | bytes 524288 | tf_op jit(solution)/shard_map/all_to_all | solution.py:33
  24.8 2.8 %copy-start = (bf16[2,16,1,3,64,512]{5,4,3,2,1,0:T(8,128)(2,1)S(1)}, bf16[2,16,1,3,64,512]{5,4,3,2,1,0:T(8,128)(2,1)}, u32[]{:S(2)}) copy-start(bf16[2,16,1,3,64,512]{5,4,3,2,1,0:T(8,128)(2,1)} %param.15) | copy-start | bytes 18874372
  34.1 0.7 copy-start.7
  34.8 0.9 copy-start.9
  35.7 0.7 copy-start.12
  36.4 32.4 %copy-start.4 = (bf16[2,16,1,64,512]{4,3,2,1,0:T(8,128)(2,1)S(1)}, bf16[2,16,1,64,512]{4,3,2,1,0:T(8,128)(2,1)}, u32[]{:S(2)}) copy-start(bf16[2,16,1,64,512]{4,3,2,1,0:T(8,128)(2,1)} %param.16) | copy-start | bytes 6291460
  36.4 0.7 copy-start.17
  37.1 19.4 %all-to-all-start.1 = ((bf16[8,400,128]{2,1,0:T(8,128)(2,1)}), bf16[8,400,128]{2,1,0:T(8,128)(2,1)S(1)}, u32[]{:S(2)}, u32[]{:S(2)}) async-start(bf16[8,400,128]{2,1,0:T(8,128)(2,1)} %copy-done.9), calls=%async_computation.1 | async-start | bytes 1638400 | tf_op jit(solution)/shard_map/all_to_all | solution.py:33
  46.2 1.8 collective-permute-start.3
  57.7 0.7 copy-start.11
  58.4 10.3 %all-to-all-start.3 = ((bf16[8,128,128]{2,1,0:T(8,128)(2,1)}), bf16[8,128,128]{2,1,0:T(8,128)(2,1)S(1)}, u32[]{:S(2)}, u32[]{:S(2)}) async-start(bf16[8,128,128]{2,1,0:T(8,128)(2,1)} %copy-done.11), calls=%async_computation.3 | async-start | bytes 524288 | tf_op jit(solution)/shard_map/all_to_all | solution.py:33
  62.7 66.6 %copy-start.8 = (f32[512,8]{1,0:T(8,128)S(1)}, f32[512,8]{1,0:T(8,128)}, u32[]{:S(2)}) copy-start(f32[512,8]{1,0:T(8,128)} %copy-done.7) | copy-start | bytes 49156
  62.7 127.9 %collective-permute-start.7 = (bf16[16,127,512]{2,0,1:T(8,128)(2,1)}, bf16[16,127,512]{2,0,1:T(8,128)(2,1)}, u32[]{:S(2)}, u32[]{:S(2)}) collective-permute-start(bf16[16,127,512]{2,0,1:T(8,128)(2,1)} %param.20), channel_id=1, source_target_pairs={{0,16},{16,0},{1,17},{17,1},{2,18},{18,2},{3,19},{19,3},{4,20},{20... | collective-permute-start | bytes 6242312 | tf_op jit(solution)/shard_map/ppermute | solution.py:29
  117.9 1.0 copy-start.13
  129.3 2.8 %copy-start.1 = (bf16[2,16,1,3,64,512]{5,4,3,2,1,0:T(8,128)(2,1)S(1)}, bf16[2,16,1,3,64,512]{5,4,3,2,1,0:T(8,128)(2,1)}, u32[]{:S(2)}) copy-start(bf16[2,16,1,3,64,512]{5,4,3,2,1,0:T(8,128)(2,1)} %param.15) | copy-start | bytes 18874372
  161.3 7.3 %copy-start.6 = (f32[16,16,512]{2,1,0:T(8,128)S(1)}, f32[16,16,512]{2,1,0:T(8,128)}, u32[]{:S(2)}) copy-start(f32[16,16,512]{2,1,0:T(8,128)} %own_ref.2) | copy-start | bytes 1572868
  165.2 10.9 %all-to-all-start.8 = ((bf16[8,128,128]{2,1,0:T(8,128)(2,1)}), bf16[8,128,128]{2,1,0:T(8,128)(2,1)S(1)}, u32[]{:S(2)}, u32[]{:S(2)}) async-start(bf16[8,128,128]{2,1,0:T(8,128)(2,1)} %project_out.3), calls=%async_computation.8 | async-start | bytes 524288 | tf_op jit(solution)/shard_map/all_to_all | solution.py:33
  168.6 32.3 %collective-permute-start.6 = (f32[16,16,512]{2,1,0:T(8,128)S(1)}, f32[16,16,512]{2,1,0:T(8,128)}, u32[]{:S(2)}, u32[]{:S(2)}) collective-permute-start(f32[16,16,512]{2,1,0:T(8,128)S(1)} %copy-done.6), channel_id=1, source_target_pairs={{0,16},{16,0},{1,17},{17,1},{2,18},{18,2},{3,19},{19,3},{4,20},{20... | collective-permute-start | bytes 1572872 | tf_op jit(solution)/shard_map/ppermute | solution.py:29
  177.0 8.9 %collective-permute-start.5 = (bf16[3,128,64]{2,1,0:T(8,128)(2,1)S(1)}, bf16[3,128,64]{2,1,0:T(8,128)(2,1)S(1)}, u32[]{:S(2)}, u32[]{:S(2)}) collective-permute-start(bf16[3,128,64]{2,1,0:T(8,128)(2,1)S(1)} %get-tuple-element.18), channel_id=1, source_target_pairs={{0,1},{1,0},{2,3},{3,2},{4,5},{5,4},{6,7},{7,6},{8,9},{9,8},{10,11... | collective-permute-start | bytes 147464 | tf_op jit(solution)/shard_map/ppermute | solution.py:29
  187.2 13.5 %all-to-all-start.9 = ((bf16[8,96,64]{1,2,0:T(8,128)(2,1)}), bf16[8,96,64]{1,2,0:T(8,128)(2,1)S(1)}, u32[]{:S(2)}, u32[]{:S(2)}) async-start(bf16[8,96,64]{1,2,0:T(8,128)(2,1)} %copy.53), calls=%async_computation.9 | async-start | bytes 262144 | tf_op jit(solution)/shard_map/all_to_all | solution.py:33
  190.6 2.9 %copy-start.3 = (bf16[16,127,512]{2,1,0:T(8,128)(2,1)S(1)}, bf16[16,127,512]{2,1,0:T(8,128)(2,1)}, u32[]{:S(2)}) copy-start(bf16[16,127,512]{2,1,0:T(8,128)(2,1)} %copy-done.2) | copy-start | bytes 6242308

commit v2 on v1

v2 whole, which is shorter than its diff:
```python
import jax
import jax.numpy as jnp
from jax import lax
from jax.experimental import pallas as pl
from jax.experimental.pallas import tpu as pltpu
from jax.sharding import Mesh, PartitionSpec as P

D = 8192
EPSILON = 1e-05
BF = jnp.bfloat16
F32 = jnp.float32
I32 = jnp.int32
HIGH = lax.Precision.HIGHEST
DP = ("y", "xl")
CHAN = ("xh", "z", "c")
XZ = ("xh", "z")
SMEM = pl.BlockSpec(memory_space=pltpu.SMEM)
HBM = pl.BlockSpec(memory_space=pltpu.HBM)
LARGE = 64 * 1024 * 1024
CHUNKS = (48, 29, 48)
EXTRA = 16


def params():
    return pltpu.CompilerParams(vmem_limit_bytes=LARGE)


def whole(*shape):
    return pl.BlockSpec(shape, lambda g: (0,) * len(shape))


def swap(value, axis):
    return lax.ppermute(value, axis, [(0, 1), (1, 0)])


def exchange(value, axes):
    return lax.all_to_all(value, axes, 0, 0, tiled=True)


def sums_kernel(
    c_ref, tok_ref, filt_ref, poles_ref, res_ref, state_ref, cache_ref, out_ref, *refs
):
    pieces, (sent_ref, taps, rows, held, sems, sem_out) = refs[: len(CHUNKS)], refs[len(CHUNKS) :]
    copies = []
    for k in range(4):
        size = 32 if k < 3 else 31
        piece = pl.ds(32 * k, size)
        copies.append(pltpu.make_async_copy(cache_ref.at[piece], held.at[piece], sems.at[k]))
        copies[-1].start()
    group = lax.broadcasted_iota(I32, (32, 512), 1) // 16
    spread = (group == lax.broadcasted_iota(I32, (32, 512), 0)).astype(F32)
    taps[0:128, :] = lax.dot_general(
        filt_ref[...], spread, (((0,), (0,)), ((), ())),
        preferred_element_type=F32, precision=HIGH,
    )
    taps[128:136, :] = jnp.zeros((8, 512), F32)
    rows[64:128, :] = jnp.zeros((64, 512), F32)
    rows[64:66, :] = taps[0:2, :]
    once = res_ref[...] * poles_ref[...]
    twice = once * poles_ref[...]
    rows[66:67, :] = jnp.sum(res_ref[...], axis=0, keepdims=True)
    rows[67:68, :] = jnp.sum(once, axis=0, keepdims=True)
    for b in range(16):
        state = state_ref[b]
        rows[32 + b : 33 + b, :] = jnp.sum(state * once, axis=0, keepdims=True)
        rows[48 + b : 49 + b, :] = jnp.sum(state * twice, axis=0, keepdims=True)
        sent_ref[b] = state.astype(BF)

    def add_tap(s, sums):
        past = held[s].astype(F32)
        return (
            sums[0] + past * taps[pl.ds(s + 1, 1), :],
            sums[1] + past * taps[pl.ds(s + 2, 1), :],
        )

    sums = (jnp.zeros((16, 512), F32),) * 2
    outs, start, size = [], 0, 0
    for k in range(4):
        copies[k].wait()
        while len(outs) < len(CHUNKS) and start + CHUNKS[len(outs)] <= 32 * k + 32:
            size = CHUNKS[len(outs)]
            outs.append(
                pltpu.make_async_copy(
                    held.at[start : start + size], pieces[len(outs)], sem_out.at[len(outs)]
                )
            )
            outs[-1].start()
            start += size
        sums = lax.fori_loop(32 * k, 32 * k + (32 if k < 3 else 31), add_tap, sums, unroll=True)
    rows[0:16, :] = sums[0]
    rows[16:32, :] = sums[1]
    columns = rows[...].T
    lane = lax.broadcasted_iota(I32, (8, 128), 1)
    start = (c_ref[1] % 4) * 32
    tok = jnp.zeros((8, 128), I32)
    for t in range(2):
        for b in range(16):
            tok = jnp.where(lane == start + 16 * t + b, tok_ref[t, b], tok)
    tok = tok.astype(F32)
    for i in range(8):
        out_ref[i, 0:64, :] = columns[64 * i : 64 * i + 64, :]
        out_ref[i, 64:72, :] = tok
    for copy in outs:
        copy.wait()


def make_sums(where, tokens, filters, poles, residues, state, cache):
    return pl.pallas_call(
        sums_kernel,
        grid=(1,),
        in_specs=[
            SMEM, SMEM, whole(32, 128), whole(16, 512), whole(16, 512), whole(16, 16, 512), HBM,
        ],
        out_specs=[whole(8, 72, 128)] + [HBM] * len(CHUNKS) + [whole(16, 16, 512)],
        out_shape=[jax.ShapeDtypeStruct((8, 72, 128), F32)]
        + [jax.ShapeDtypeStruct((size, 16, 512), BF) for size in CHUNKS + (16,)],
        scratch_shapes=[
            pltpu.VMEM((136, 512), F32),
            pltpu.VMEM((128, 512), F32),
            pltpu.VMEM((127, 16, 512), BF),
            pltpu.SemaphoreType.DMA((4,)),
            pltpu.SemaphoreType.DMA((len(CHUNKS),)),
        ],
        compiler_params=params(),
        name="state_sums",
    )(where, tokens, filters, poles, residues, state, cache)


def index_kernel(c_ref, par_ref, out_ref):
    base = c_ref[0] * 64
    lane = lax.broadcasted_iota(I32, (1, 128), 1)
    fir, onward = jnp.zeros((1, 128), I32), lane
    earlier = jnp.full((1, 128), -1, I32)
    place = lambda beam, wide: (beam >> 4) * wide + (beam & 15)
    for j in range(64):
        after = par_ref[1, base + j]
        old, older = par_ref[0, base + j] - base, par_ref[0, after] - base
        source = place(after - base, 32)
        first = lane == j // 16 * 32 + j % 16
        second = lane == j // 16 * 32 + 16 + j % 16
        fir = jnp.where(first, place(old, 128), jnp.where(second, place(older, 128) + 16, fir))
        earlier = jnp.where(second, source, earlier)
        onward = jnp.where(first, source, onward)
    out_ref[0:1, :] = fir
    out_ref[1:2, :] = fir + 32
    out_ref[2:3, :] = earlier
    out_ref[3:4, :] = onward
    out_ref[4:8, :] = jnp.zeros((4, 128), I32)


def indices(where, parents):
    return pl.pallas_call(
        index_kernel,
        grid=(1,),
        in_specs=[SMEM, SMEM],
        out_specs=whole(8, 128),
        out_shape=jax.ShapeDtypeStruct((8, 128), I32),
        compiler_params=params(),
        name="indices",
    )(where, parents)


def turn_kernel(own_ref, oth_ref, out_ref):
    for k, table in enumerate((own_ref, oth_ref)):
        out_ref[k] = table[...].T


def turn(own, oth):
    return pl.pallas_call(
        turn_kernel,
        grid=(1,),
        in_specs=[whole(512, 512)] * 2,
        out_specs=whole(2, 512, 512),
        out_shape=jax.ShapeDtypeStruct((2, 512, 512), BF),
        compiler_params=params(),
        name="turn",
    )(own, oth)


def weights(block, rows):
    return [pl.BlockSpec((1, rows // 2, 512), lambda g: (block, g, 0))] * 2


def squares_rows(x_own, x_oth):
    total = jnp.sum(x_own * x_own, axis=0, keepdims=True)
    total = total + jnp.sum(x_oth * x_oth, axis=0, keepdims=True)
    high = total.astype(BF).astype(F32)
    low = total - high
    place = lax.broadcasted_iota(I32, (EXTRA, 128), 0)
    return jnp.where(place == 0, high, jnp.where(place == 1, low, 0.0)).astype(BF)


def column(gain_ref, k):
    return jnp.broadcast_to(gain_ref[k : k + 1, :], (8, 512)).T[:, 0:1]


def hand_out(acc, rows, where_ref, outs, spread):
    half = pl.program_id(0) ^ where_ref[2]
    spread[...] = acc
    for s in range(4):
        start = pl.multiple_of(((where_ref[3] + s) & 3) * rows, rows)
        outs[s][half, 0:rows, :] = spread[pl.ds(start, rows), :]
    return half


def product_in(where_ref, w_own, w_oth, scaled, squares, spread, outs):
    acc = jnp.dot(w_own[0], scaled[0], preferred_element_type=F32)
    acc = (acc + jnp.dot(w_oth[0], scaled[1], preferred_element_type=F32)).astype(BF)
    half = hand_out(acc, 384, where_ref, outs, spread)
    for out in outs:
        out[half, 384:400, :] = squares[...]


def embed_kernel(
    c_ref, got_ref, tables, g_own, g_oth, w_own, w_oth, *refs
):
    *outs, x_ref, send_ref, scaled, squares, spread = refs

    @pl.when(pl.program_id(0) == 0)
    def _():
        c = c_ref[0]
        tok = jnp.zeros((8, 128), F32)
        for q in range(4):
            tok = tok + got_ref[c * 4 + q, 64:72, :]
            send_ref[q] = got_ref[4 - c * 4 + q, 0:64, :]
        vocab = lax.broadcasted_iota(I32, (512, 128), 0)
        onehot = (vocab == tok[0:1, :].astype(I32)).astype(BF)
        halves = []
        for k, gain in enumerate((g_own, g_oth)):
            x = jnp.dot(tables[k], onehot, preferred_element_type=F32)
            x_ref[k] = x.astype(BF)
            scaled[k] = (x * column(gain, 0)).astype(BF)
            halves.append(x)
        squares[...] = squares_rows(*halves)

    product_in(c_ref, w_own, w_oth, scaled, squares, spread, outs)


IN_SCRATCH = [
    pltpu.VMEM((2, 512, 128), BF), pltpu.VMEM((EXTRA, 128), BF), pltpu.VMEM((1536, 128), BF)
]
IN_SHAPE = [jax.ShapeDtypeStruct((2, 400, 128), BF)] * 4
IN_SPECS = [whole(2, 400, 128)] * 4
COST_IN = pl.CostEstimate(flops=2 * 3072 * 1024 * 128, bytes_accessed=7 << 20, transcendentals=0)
COST_OUT = pl.CostEstimate(flops=2 * 1024 * 1024 * 128, bytes_accessed=5 << 19, transcendentals=0)


def project_embed(where, got, tables, g_own, g_oth, w_own, w_oth):
    return pl.pallas_call(
        embed_kernel,
        grid=(2,),
        in_specs=[
            SMEM, whole(8, 72, 128), whole(2, 512, 512), whole(2, 512), whole(2, 512),
            *weights(0, 3072),
        ],
        out_specs=[*IN_SPECS, whole(2, 512, 128), whole(4, 64, 128)],
        out_shape=[
            *IN_SHAPE,
            jax.ShapeDtypeStruct((2, 512, 128), BF),
            jax.ShapeDtypeStruct((4, 64, 128), F32),
        ],
        scratch_shapes=IN_SCRATCH,
        compiler_params=params(),
        cost_estimate=COST_IN,
        name="embed_project",
    )(where, got, tables, g_own, g_oth, w_own, w_oth)


def gather_rows(c, a_ref, k):
    start = pl.multiple_of((c ^ k) * 64, 64)
    return jnp.concatenate([a_ref[i, pl.ds(start, 64), :] for i in range(8)], axis=0)


def in_kernel(c_ref, a_ref, g_own, g_oth, w_own, w_oth, *refs):
    *outs, scaled, squares, spread = refs

    @pl.when(pl.program_id(0) == 0)
    def _():
        halves = []
        for k, gain in enumerate((g_own, g_oth)):
            x = gather_rows(c_ref[0], a_ref, k).astype(F32)
            scaled[k] = (x * column(gain, 1)).astype(BF)
            halves.append(x)
        squares[...] = squares_rows(*halves)

    product_in(c_ref, w_own, w_oth, scaled, squares, spread, outs)


def project_in(where, rows, g_own, g_oth, w_own, w_oth):
    return pl.pallas_call(
        in_kernel,
        grid=(2,),
        in_specs=[
            SMEM, whole(8, 128, 128), whole(2, 512), whole(2, 512), *weights(1, 3072),
        ],
        out_specs=IN_SPECS,
        out_shape=IN_SHAPE,
        scratch_shapes=IN_SCRATCH,
        compiler_params=params(),
        cost_estimate=COST_IN,
        name="norm_project",
    )(where, rows, g_own, g_oth, w_own, w_oth)


def add_up(terms):
    *near, far = terms
    total = far[...].astype(F32)
    for term in near:
        total = total + term[0].astype(F32)
    return total


def terms_specs(rows):
    return [pl.BlockSpec((1, rows, 128), lambda g: (0, 0, 0))] * 4 + [whole(rows, 128)]


def mix_kernel(block, c_ref, *refs):
    t_own, t_oth, idx_ref, gated_ref, kv_ref = refs[5:]
    c = c_ref[0]
    total = add_up(refs[:5])
    squares = total[384:385, :] + total[385:386, :]
    feats = (total[0:384, :] * lax.rsqrt(squares / D + EPSILON)).astype(BF).astype(F32)
    kind = lambda m: jnp.concatenate(
        [feats[64 * m : 64 * m + 64, :], feats[192 + 64 * m : 256 + 64 * m, :]], axis=0
    )
    kv = (kind(1) * kind(2)).astype(BF)
    square = lax.broadcasted_iota(I32, (128, 128), 0)
    earlier = (square == idx_ref[2:3, :]).astype(BF)
    onward = (square == idx_ref[3:4, :]).astype(BF)
    kv_before = jnp.dot(kv, earlier, preferred_element_type=F32)
    kv_ref[...] = jnp.dot(kv, onward, preferred_element_type=F32).T.astype(BF)
    parts, first, second = [], [], []
    for k in range(2):
        own = c == k
        acc = jnp.zeros((64, 128), F32)
        for q in range(4):
            sums = jnp.where(own, t_own[c * 4 + q, 0:64, :], t_oth[q])
            pick = (square + 128 * q == idx_ref[block : block + 1, :]).astype(F32)
            acc = acc + jnp.dot(sums, pick, preferred_element_type=F32, precision=HIGH)
            if q == 0:
                first.append(sums[:, 64 + 2 * block : 65 + 2 * block])
                second.append(sums[:, 65 + 2 * block : 66 + 2 * block])
        parts.append(acc)
    first, second = jnp.concatenate(first, axis=0), jnp.concatenate(second, axis=0)
    filtered = first * kv.astype(F32) + second * kv_before + jnp.concatenate(parts, axis=0)
    gated = (kind(0) * filtered).astype(BF)
    for i in range(8):
        gated_ref[i] = gated


def mix(block, where, received, t_own, t_oth, idx):
    return pl.pallas_call(
        lambda *refs: mix_kernel(block, *refs),
        grid=(1,),
        in_specs=[
            SMEM, *terms_specs(400), whole(8, 72, 128), whole(4, 64, 128), whole(8, 128)
        ],
        out_specs=[whole(8, 128, 128), whole(128, 128)],
        out_shape=[
            jax.ShapeDtypeStruct((8, 128, 128), BF),
            jax.ShapeDtypeStruct((128, 128), BF),
        ],
        compiler_params=params(),
        name="mix",
    )(where, *received, t_own, t_oth, idx)


def out_kernel(c_ref, a_ref, w_own, w_oth, *refs):
    *outs, rows, spread = refs

    @pl.when(pl.program_id(0) == 0)
    def _():
        for k in range(2):
            rows[k] = gather_rows(c_ref[0], a_ref, k)

    acc = jnp.dot(w_own[0], rows[0], preferred_element_type=F32)
    acc = (acc + jnp.dot(w_oth[0], rows[1], preferred_element_type=F32)).astype(BF)
    hand_out(acc, 128, c_ref, outs, spread)


def project_out(block, where, rows, w_own, w_oth):
    return pl.pallas_call(
        out_kernel,
        grid=(2,),
        in_specs=[SMEM, whole(8, 128, 128), *weights(block, 1024)],
        out_specs=[whole(2, 128, 128)] * 4,
        out_shape=[jax.ShapeDtypeStruct((2, 128, 128), BF)] * 4,
        scratch_shapes=[pltpu.VMEM((2, 512, 128), BF), pltpu.VMEM((512, 128), BF)],
        compiler_params=params(),
        cost_estimate=COST_OUT,
        name="project_out",
    )(where, rows, w_own, w_oth)


def residual_kernel(c_ref, *refs):
    x_ref, out_ref = refs[5:]
    outward = add_up(refs[:5]).astype(BF).astype(F32)
    start = pl.multiple_of(c_ref[1] * 64, 64)
    before = jnp.concatenate(
        [x_ref[c_ref[0] ^ k, pl.ds(start, 64), :] for k in range(2)], axis=0
    )
    hidden = (before.astype(F32) + outward).astype(BF)
    for i in range(8):
        out_ref[i] = hidden


def residual(where, received, embedded):
    return pl.pallas_call(
        residual_kernel,
        grid=(1,),
        in_specs=[SMEM, *terms_specs(128), whole(2, 512, 128)],
        out_specs=whole(8, 128, 128),
        out_shape=jax.ShapeDtypeStruct((8, 128, 128), BF),
        compiler_params=params(),
        name="residual",
    )(where, *received, embedded)


def last_kernel(c_ref, *refs):
    h_ref, kv0_ref, kv1_ref, keep_ref, send_ref = refs[5:]
    outward = add_up(refs[:5]).astype(BF).astype(F32)
    hidden = (h_ref[0].astype(F32) + outward).astype(BF).astype(F32).T
    first = c_ref[0] == 0
    kv0, kv1 = kv0_ref[...].astype(F32), kv1_ref[...].astype(F32)
    pair = lambda k: jnp.concatenate(
        [hidden[:, 64 * k : 64 * k + 64], kv0[:, 64 * k : 64 * k + 64]], axis=1
    )
    low, high = pair(0), pair(1)
    keep_ref[0] = jnp.where(first, low, high).astype(BF)
    send_ref[0] = jnp.where(first, high, low).astype(BF)
    turned = pltpu.roll(kv1, 64, 1)
    keep_ref[1] = jnp.where(first, kv1, turned).astype(BF)
    send_ref[1] = jnp.where(first, turned, kv1).astype(BF)


def last(where, received, hidden, kv0, kv1):
    return pl.pallas_call(
        last_kernel,
        grid=(1,),
        in_specs=[
            SMEM, *terms_specs(128), pl.BlockSpec((1, 128, 128), lambda g: (0, 0, 0)),
            whole(128, 128), whole(128, 128),
        ],
        out_specs=[whole(2, 128, 128)] * 2,
        out_shape=[jax.ShapeDtypeStruct((2, 128, 128), BF)] * 2,
        compiler_params=params(),
        name="last",
    )(where, *received, hidden, kv0, kv1)


def arrange_kernel(c_ref, keep_ref, got_ref, out_ref):
    first = c_ref[0] == 0
    for k in range(2):
        keep, got = keep_ref[k].astype(F32), got_ref[k].astype(F32)
        for half in range(2):
            rows = jnp.where(first == (half == 0), keep, got).astype(BF)
            for q in range(4):
                out_ref[4 * half + q, 32 * k : 32 * k + 32, :] = rows[32 * q : 32 * q + 32, :]


def arrange(where, keep, got):
    return pl.pallas_call(
        arrange_kernel,
        grid=(1,),
        in_specs=[SMEM, whole(2, 128, 128), whole(2, 128, 128)],
        out_specs=whole(8, 64, 128),
        out_shape=jax.ShapeDtypeStruct((8, 64, 128), BF),
        compiler_params=params(),
        name="arrange",
    )(where, keep, got)


def origin(where_ref, par_ref, b):
    dp = where_ref[1]
    beam = par_ref[0, par_ref[1, dp * 16 + b]]
    return beam & 15, (beam >> 4) == dp


def reorder_kernel(where_ref, par_ref, own_ref, *refs):
    pieces, (out_ref, held, ready, sems, sem_out) = refs[: len(CHUNKS)], refs[len(CHUNKS) :]
    copies = [pltpu.make_async_copy(own_ref.at[0:125], held.at[0, 0:125], sems.at[0])]
    start = 0
    for k, size in enumerate(CHUNKS):
        copies.append(
            pltpu.make_async_copy(pieces[k], held.at[1, start : start + size], sems.at[k + 1])
        )
        start += size
    for copy in copies:
        copy.start()
    held[0, 125:128] = jnp.zeros((3, 16, 512), BF)
    held[1, 125:128] = jnp.zeros((3, 16, 512), BF)
    row = lax.broadcasted_iota(I32, (128, 256), 0)
    col = lax.broadcasted_iota(I32, (128, 256), 1)
    wanted = jnp.zeros((128, 256), I32)
    for b in range(16):
        slot, here = origin(where_ref, par_ref, b)
        wanted = jnp.where((row & 15) == b, slot + jnp.where(here, 0, 16), wanted)
    same_tap = ((col >> 4) & 7) == (row >> 4)
    pick = (same_tap & ((col & 15) + (col >> 7) * 16 == wanted)).astype(BF)
    for copy in copies:
        copy.wait()
    outs = []
    for k in range(16):
        taps = slice(8 * k, 8 * k + 8)
        both = jnp.concatenate(
            [held[0, taps].reshape(128, 512), held[1, taps].reshape(128, 512)], axis=0
        )
        moved = jnp.dot(pick, both, preferred_element_type=F32).astype(BF)
        ready[taps] = moved.reshape(8, 16, 512)
        size = 8 if k < 15 else 5
        outs.append(
            pltpu.make_async_copy(
                ready.at[8 * k : 8 * k + size], out_ref.at[8 * k + 2 : 8 * k + 2 + size],
                sem_out.at[k],
            )
        )
        outs[-1].start()
    for copy in outs:
        copy.wait()


def reorder(where, parents, own, pieces):
    return pl.pallas_call(
        reorder_kernel,
        in_specs=[SMEM, SMEM, HBM] + [HBM] * len(CHUNKS),
        out_specs=HBM,
        out_shape=jax.ShapeDtypeStruct((127, 16, 512), BF),
        scratch_shapes=[
            pltpu.VMEM((2, 128, 16, 512), BF),
            pltpu.VMEM((128, 16, 512), BF),
            pltpu.SemaphoreType.DMA((len(CHUNKS) + 1,)),
            pltpu.SemaphoreType.DMA((16,)),
        ],
        compiler_params=params(),
        cost_estimate=pl.CostEstimate(flops=1 << 29, bytes_accessed=6 << 20, transcendentals=0),
        name="reorder",
    )(where, parents, own, *pieces)


def final_kernel(
    where_ref, par_ref, r_ref, poles_ref, own_ref, oth_ref, fir_ref,
    hid_ref, fir_out, state_ref, fresh, sem,
):
    wide = lambda row, lane: jnp.concatenate(
        [r_ref[i, row : row + 16, :].astype(F32)[:, lane : lane + 64] for i in range(8)], axis=1
    )
    fresh[0] = wide(16, 64).astype(BF)
    fresh[1] = wide(0, 64).astype(BF)
    copy = pltpu.make_async_copy(fresh, fir_out.at[0:2], sem)
    copy.start()
    for t in range(2):
        hid_ref[t] = wide(16 * t, 0).astype(BF)
    before, now = wide(32, 0), wide(48, 0)
    poles = poles_ref[...]
    for b in range(16):
        slot, here = origin(where_ref, par_ref, b)
        old = jnp.where(here, own_ref[slot], oth_ref[slot].astype(F32))
        state_ref[b] = poles * (poles * old + before[b : b + 1, :]) + now[b : b + 1, :]
    copy.wait()


def final(where, parents, received, poles, own, oth, fir):
    return pl.pallas_call(
        final_kernel,
        grid=(1,),
        in_specs=[
            SMEM, SMEM, whole(8, 64, 128), whole(16, 512), whole(16, 16, 512),
            whole(16, 16, 512), HBM,
        ],
        out_specs=[whole(2, 16, 512), HBM, whole(16, 16, 512)],
        out_shape=[
            jax.ShapeDtypeStruct((2, 16, 512), BF),
            jax.ShapeDtypeStruct((127, 16, 512), BF),
            jax.ShapeDtypeStruct((16, 16, 512), F32),
        ],
        scratch_shapes=[pltpu.VMEM((2, 16, 512), BF), pltpu.SemaphoreType.DMA],
        input_output_aliases={6: 1},
        compiler_params=params(),
        name="final",
    )(where, parents, received, poles, own, oth, fir)


def local(
    tokens, parents, embed_table, norm_gain, weight_in, weight_out, fir_filters, mode_poles,
    residues, fir_cache, modal_state,
):
    dp = lax.axis_index(DP).astype(I32)
    c = lax.axis_index("c").astype(I32)
    where = jnp.stack([c, dp, lax.axis_index("xh").astype(I32), lax.axis_index("z").astype(I32)])
    w_in = weight_in.reshape(2, 3072, 512)
    w_out = weight_out.reshape(2, 1024, 512)
    cache = jnp.transpose(fir_cache, (1, 0, 2))
    e_oth = swap(embed_table, "c")
    g_oth = swap(norm_gain, "c")
    sums, *pieces = make_sums(
        where, tokens, fir_filters, mode_poles, residues, modal_state, cache
    )
    w_in, w_out, e_oth, sums = lax.optimization_barrier((w_in, w_out, e_oth, sums))
    w_in_oth = swap(w_in, "c")
    w_out_oth = swap(w_out, "c")
    moved = []

    def send(trigger):
        piece, trigger, moved[-1:] = lax.optimization_barrier(
            (pieces[len(moved)], trigger, moved[-1:])
        )
        moved.append(swap(piece, "xl"))
        return trigger

    def scatter(terms):
        terms = list(terms)
        for s in (2, 1, 3):
            terms[s] = lax.ppermute(terms[s], "z", [(z, (z + s) % 4) for z in range(4)])
        far = sum(term[1].astype(F32) for term in terms).astype(BF)
        far, moved[-1] = lax.optimization_barrier((far, moved[-1]))
        return *terms, swap(far, "xh")

    idx = indices(where, parents)
    tables = turn(embed_table, e_oth)
    got, idx, tables = lax.optimization_barrier((exchange(sums, DP), idx, tables))
    *partial, embedded, t_send = project_embed(
        where, send(got), tables, norm_gain, g_oth, w_in, w_in_oth
    )
    t_oth = swap(t_send, "c")
    gated, kv0 = mix(0, where, scatter(partial), got, t_oth, idx)
    partial = project_out(
        0, where, send(exchange(gated, DP)), w_out, w_out_oth
    )
    hidden = residual(where, scatter(partial), embedded)
    partial = project_in(
        where, send(exchange(hidden, DP)), norm_gain, g_oth, w_in, w_in_oth
    )
    gated, kv1 = mix(1, where, scatter(partial), got, t_oth, idx)
    partial = project_out(
        1, where, send(exchange(gated, DP)), w_out, w_out_oth
    )
    keep, crossing = last(where, scatter(partial), hidden, kv0, kv1)
    received = exchange(arrange(where, keep, swap(crossing, "c")), DP)
    *moved, state_oth = moved
    fir_before = reorder(where, parents, cache, moved)
    hidden_out, fir_next, state_next = final(
        where, parents, received, mode_poles, modal_state, state_oth, fir_before
    )
    return hidden_out, jnp.transpose(fir_next, (1, 0, 2)), state_next


def solution(mesh):
    fine = Mesh(mesh.devices.reshape(4, 2, 2, 4, 2), ("y", "xl", "xh", "z", "c"))
    return jax.shard_map(
        local,
        mesh=fine,
        in_specs=(
            P(None, DP),
            P(),
            P(None, CHAN),
            P(None, CHAN),
            P(None, None, DP, None, None, CHAN),
            P(None, None, DP, None, CHAN),
            P(CHAN, None),
            P(None, CHAN),
            P(None, CHAN),
            P(DP, None, CHAN),
            P(DP, None, CHAN),
        ),
        out_specs=(P(None, DP, CHAN), P(DP, None, CHAN), P(DP, None, CHAN)),
        check_vma=False,
    )
```

time: 207 us -> 176 us (0.85)
  blocking collectives: 77.8 us -> 30.5 us
  local copies, waits for them, and re-layouts: 26.1 us -> 0.04 us
  waiting for transfers between devices: 21.5 us -> 39.1 us
  starting transfers between devices: 42 us -> 56.4 us
  Pallas kernels: 35.8 us -> 43.5 us
  other arithmetic: 1.31 us -> 4.27 us
    all_to_all x4 -> x3, blocking collectives: 77.8 us -> 30.5 us  [exchange(): return lax.all_to_all(value, axes, 0, 0, tiled=True)]
    ppermute x0 -> x12, waiting for transfers between devices: none -> 20.3 us  [scatter(): terms[s] = lax.ppermute(terms[s], 'z', [(z, (z + s) % 4) for z in range(4)])]
    all_to_all x6 -> x2, starting transfers between devices: 29 us -> 9.21 us  [exchange(): return lax.all_to_all(value, axes, 0, 0, tiled=True)]
    ppermute x8 -> x14, starting transfers between devices: 13.1 us -> 30.9 us  [swap(): return lax.ppermute(value, axis, [(0, 1), (1, 0)])]
    ppermute x0 -> x12, starting transfers between devices: none -> 16.4 us  [scatter(): terms[s] = lax.ppermute(terms[s], 'z', [(z, (z + s) % 4) for z in range(4)])]
    all_to_all x6 -> x2, waiting for transfers between devices: 19.9 us -> 4.37 us  [exchange(): return lax.all_to_all(value, axes, 0, 0, tiled=True)]
    unnamed x38 -> x24, local copies, waits for them, and re-layouts: 15.2 us -> 0.04 us
    ppermute x8 -> x14, waiting for transfers between devices: 1.59 us -> 14.5 us  [swap(): return lax.ppermute(value, axis, [(0, 1), (1, 0)])]
  transfers between devices with their start and end apart: 14 -> 28, of which waited for: 5 -> 19; matrix products, arithmetic and copies ran while one was open for 6% -> 2% of each run, Pallas kernels for 16% -> 17%
where the time goes in v2:
time: 176 us; the launch traced here: 175 us
  starting transfers between devices  56.4 us (32%)
  Pallas kernels  43.5 us (25%)
  waiting for transfers between devices  39.1 us (22%)
  blocking collectives  30.5 us (17%)
  other arithmetic  4.27 us (2%)
    ppermute x14, starting transfers between devices, swap(): return lax.ppermute(value, axis, [(0, 1), (1, 0)])  30.9 us
    all_to_all x3, blocking collectives, exchange(): return lax.all_to_all(value, axes, 0, 0, tiled=True)  30.5 us
    ppermute x12, waiting for transfers between devices, scatter(): terms[s] = lax.ppermute(terms[s], 'z', [(z, (z + s) % 4) for z in range(4)])  20.3 us
    ppermute x12, starting transfers between devices, scatter(): terms[s] = lax.ppermute(terms[s], 'z', [(z, (z + s) % 4) for z in range(4)])  16.4 us
    ppermute x14, waiting for transfers between devices, swap(): return lax.ppermute(value, axis, [(0, 1), (1, 0)])  14.5 us
    all_to_all x2, starting transfers between devices, exchange(): return lax.all_to_all(value, axes, 0, 0, tiled=True)  9.21 us
    pallas_call x1, Pallas kernels, project_embed(): pl.pallas_call(embed_kernel, grid=(2,), in_specs=[SMEM, whole(8, 72, 128)...  6.02 us
    pallas_call x2, Pallas kernels, project_out(): pl.pallas_call(out_kernel, grid=(2,), in_specs=[SMEM, whole(8, 128, 128),...  5.94 us
  transfers between devices with their start and end apart: 28, of which 19 were waited for; matrix products, arithmetic and copies ran while one was open for 2% of the time, Pallas kernels for 17%

profile of v2, /device:TPU:1, one launch (start us, length us, event | category | flops | bytes accessed | tf_op | source)
XLA Modules:
  0.0 174.8 jit_solution(13163428087812619028)
XLA Ops:
  0.6 1.5 collective-permute-start
  2.7 4.5 %state_sums.1 = (f32[8,72,128]{2,1,0:T(8,128)}, bf16[48,16,512]{2,1,0:T(8,128)(2,1)}, bf16[29,16,512]{2,1,0:T(8,128)(2,1)}, bf16[48,16,512]{2,1,0:T(8,128)(2,1)}, bf16[16,16,512]{2,1,0:T(8,128)(2,1)}) custom-call(s32[4]{0:T(128)} %pad_add_fusion.c_ref.refs_0_.where_ref, s32[2,16]{1,0:T(2,128)} %tok_ref.1, f32[32,128]{1,0:T(8,128)} %filt_ref.1, ...), custom_call_target="tpu_custom_call" | custom-call | tf_op jit(solution)/shard_map/state_sums/pallas_call | solution.py:108
  7.8 5.2 %all-to-all-start = ((f32[8,72,128]{2,1,0:T(8,128)}), f32[8,72,128]{2,1,0:T(8,128)}, u32[]{:S(2)}, u32[]{:S(2)}) async-start(f32[8,72,128]{2,1,0:T(8,128)} %get-tuple-element.66), calls=%async_computation | async-start | bytes 589824 | tf_op jit(solution)/shard_map/all_to_all | solution.py:37
  13.1 1.8 %indices.1.refs_8_ = s32[8,128]{1,0:T(8,128)} custom-call(s32[4]{0:T(128)} %pad_add_fusion.c_ref.refs_0_.where_ref, s32[2,128]{1,0:T(2,128)} %par_ref.5), custom_call_target="tpu_custom_call" | custom-call | tf_op jit(solution)/shard_map/indices/pallas_call | solution.py:152
  14.8 2.5 %turn.1.tables = bf16[2,512,512]{2,1,0:T(8,128)(2,1)} custom-call(bf16[512,512]{1,0:T(8,128)(2,1)} %own_ref.2, bf16[512,512]{1,0:T(8,128)(2,1)} %collective-permute-done.oth_ref), custom_call_target="tpu_custom_call" | custom-call | tf_op jit(solution)/shard_map/turn/pallas_call | solution.py:169
  17.3 3.2 %all-to-all-done.got_ref.refs_6_ = f32[8,72,128]{2,1,0:T(8,128)} async-done(((f32[8,72,128]{2,1,0:T(8,128)}), f32[8,72,128]{2,1,0:T(8,128)}, u32[]{:S(2)}, u32[]{:S(2)}) %all-to-all-start) | async-done | bytes 294944 | tf_op jit(solution)/shard_map/all_to_all | solution.py:37
  20.8 1.8 %collective-permute-start.1 = (f32[2,512]{1,0:T(2,128)}, f32[2,512]{1,0:T(2,128)}, u32[]{:S(2)}, u32[]{:S(2)}) collective-permute-start(f32[2,512]{1,0:T(2,128)} %g_own.3), channel_id=1, source_target_pairs={{0,1},{1,0},{2,3},{3,2},{4,5},{5,4},{6,7},{7,6},{8,9},{9,8},{10,11... | collective-permute-start | bytes 12296 | tf_op jit(solution)/shard_map/ppermute | solution.py:33
  22.6 1.2 collective-permute-done.1.g_oth
  23.8 6.0 %embed_project.1 = (bf16[2,400,128]{2,1,0:T(8,128)(2,1)}, bf16[2,400,128]{2,1,0:T(8,128)(2,1)}, bf16[2,400,128]{2,1,0:T(8,128)(2,1)}, bf16[2,400,128]{2,1,0:T(8,...) custom-call(s32[4]{0:T(128)} %pad_add_fusion.c_ref.refs_0_.where_ref, ...), custom_call_target="tpu_custom_call" | custom-call | flops 805306368 | bytes 7340032 | tf_op jit(solution)/shard_map/embed_project/pallas_call | solution.py:249
  29.8 1.7 collective-permute-start.3
  31.5 3.3 %collective-permute-start.4 = (bf16[2,400,128]{2,1,0:T(8,128)(2,1)}, bf16[2,400,128]{2,1,0:T(8,128)(2,1)S(1)}, u32[]{:S(2)}, u32[]{:S(2)}) collective-permute-start(bf16[2,400,128]{2,1,0:T(8,128)(2,1)} %get-tuple-element.74), channel_id=1, source_target_pairs={{0,4},{2,6},{4,0},{6,2},{1,5},{3,7},{5,1},{7,3},{8,12},{10,14},{12... | collective-permute-start | bytes 614408 | tf_op jit(solution)/shard_map/ppermute | solution.py:613
  35.6 3.5 %collective-permute-done.3.refs_2_ = bf16[2,400,128]{2,1,0:T(8,128)(2,1)S(1)} collective-permute-done((bf16[2,400,128]{2,1,0:T(8,128)(2,1)}, bf16[2,400,128]{2,1,0:T(8,128)(2,1)S(1)}, u32[]{:S(2)}, u32[]{:S(2)}) %collective-permute-start.3) | collective-permute-done | bytes 204832 | tf_op jit(solution)/shard_map/ppermute | solution.py:613
  39.9 4.4 %collective-permute-done.4.refs_3_ = bf16[2,400,128]{2,1,0:T(8,128)(2,1)S(1)} collective-permute-done((bf16[2,400,128]{2,1,0:T(8,128)(2,1)}, bf16[2,400,128]{2,1,0:T(8,128)(2,1)S(1)}, u32[]{:S(2)}, u32[]{:S(2)}) %collective-permute-start.4) | collective-permute-done | bytes 204832 | tf_op jit(solution)/shard_map/ppermute | solution.py:613
  44.3 1.1 fusion
  45.4 2.5 %collective-permute-start.7 = (bf16[400,128]{1,0:T(8,128)(2,1)S(1)}, bf16[400,128]{1,0:T(8,128)(2,1)}, u32[]{:S(2)}, u32[]{:S(2)}) collective-permute-start(bf16[400,128]{1,0:T(8,128)(2,1)S(1)} %fusion), channel_id=1, source_target_pairs={{0,8},{8,0},{1,9},{9,1},{2,10},{10,2},{3,11},{11,3},{4,12},{12,4},... | collective-permute-start | bytes 307208 | tf_op jit(solution)/shard_map/ppermute | solution.py:33
  48.0 2.7 %collective-permute-done.7.refs_5_ = bf16[400,128]{1,0:T(8,128)(2,1)} collective-permute-done((bf16[400,128]{1,0:T(8,128)(2,1)S(1)}, bf16[400,128]{1,0:T(8,128)(2,1)}, u32[]{:S(2)}, u32[]{:S(2)}) %collective-permute-start.7) | collective-permute-done | bytes 102432 | tf_op jit(solution)/shard_map/ppermute | solution.py:33
  50.6 2.5 %mix.2 = (bf16[8,128,128]{2,1,0:T(8,128)(2,1)}, bf16[128,128]{1,0:T(8,128)(2,1)}) custom-call(s32[4]{0:T(128)} %pad_add_fusion.c_ref.refs_0_.where_ref, bf16[2,400,128]{2,1,0:T(8,128)(2,1)} %get-tuple-element.72.refs_1_, bf16[2,400,128]{2,1,0:T(8,128)(2,1)} %copy-done, bf16[2,400,128]{2,1,0:T(8,128)(2,1)} %copy-done.1, bf16[2,400,128]{2,1,0:T(8,128)(2,1)} %copy-done.3, ...), custom_call_target="tpu_custom_call" | custom-call | tf_op jit(solution)/shard_map/mix/pallas_call | solution.py:352
  53.2 10.2 %all_to_all.25.a_ref = bf16[8,128,128]{2,1,0:T(8,128)(2,1)} all-to-all(bf16[8,128,128]{2,1,0:T(8,128)(2,1)} %get-tuple-element.80), channel_id=1, replica_groups=mesh['y'=4,'xl'=2,'xh'=2,'z'=4,'c'=2] {'y','xl'}, dimensions={0} | all-to-all | bytes 524288 | tf_op jit(solution)/shard_map/all_to_all | solution.py:37
  63.9 3.0 %project_out.2 = (bf16[2,128,128]{2,1,0:T(8,128)(2,1)}, bf16[2,128,128]{2,1,0:T(8,128)(2,1)}, bf16[2,128,128]{2,1,0:T(8,128)(2,1)}, bf16[2,128,128]{2,1,0:T(8,128)(2,1)}) custom-call(s32[4]{0:T(128)} %pad_add_fusion.c_ref.refs_0_.where_ref, bf16[8,128,128]{2,1,0:T(8,128)(2,1)} %all_to_all.25.a_ref, bf16[2,1024,512]{2,1,0:T(8,128)(2,1)} %bitcast.20, ...), custom_call_target="tpu_custom_call" | custom-call | flops 268435456 | bytes 2621440 | tf_op jit(solution)/shard_map/project_out/pallas_call | solution.py:382
  66.9 1.2 collective-permute-start.10
  68.1 2.9 %collective-permute-start.11 = (bf16[2,128,128]{2,1,0:T(8,128)(2,1)}, bf16[2,128,128]{2,1,0:T(8,128)(2,1)S(1)}, u32[]{:S(2)}, u32[]{:S(2)}) collective-permute-start(bf16[2,128,128]{2,1,0:T(8,128)(2,1)} %get-tuple-element.86), channel_id=1, source_target_pairs={{0,4},{2,6},{4,0},{6,2},{1,5},{3,7},{5,1},{7,3},{8,12},{10,14},{12... | collective-permute-start | bytes 196616 | tf_op jit(solution)/shard_map/ppermute | solution.py:613
  71.7 1.9 %collective-permute-done.11.refs_2_ = bf16[2,128,128]{2,1,0:T(8,128)(2,1)S(1)} collective-permute-done((bf16[2,128,128]{2,1,0:T(8,128)(2,1)}, bf16[2,128,128]{2,1,0:T(8,128)(2,1)S(1)}, u32[]{:S(2)}, u32[]{:S(2)}) %collective-permute-start.11) | collective-permute-done | bytes 65568 | tf_op jit(solution)/shard_map/ppermute | solution.py:613
  73.6 1.2 collective-permute-done.12.refs_3_
  75.6 2.5 %collective-permute-start.14 = (bf16[128,128]{1,0:T(8,128)(2,1)S(1)}, bf16[128,128]{1,0:T(8,128)(2,1)}, u32[]{:S(2)}, u32[]{:S(2)}) collective-permute-start(bf16[128,128]{1,0:T(8,128)(2,1)S(1)} %fusion.2), channel_id=1, source_target_pairs={{0,8},{8,0},{1,9},{9,1},{2,10},{10,2},{3,11},{11,3},{4,12},{12,4},... | collective-permute-start | bytes 98312 | tf_op jit(solution)/shard_map/ppermute | solution.py:33
  78.1 1.9 %collective-permute-done.14.refs_4_ = bf16[128,128]{1,0:T(8,128)(2,1)} collective-permute-done((bf16[128,128]{1,0:T(8,128)(2,1)S(1)}, bf16[128,128]{1,0:T(8,128)(2,1)}, u32[]{:S(2)}, u32[]{:S(2)}) %collective-permute-start.14) | collective-permute-done | bytes 32800 | tf_op jit(solution)/shard_map/ppermute | solution.py:33
  80.0 1.8 %residual.1.refs_5_ = bf16[8,128,128]{2,1,0:T(8,128)(2,1)} custom-call(s32[4]{0:T(128)} %pad_add_fusion.c_ref.refs_0_.where_ref, bf16[2,128,128]{2,1,0:T(8,128)(2,1)} %get-tuple-element.84.refs_0_, bf16[2,128,128]{2,1,0:T(8,128)(2,1)} %copy-done.9, bf16[2,128,128]{2,1,0:T(8,128)(2,1)} %copy-done.10, bf16[2,128,128]{2,1,0:T(8,128)(2,1)} %copy-done.11, ...), custom_call_target="tpu_custom_call" | custom-call | tf_op jit(solution)/shard_map/residual/pallas_call | solution.py:408
  81.8 10.2 %all_to_all.26.a_ref = bf16[8,128,128]{2,1,0:T(8,128)(2,1)} all-to-all(bf16[8,128,128]{2,1,0:T(8,128)(2,1)} %residual.1.refs_5_), channel_id=1, replica_groups=mesh['y'=4,'xl'=2,'xh'=2,'z'=4,'c'=2] {'y','xl'}, dimensions={0} | all-to-all | bytes 524288 | tf_op jit(solution)/shard_map/all_to_all | solution.py:37
  92.6 5.3 %norm_project.1 = (bf16[2,400,128]{2,1,0:T(8,128)(2,1)}, bf16[2,400,128]{2,1,0:T(8,128)(2,1)}, bf16[2,400,128]{2,1,0:T(8,128)(2,1)}, bf16[2,400,128]{2,1,0:T(8,128)(2,1)}) custom-call(s32[4]{0:T(128)} %pad_add_fusion.c_ref.refs_0_.where_ref, bf16[8,128,128]{2,1,0:T(8,128)(2,1)} %all_to_all.26.a_ref, f32[2,512]{1,0:T(2,128)} %g_own.3, ...), custom_call_target="tpu_custom_call" | custom-call | flops 805306368 | bytes 7340032 | tf_op jit(solution)/shard_map/norm_project/pallas_call | solution.py:290
  97.9 2.3 %collective-permute-start.16 = (bf16[2,400,128]{2,1,0:T(8,128)(2,1)}, bf16[2,400,128]{2,1,0:T(8,128)(2,1)S(1)}, u32[]{:S(2)}, u32[]{:S(2)}) collective-permute-start(bf16[2,400,128]{2,1,0:T(8,128)(2,1)} %get-tuple-element.95), channel_id=1, source_target_pairs={{0,4},{2,6},{4,0},{6,2},{1,5},{3,7},{5,1},{7,3},{8,12},{10,14},{12... | collective-permute-start | bytes 614408 | tf_op jit(solution)/shard_map/ppermute | solution.py:613
  101.1 4.9 %collective-permute-done.15.refs_2_ = bf16[2,400,128]{2,1,0:T(8,128)(2,1)S(1)} collective-permute-done((bf16[2,400,128]{2,1,0:T(8,128)(2,1)}, bf16[2,400,128]{2,1,0:T(8,128)(2,1)S(1)}, u32[]{:S(2)}, u32[]{:S(2)}) %collective-permute-start.15) | collective-permute-done | bytes 204832 | tf_op jit(solution)/shard_map/ppermute | solution.py:613
  108.2 2.7 %collective-permute-start.19 = (bf16[400,128]{1,0:T(8,128)(2,1)S(1)}, bf16[400,128]{1,0:T(8,128)(2,1)}, u32[]{:S(2)}, u32[]{:S(2)}) collective-permute-start(bf16[400,128]{1,0:T(8,128)(2,1)S(1)} %fusion.1), channel_id=1, source_target_pairs={{0,8},{8,0},{1,9},{9,1},{2,10},{10,2},{3,11},{11,3},{4,12},{12,4},... | collective-permute-start | bytes 307208 | tf_op jit(solution)/shard_map/ppermute | solution.py:33
  110.9 3.5 %collective-permute-done.19.refs_5_ = bf16[400,128]{1,0:T(8,128)(2,1)} collective-permute-done((bf16[400,128]{1,0:T(8,128)(2,1)S(1)}, bf16[400,128]{1,0:T(8,128)(2,1)}, u32[]{:S(2)}, u32[]{:S(2)}) %collective-permute-start.19) | collective-permute-done | bytes 102432 | tf_op jit(solution)/shard_map/ppermute | solution.py:33
  114.4 2.5 %mix.3 = (bf16[8,128,128]{2,1,0:T(8,128)(2,1)}, bf16[128,128]{1,0:T(8,128)(2,1)}) custom-call(s32[4]{0:T(128)} %pad_add_fusion.c_ref.refs_0_.where_ref, bf16[2,400,128]{2,1,0:T(8,128)(2,1)} %get-tuple-element.93.refs_1_, bf16[2,400,128]{2,1,0:T(8,128)(2,1)} %copy-done.2, bf16[2,400,128]{2,1,0:T(8,128)(2,1)} %copy-done.4, bf16[2,400,128]{2,1,0:T(8,128)(2,1)} %copy-done.5, ...), custom_call_target="tpu_custom_call" | custom-call | tf_op jit(solution)/shard_map/mix/pallas_call | solution.py:352
  117.0 10.2 %all_to_all.27.a_ref = bf16[8,128,128]{2,1,0:T(8,128)(2,1)} all-to-all(bf16[8,128,128]{2,1,0:T(8,128)(2,1)} %get-tuple-element.99), channel_id=1, replica_groups=mesh['y'=4,'xl'=2,'xh'=2,'z'=4,'c'=2] {'y','xl'}, dimensions={0} | all-to-all | bytes 524288 | tf_op jit(solution)/shard_map/all_to_all | solution.py:37
  127.1 3.0 %project_out.3 = (bf16[2,128,128]{2,1,0:T(8,128)(2,1)}, bf16[2,128,128]{2,1,0:T(8,128)(2,1)}, bf16[2,128,128]{2,1,0:T(8,128)(2,1)}, bf16[2,128,128]{2,1,0:T(8,128)(2,1)}) custom-call(s32[4]{0:T(128)} %pad_add_fusion.c_ref.refs_0_.where_ref, bf16[8,128,128]{2,1,0:T(8,128)(2,1)} %all_to_all.27.a_ref, bf16[2,1024,512]{2,1,0:T(8,128)(2,1)} %bitcast.21, ...), custom_call_target="tpu_custom_call" | custom-call | flops 268435456 | bytes 2621440 | tf_op jit(solution)/shard_map/project_out/pallas_call | solution.py:382
  130.2 2.9 %collective-permute-start.21 = (bf16[2,128,128]{2,1,0:T(8,128)(2,1)}, bf16[2,128,128]{2,1,0:T(8,128)(2,1)S(1)}, u32[]{:S(2)}, u32[]{:S(2)}) collective-permute-start(bf16[2,128,128]{2,1,0:T(8,128)(2,1)} %get-tuple-element.104), channel_id=1, source_target_pairs={{0,4},{2,6},{4,0},{6,2},{1,5},{3,7},{5,1},{7,3},{8,12},{10,14},{12... | collective-permute-start | bytes 196616 | tf_op jit(solution)/shard_map/ppermute | solution.py:613
  133.8 1.2 collective-permute-done.20.refs_1_
  137.4 1.4 collective-permute-done.23.oth_ref
  138.8 1.9 %collective-permute-start.24 = (bf16[128,128]{1,0:T(8,128)(2,1)S(1)}, bf16[128,128]{1,0:T(8,128)(2,1)}, u32[]{:S(2)}, u32[]{:S(2)}) collective-permute-start(bf16[128,128]{1,0:T(8,128)(2,1)S(1)} %fusion.3), channel_id=1, source_target_pairs={{0,8},{8,0},{1,9},{9,1},{2,10},{10,2},{3,11},{11,3},{4,12},{12,4},... | collective-permute-start | bytes 98312 | tf_op jit(solution)/shard_map/ppermute | solution.py:33
  140.7 2.5 %collective-permute-done.24.refs_4_ = bf16[128,128]{1,0:T(8,128)(2,1)} collective-permute-done((bf16[128,128]{1,0:T(8,128)(2,1)S(1)}, bf16[128,128]{1,0:T(8,128)(2,1)}, u32[]{:S(2)}, u32[]{:S(2)}) %collective-permute-start.24) | collective-permute-done | bytes 32800 | tf_op jit(solution)/shard_map/ppermute | solution.py:33
  143.2 1.7 last.1
  144.9 14.5 %collective-permute-start.25 = (bf16[2,128,128]{2,1,0:T(8,128)(2,1)}, bf16[2,128,128]{2,1,0:T(8,128)(2,1)}, u32[]{:S(2)}, u32[]{:S(2)}) collective-permute-start(bf16[2,128,128]{2,1,0:T(8,128)(2,1)} %get-tuple-element.111), channel_id=1, source_target_pairs={{0,1},{1,0},{2,3},{3,2},{4,5},{5,4},{6,7},{7,6},{8,9},{9,8},{10,11... | collective-permute-start | bytes 196616 | tf_op jit(solution)/shard_map/ppermute | solution.py:33
  159.4 1.2 collective-permute-done.25.got_ref
  160.7 1.6 arrange.1
  162.2 4.0 %all-to-all-start.4 = ((bf16[8,64,128]{2,1,0:T(8,128)(2,1)}), bf16[8,64,128]{2,1,0:T(8,128)(2,1)}, u32[]{:S(2)}, u32[]{:S(2)}) async-start(bf16[8,64,128]{2,1,0:T(8,128)(2,1)} %arrange.1), calls=%async_computation.4 | async-start | bytes 262144 | tf_op jit(solution)/shard_map/all_to_all | solution.py:37
  166.2 4.5 %reorder.1.fir_ref = bf16[127,16,512]{2,1,0:T(8,128)(2,1)} custom-call(s32[4]{0:T(128)} %pad_add_fusion.c_ref.refs_0_.where_ref, s32[2,128]{1,0:T(2,128)} %par_ref.5, bf16[127,16,512]{2,1,0:T(8,128)(2,1)} %bitcast.23, bf16[48,16,512]{2,1,0:T(8,128)(2,1)} %collective-permute-done.6.refs_0_, bf16[29,16,512]{2,1,0:T(8,128)(2,1)} %collective-permute-done.13.refs_1_, ...), custom_call_target="tpu_custom_call" | custom-call | flops 536870912 | bytes 6291456 | tf_op jit(solution)/shard_map/reorder/pallas_call | solution.py:523
  170.7 1.1 all-to-all-done.4.r_ref
  171.9 2.8 %final.1 = (bf16[2,16,512]{2,1,0:T(8,128)(2,1)}, bf16[127,16,512]{2,1,0:T(8,128)(2,1)}, f32[16,16,512]{2,1,0:T(8,128)}) custom-call(s32[4]{0:T(128)} %pad_add_fusion.c_ref.refs_0_.where_ref, s32[2,128]{1,0:T(2,128)} %par_ref.5, bf16[8,64,128]{2,1,0:T(8,128)(2,1)} %all-to-all-done.4.r_ref, f32[16,512]{1,0:T(8,128)} %poles_ref.3, ...), custom_call_target="tpu_custom_call", output_to_operand_aliasing={{1}: (6, {})} | custom-call | tf_op jit(solution)/shard_map/final/pallas_call | solution.py:563
  (54 shorter events, 12.0 us)
Async XLA Ops:
  0.6 6.6 %collective-permute-start = (bf16[512,512]{1,0:T(8,128)(2,1)}, bf16[512,512]{1,0:T(8,128)(2,1)}, u32[]{:S(2)}, u32[]{:S(2)}) collective-permute-start(bf16[512,512]{1,0:T(8,128)(2,1)} %own_ref.2), channel_id=1, source_target_pairs={{0,1},{1,0},{2,3},{3,2},{4,5},{5,4},{6,7},{7,6},{8,9},{9,8},{10,11... | collective-permute-start | bytes 1572872 | tf_op jit(solution)/shard_map/ppermute | solution.py:33
  7.3 16.5 %collective-permute-start.2 = (bf16[2,3072,512]{2,1,0:T(8,128)(2,1)}, bf16[2,3072,512]{2,1,0:T(8,128)(2,1)}, u32[]{:S(2)}, u32[]{:S(2)}) collective-permute-start(bf16[2,3072,512]{2,1,0:T(8,128)(2,1)} %bitcast.16), channel_id=1, source_target_pairs={{0,1},{1,0},{2,3},{3,2},{4,5},{5,4},{6,7},{7,6},{8,9},{9,8},{10,11... | collective-permute-start | bytes 18874376 | tf_op jit(solution)/shard_map/ppermute | solution.py:33
  7.4 56.5 %collective-permute-start.9 = (bf16[2,1024,512]{2,1,0:T(8,128)(2,1)}, bf16[2,1024,512]{2,1,0:T(8,128)(2,1)}, u32[]{:S(2)}, u32[]{:S(2)}) collective-permute-start(bf16[2,1024,512]{2,1,0:T(8,128)(2,1)} %bitcast.19), channel_id=1, source_target_pairs={{0,1},{1,0},{2,3},{3,2},{4,5},{5,4},{6,7},{7,6},{8,9},{9,8},{10,11... | collective-permute-start | bytes 6291464 | tf_op jit(solution)/shard_map/ppermute | solution.py:33
  7.8 12.7 %all-to-all-start = ((f32[8,72,128]{2,1,0:T(8,128)}), f32[8,72,128]{2,1,0:T(8,128)}, u32[]{:S(2)}, u32[]{:S(2)}) async-start(f32[8,72,128]{2,1,0:T(8,128)} %get-tuple-element.66), calls=%async_computation | async-start | bytes 589824 | tf_op jit(solution)/shard_map/all_to_all | solution.py:37
  20.6 24.8 %collective-permute-start.6 = (bf16[48,16,512]{2,1,0:T(8,128)(2,1)}, bf16[48,16,512]{2,1,0:T(8,128)(2,1)}, u32[]{:S(2)}, u32[]{:S(2)}) collective-permute-start(bf16[48,16,512]{2,1,0:T(8,128)(2,1)} %get-tuple-element.76), channel_id=1, source_target_pairs={{0,16},{16,0},{1,17},{17,1},{2,18},{18,2},{3,19},{19,3},{4,20},{20... | collective-permute-start | bytes 2359304 | tf_op jit(solution)/shard_map/ppermute | solution.py:33
  20.8 2.9 %collective-permute-start.1 = (f32[2,512]{1,0:T(2,128)}, f32[2,512]{1,0:T(2,128)}, u32[]{:S(2)}, u32[]{:S(2)}) collective-permute-start(f32[2,512]{1,0:T(2,128)} %g_own.3), channel_id=1, source_target_pairs={{0,1},{1,0},{2,3},{3,2},{4,5},{5,4},{6,7},{7,6},{8,9},{9,8},{10,11... | collective-permute-start | bytes 12296 | tf_op jit(solution)/shard_map/ppermute | solution.py:33
  29.8 9.2 %collective-permute-start.3 = (bf16[2,400,128]{2,1,0:T(8,128)(2,1)}, bf16[2,400,128]{2,1,0:T(8,128)(2,1)S(1)}, u32[]{:S(2)}, u32[]{:S(2)}) collective-permute-start(bf16[2,400,128]{2,1,0:T(8,128)(2,1)} %get-tuple-element.73), channel_id=1, source_target_pairs={{0,2},{2,4},{4,6},{6,0},{1,3},{3,5},{5,7},{7,1},{8,10},{10,12},{12... | collective-permute-start | bytes 614408 | tf_op jit(solution)/shard_map/ppermute | solution.py:613
  31.5 12.8 %collective-permute-start.4 = (bf16[2,400,128]{2,1,0:T(8,128)(2,1)}, bf16[2,400,128]{2,1,0:T(8,128)(2,1)S(1)}, u32[]{:S(2)}, u32[]{:S(2)}) collective-permute-start(bf16[2,400,128]{2,1,0:T(8,128)(2,1)} %get-tuple-element.74), channel_id=1, source_target_pairs={{0,4},{2,6},{4,0},{6,2},{1,5},{3,7},{5,1},{7,3},{8,12},{10,14},{12... | collective-permute-start | bytes 614408 | tf_op jit(solution)/shard_map/ppermute | solution.py:613
  34.8 9.4 %collective-permute-start.5 = (bf16[2,400,128]{2,1,0:T(8,128)(2,1)}, bf16[2,400,128]{2,1,0:T(8,128)(2,1)S(1)}, u32[]{:S(2)}, u32[]{:S(2)}) collective-permute-start(bf16[2,400,128]{2,1,0:T(8,128)(2,1)} %get-tuple-element.75), channel_id=1, source_target_pairs={{0,6},{2,0},{4,2},{6,4},{1,7},{3,1},{5,3},{7,5},{8,14},{10,8},{12,... | collective-permute-start | bytes 614408 | tf_op jit(solution)/shard_map/ppermute | solution.py:613
  39.0 5.3 %copy-start = (bf16[2,400,128]{2,1,0:T(8,128)(2,1)}, bf16[2,400,128]{2,1,0:T(8,128)(2,1)S(1)}, u32[]{:S(2)}) copy-start(bf16[2,400,128]{2,1,0:T(8,128)(2,1)S(1)} %collective-permute-done.3.refs_2_) | copy-start | bytes 614404
  39.0 8.9 %collective-permute-start.8 = (f32[4,64,128]{2,1,0:T(8,128)}, f32[4,64,128]{2,1,0:T(8,128)}, u32[]{:S(2)}, u32[]{:S(2)}) collective-permute-start(f32[4,64,128]{2,1,0:T(8,128)} %get-tuple-element.78), channel_id=1, source_target_pairs={{0,1},{1,0},{2,3},{3,2},{4,5},{5,4},{6,7},{7,6},{8,9},{9,8},{10,11... | collective-permute-start | bytes 393224 | tf_op jit(solution)/shard_map/ppermute | solution.py:33
  44.3 1.1 copy-start.1
  44.3 1.1 copy-start.3
  45.4 5.2 %collective-permute-start.7 = (bf16[400,128]{1,0:T(8,128)(2,1)S(1)}, bf16[400,128]{1,0:T(8,128)(2,1)}, u32[]{:S(2)}, u32[]{:S(2)}) collective-permute-start(bf16[400,128]{1,0:T(8,128)(2,1)S(1)} %fusion), channel_id=1, source_target_pairs={{0,8},{8,0},{1,9},{9,1},{2,10},{10,2},{3,11},{11,3},{4,12},{12,4},... | collective-permute-start | bytes 307208 | tf_op jit(solution)/shard_map/ppermute | solution.py:33
  63.3 12.2 %collective-permute-start.13 = (bf16[29,16,512]{2,1,0:T(8,128)(2,1)}, bf16[29,16,512]{2,1,0:T(8,128)(2,1)}, u32[]{:S(2)}, u32[]{:S(2)}) collective-permute-start(bf16[29,16,512]{2,1,0:T(8,128)(2,1)} %get-tuple-element.88), channel_id=1, source_target_pairs={{0,16},{16,0},{1,17},{17,1},{2,18},{18,2},{3,19},{19,3},{4,20},{20... | collective-permute-start | bytes 1425416 | tf_op jit(solution)/shard_map/ppermute | solution.py:33
  66.9 4.8 %collective-permute-start.10 = (bf16[2,128,128]{2,1,0:T(8,128)(2,1)}, bf16[2,128,128]{2,1,0:T(8,128)(2,1)S(1)}, u32[]{:S(2)}, u32[]{:S(2)}) collective-permute-start(bf16[2,128,128]{2,1,0:T(8,128)(2,1)} %get-tuple-element.85), channel_id=1, source_target_pairs={{0,2},{2,4},{4,6},{6,0},{1,3},{3,5},{5,7},{7,1},{8,10},{10,12},{12... | collective-permute-start | bytes 196616 | tf_op jit(solution)/shard_map/ppermute | solution.py:613
  68.1 5.5 %collective-permute-start.11 = (bf16[2,128,128]{2,1,0:T(8,128)(2,1)}, bf16[2,128,128]{2,1,0:T(8,128)(2,1)S(1)}, u32[]{:S(2)}, u32[]{:S(2)}) collective-permute-start(bf16[2,128,128]{2,1,0:T(8,128)(2,1)} %get-tuple-element.86), channel_id=1, source_target_pairs={{0,4},{2,6},{4,0},{6,2},{1,5},{3,7},{5,1},{7,3},{8,12},{10,14},{12... | collective-permute-start | bytes 196616 | tf_op jit(solution)/shard_map/ppermute | solution.py:613
  71.0 3.7 %collective-permute-start.12 = (bf16[2,128,128]{2,1,0:T(8,128)(2,1)}, bf16[2,128,128]{2,1,0:T(8,128)(2,1)S(1)}, u32[]{:S(2)}, u32[]{:S(2)}) collective-permute-start(bf16[2,128,128]{2,1,0:T(8,128)(2,1)} %get-tuple-element.87), channel_id=1, source_target_pairs={{0,6},{2,0},{4,2},{6,4},{1,7},{3,1},{5,3},{7,5},{8,14},{10,8},{12,... | collective-permute-start | bytes 196616 | tf_op jit(solution)/shard_map/ppermute | solution.py:613
  71.7 3.1 %copy-start.9 = (bf16[2,128,128]{2,1,0:T(8,128)(2,1)}, bf16[2,128,128]{2,1,0:T(8,128)(2,1)S(1)}, u32[]{:S(2)}) copy-start(bf16[2,128,128]{2,1,0:T(8,128)(2,1)S(1)} %collective-permute-done.10.refs_1_) | copy-start | bytes 196612
  73.6 2.0 %copy-start.10 = (bf16[2,128,128]{2,1,0:T(8,128)(2,1)}, bf16[2,128,128]{2,1,0:T(8,128)(2,1)S(1)}, u32[]{:S(2)}) copy-start(bf16[2,128,128]{2,1,0:T(8,128)(2,1)S(1)} %collective-permute-done.11.refs_2_) | copy-start | bytes 196612
  74.8 0.8 copy-start.11
  75.6 4.5 %collective-permute-start.14 = (bf16[128,128]{1,0:T(8,128)(2,1)S(1)}, bf16[128,128]{1,0:T(8,128)(2,1)}, u32[]{:S(2)}, u32[]{:S(2)}) collective-permute-start(bf16[128,128]{1,0:T(8,128)(2,1)S(1)} %fusion.2), channel_id=1, source_target_pairs={{0,8},{8,0},{1,9},{9,1},{2,10},{10,2},{3,11},{11,3},{4,12},{12,4},... | collective-permute-start | bytes 98312 | tf_op jit(solution)/shard_map/ppermute | solution.py:33
  92.0 16.2 %collective-permute-start.18 = (bf16[48,16,512]{2,1,0:T(8,128)(2,1)}, bf16[48,16,512]{2,1,0:T(8,128)(2,1)}, u32[]{:S(2)}, u32[]{:S(2)}) collective-permute-start(bf16[48,16,512]{2,1,0:T(8,128)(2,1)} %get-tuple-element.97), channel_id=1, source_target_pairs={{0,16},{16,0},{1,17},{17,1},{2,18},{18,2},{3,19},{19,3},{4,20},{20... | collective-permute-start | bytes 2359304 | tf_op jit(solution)/shard_map/ppermute | solution.py:33
  97.9 8.2 %collective-permute-start.15 = (bf16[2,400,128]{2,1,0:T(8,128)(2,1)}, bf16[2,400,128]{2,1,0:T(8,128)(2,1)S(1)}, u32[]{:S(2)}, u32[]{:S(2)}) collective-permute-start(bf16[2,400,128]{2,1,0:T(8,128)(2,1)} %get-tuple-element.94), channel_id=1, source_target_pairs={{0,2},{2,4},{4,6},{6,0},{1,3},{3,5},{5,7},{7,1},{8,10},{10,12},{12... | collective-permute-start | bytes 614408 | tf_op jit(solution)/shard_map/ppermute | solution.py:613
  97.9 8.2 %collective-permute-start.16 = (bf16[2,400,128]{2,1,0:T(8,128)(2,1)}, bf16[2,400,128]{2,1,0:T(8,128)(2,1)S(1)}, u32[]{:S(2)}, u32[]{:S(2)}) collective-permute-start(bf16[2,400,128]{2,1,0:T(8,128)(2,1)} %get-tuple-element.95), channel_id=1, source_target_pairs={{0,4},{2,6},{4,0},{6,2},{1,5},{3,7},{5,1},{7,3},{8,12},{10,14},{12... | collective-permute-start | bytes 614408 | tf_op jit(solution)/shard_map/ppermute | solution.py:613
  100.2 6.9 %collective-permute-start.17 = (bf16[2,400,128]{2,1,0:T(8,128)(2,1)}, bf16[2,400,128]{2,1,0:T(8,128)(2,1)S(1)}, u32[]{:S(2)}, u32[]{:S(2)}) collective-permute-start(bf16[2,400,128]{2,1,0:T(8,128)(2,1)} %get-tuple-element.96), channel_id=1, source_target_pairs={{0,6},{2,0},{4,2},{6,4},{1,7},{3,1},{5,3},{7,5},{8,14},{10,8},{12,... | collective-permute-start | bytes 614408 | tf_op jit(solution)/shard_map/ppermute | solution.py:613
  106.1 1.0 copy-start.2
  106.1 2.1 %copy-start.4 = (bf16[2,400,128]{2,1,0:T(8,128)(2,1)}, bf16[2,400,128]{2,1,0:T(8,128)(2,1)S(1)}, u32[]{:S(2)}) copy-start(bf16[2,400,128]{2,1,0:T(8,128)(2,1)S(1)} %collective-permute-done.16.refs_3_) | copy-start | bytes 614404
  107.1 1.1 copy-start.5
  108.2 6.2 %collective-permute-start.19 = (bf16[400,128]{1,0:T(8,128)(2,1)S(1)}, bf16[400,128]{1,0:T(8,128)(2,1)}, u32[]{:S(2)}, u32[]{:S(2)}) collective-permute-start(bf16[400,128]{1,0:T(8,128)(2,1)S(1)} %fusion.1), channel_id=1, source_target_pairs={{0,8},{8,0},{1,9},{9,1},{2,10},{10,2},{3,11},{11,3},{4,12},{12,4},... | collective-permute-start | bytes 307208 | tf_op jit(solution)/shard_map/ppermute | solution.py:33
  130.1 4.9 %collective-permute-start.20 = (bf16[2,128,128]{2,1,0:T(8,128)(2,1)}, bf16[2,128,128]{2,1,0:T(8,128)(2,1)S(1)}, u32[]{:S(2)}, u32[]{:S(2)}) collective-permute-start(bf16[2,128,128]{2,1,0:T(8,128)(2,1)} %get-tuple-element.103), channel_id=1, source_target_pairs={{0,2},{2,4},{4,6},{6,0},{1,3},{3,5},{5,7},{7,1},{8,10},{10,12},{12... | collective-permute-start | bytes 196616 | tf_op jit(solution)/shard_map/ppermute | solution.py:613
  130.2 5.8 %collective-permute-start.21 = (bf16[2,128,128]{2,1,0:T(8,128)(2,1)}, bf16[2,128,128]{2,1,0:T(8,128)(2,1)S(1)}, u32[]{:S(2)}, u32[]{:S(2)}) collective-permute-start(bf16[2,128,128]{2,1,0:T(8,128)(2,1)} %get-tuple-element.104), channel_id=1, source_target_pairs={{0,4},{2,6},{4,0},{6,2},{1,5},{3,7},{5,1},{7,3},{8,12},{10,14},{12... | collective-permute-start | bytes 196616 | tf_op jit(solution)/shard_map/ppermute | solution.py:613
  133.1 3.5 %collective-permute-start.22 = (bf16[2,128,128]{2,1,0:T(8,128)(2,1)}, bf16[2,128,128]{2,1,0:T(8,128)(2,1)S(1)}, u32[]{:S(2)}, u32[]{:S(2)}) collective-permute-start(bf16[2,128,128]{2,1,0:T(8,128)(2,1)} %get-tuple-element.105), channel_id=1, source_target_pairs={{0,6},{2,0},{4,2},{6,4},{1,7},{3,1},{5,3},{7,5},{8,14},{10,8},{12,... | collective-permute-start | bytes 196616 | tf_op jit(solution)/shard_map/ppermute | solution.py:613
  133.3 5.5 %collective-permute-start.23 = (bf16[16,16,512]{2,1,0:T(8,128)(2,1)}, bf16[16,16,512]{2,1,0:T(8,128)(2,1)}, u32[]{:S(2)}, u32[]{:S(2)}) collective-permute-start(bf16[16,16,512]{2,1,0:T(8,128)(2,1)} %get-tuple-element.106), channel_id=1, source_target_pairs={{0,16},{16,0},{1,17},{17,1},{2,18},{18,2},{3,19},{19,3},{4,20},{20... | collective-permute-start | bytes 786440 | tf_op jit(solution)/shard_map/ppermute | solution.py:33
  135.0 1.6 copy-start.6
  136.1 1.3 copy-start.7
  136.6 2.2 %copy-start.8 = (bf16[2,128,128]{2,1,0:T(8,128)(2,1)}, bf16[2,128,128]{2,1,0:T(8,128)(2,1)S(1)}, u32[]{:S(2)}) copy-start(bf16[2,128,128]{2,1,0:T(8,128)(2,1)S(1)} %collective-permute-done.22.refs_3_) | copy-start | bytes 196612
  138.8 4.4 %collective-permute-start.24 = (bf16[128,128]{1,0:T(8,128)(2,1)S(1)}, bf16[128,128]{1,0:T(8,128)(2,1)}, u32[]{:S(2)}, u32[]{:S(2)}) collective-permute-start(bf16[128,128]{1,0:T(8,128)(2,1)S(1)} %fusion.3), channel_id=1, source_target_pairs={{0,8},{8,0},{1,9},{9,1},{2,10},{10,2},{3,11},{11,3},{4,12},{12,4},... | collective-permute-start | bytes 98312 | tf_op jit(solution)/shard_map/ppermute | solution.py:33
  144.9 15.7 %collective-permute-start.25 = (bf16[2,128,128]{2,1,0:T(8,128)(2,1)}, bf16[2,128,128]{2,1,0:T(8,128)(2,1)}, u32[]{:S(2)}, u32[]{:S(2)}) collective-permute-start(bf16[2,128,128]{2,1,0:T(8,128)(2,1)} %get-tuple-element.111), channel_id=1, source_target_pairs={{0,1},{1,0},{2,3},{3,2},{4,5},{5,4},{6,7},{7,6},{8,9},{9,8},{10,11... | collective-permute-start | bytes 196616 | tf_op jit(solution)/shard_map/ppermute | solution.py:33
  162.2 9.6 %all-to-all-start.4 = ((bf16[8,64,128]{2,1,0:T(8,128)(2,1)}), bf16[8,64,128]{2,1,0:T(8,128)(2,1)}, u32[]{:S(2)}, u32[]{:S(2)}) async-start(bf16[8,64,128]{2,1,0:T(8,128)(2,1)} %arrange.1), calls=%async_computation.4 | async-start | bytes 262144 | tf_op jit(solution)/shard_map/all_to_all | solution.py:37

commit v3 on v2

--- a/solution.py
+++ b/solution.py
@@ -16,13 +16,14 @@
 XZ = ("xh", "z")
 SMEM = pl.BlockSpec(memory_space=pltpu.SMEM)
 HBM = pl.BlockSpec(memory_space=pltpu.HBM)
-LARGE = 64 * 1024 * 1024
+LARGE = 62 * 1024 * 1024 + 512 * 1024
+SMALL = 8 * 1024 * 1024
 CHUNKS = (48, 29, 48)
 EXTRA = 16
 
 
-def params():
-    return pltpu.CompilerParams(vmem_limit_bytes=LARGE)
+def params(limit=LARGE):
+    return pltpu.CompilerParams(vmem_limit_bytes=limit)
 
 
 def whole(*shape):
@@ -360,7 +361,7 @@
             jax.ShapeDtypeStruct((8, 128, 128), BF),
             jax.ShapeDtypeStruct((128, 128), BF),
         ],
-        compiler_params=params(),
+        compiler_params=params(SMALL),
         name="mix",
     )(where, *received, t_own, t_oth, idx)
 
@@ -411,7 +412,7 @@
         in_specs=[SMEM, *terms_specs(128), whole(2, 512, 128)],
         out_specs=whole(8, 128, 128),
         out_shape=jax.ShapeDtypeStruct((8, 128, 128), BF),
-        compiler_params=params(),
+        compiler_params=params(SMALL),
         name="residual",
     )(where, *received, embedded)
 
@@ -443,7 +444,7 @@
         ],
         out_specs=[whole(2, 128, 128)] * 2,
         out_shape=[jax.ShapeDtypeStruct((2, 128, 128), BF)] * 2,
-        compiler_params=params(),
+        compiler_params=params(SMALL),
         name="last",
     )(where, *received, hidden, kv0, kv1)
 
@@ -465,7 +466,7 @@
         in_specs=[SMEM, whole(2, 128, 128), whole(2, 128, 128)],
         out_specs=whole(8, 64, 128),
         out_shape=jax.ShapeDtypeStruct((8, 64, 128), BF),
-        compiler_params=params(),
+        compiler_params=params(SMALL),
         name="arrange",
     )(where, keep, got)
 
@@ -595,7 +596,9 @@
     sums, *pieces = make_sums(
         where, tokens, fir_filters, mode_poles, residues, modal_state, cache
     )
-    w_in, w_out, e_oth, sums = lax.optimization_barrier((w_in, w_out, e_oth, sums))
+    w_in, w_out, e_oth, g_oth, sums = lax.optimization_barrier(
+        (w_in, w_out, e_oth, g_oth, sums)
+    )
     w_in_oth = swap(w_in, "c")
     w_out_oth = swap(w_out, "c")
     moved = []

time: 176 us -> 169 us (0.960)
  waiting for transfers between devices: 39.1 us -> 31.1 us
  local copies, waits for them, and re-layouts: 0.04 us -> 5.45 us
  Pallas kernels: 43.5 us -> 38.2 us
  starting transfers between devices: 56.4 us -> 60.3 us
  blocking collectives: 30.5 us -> 28 us
    ppermute x12, waiting for transfers between devices: 20.3 us -> 14.8 us  [scatter(): terms[s] = lax.ppermute(terms[s], 'z', [(z, (z + s) % 4) for z in range(4)])]
    unnamed x24 -> x40, local copies, waits for them, and re-layouts: 0.04 us -> 5.45 us
    pallas_call x2, Pallas kernels: 5.09 us -> 2.31 us  [mix(): pl.pallas_call(lambda *refs: mix_kernel(block, *refs), grid=(1,), in_spec...]
    ppermute x14, starting transfers between devices: 30.9 us -> 33.6 us  [swap(): return lax.ppermute(value, axis, [(0, 1), (1, 0)])]
    all_to_all x3, blocking collectives: 30.5 us -> 28 us  [exchange(): return lax.all_to_all(value, axes, 0, 0, tiled=True)]
    ppermute x14, waiting for transfers between devices: 14.5 us -> 12.6 us  [swap(): return lax.ppermute(value, axis, [(0, 1), (1, 0)])]
  transfers between devices with their start and end apart: 28 -> 28, of which waited for: 19 -> 18; matrix products, arithmetic and copies ran while one was open for 2% -> 2% of each run, Pallas kernels for 17% -> 17%
where the time goes in v3:
time: 169 us; the launch traced here: 168 us
  starting transfers between devices  60.3 us (36%)
  Pallas kernels  38.2 us (23%)
  waiting for transfers between devices  31.1 us (18%)
  blocking collectives  28 us (17%)
  local copies, waits for them, and re-layouts  5.45 us (3%)
  other arithmetic  4.13 us (2%)
    ppermute x14, starting transfers between devices, swap(): return lax.ppermute(value, axis, [(0, 1), (1, 0)])  33.6 us
    all_to_all x3, blocking collectives, exchange(): return lax.all_to_all(value, axes, 0, 0, tiled=True)  28 us
    ppermute x12, starting transfers between devices, scatter(): terms[s] = lax.ppermute(terms[s], 'z', [(z, (z + s) % 4) for z in range(4)])  18.1 us
    ppermute x12, waiting for transfers between devices, scatter(): terms[s] = lax.ppermute(terms[s], 'z', [(z, (z + s) % 4) for z in range(4)])  14.8 us
    ppermute x14, waiting for transfers between devices, swap(): return lax.ppermute(value, axis, [(0, 1), (1, 0)])  12.6 us
    all_to_all x2, starting transfers between devices, exchange(): return lax.all_to_all(value, axes, 0, 0, tiled=True)  8.57 us
    pallas_call x2, Pallas kernels, project_out(): pl.pallas_call(out_kernel, grid=(2,), in_specs=[SMEM, whole(8, 128, 128),...  6 us
    pallas_call x1, Pallas kernels, project_embed(): pl.pallas_call(embed_kernel, grid=(2,), in_specs=[SMEM, whole(8, 72, 128)...  5.98 us
  transfers between devices with their start and end apart: 28, of which 18 were waited for; matrix products, arithmetic and copies ran while one was open for 2% of the time, Pallas kernels for 17%

profile of v3, /device:TPU:1, one launch (start us, length us, event | category | flops | bytes accessed | tf_op | source)
XLA Modules:
  0.0 168.1 jit_solution(11981106466538720173)
XLA Ops:
  0.6 1.5 collective-permute-start
  2.9 4.5 %state_sums.1 = (f32[8,72,128]{2,1,0:T(8,128)}, bf16[48,16,512]{2,1,0:T(8,128)(2,1)}, bf16[29,16,512]{2,1,0:T(8,128)(2,1)}, bf16[48,16,512]{2,1,0:T(8,128)(2,1)}, bf16[16,16,512]{2,1,0:T(8,128)(2,1)}) custom-call(s32[4]{0:T(128)} %pad_add_fusion.c_ref.refs_0_.where_ref, s32[2,16]{1,0:T(2,128)} %tok_ref.1, f32[32,128]{1,0:T(8,128)} %filt_ref.1, ...), custom_call_target="tpu_custom_call" | custom-call | tf_op jit(solution)/shard_map/state_sums/pallas_call | solution.py:109
  8.0 5.2 %all-to-all-start = ((f32[8,72,128]{2,1,0:T(8,128)}), f32[8,72,128]{2,1,0:T(8,128)S(1)}, u32[]{:S(2)}, u32[]{:S(2)}) async-start(f32[8,72,128]{2,1,0:T(8,128)} %get-tuple-element.67), calls=%async_computation | async-start | bytes 589824 | tf_op jit(solution)/shard_map/all_to_all | solution.py:38
  13.2 1.8 %indices.1.refs_8_ = s32[8,128]{1,0:T(8,128)} custom-call(s32[4]{0:T(128)} %pad_add_fusion.c_ref.refs_0_.where_ref, s32[2,128]{1,0:T(2,128)} %par_ref.5), custom_call_target="tpu_custom_call" | custom-call | tf_op jit(solution)/shard_map/indices/pallas_call | solution.py:153
  15.0 2.5 %turn.1.tables = bf16[2,512,512]{2,1,0:T(8,128)(2,1)} custom-call(bf16[512,512]{1,0:T(8,128)(2,1)} %own_ref.2, bf16[512,512]{1,0:T(8,128)(2,1)} %copy-done.15), custom_call_target="tpu_custom_call" | custom-call | tf_op jit(solution)/shard_map/turn/pallas_call | solution.py:170
  17.5 2.7 %all-to-all-done.got_ref.refs_6_ = f32[8,72,128]{2,1,0:T(8,128)S(1)} async-done(((f32[8,72,128]{2,1,0:T(8,128)}), f32[8,72,128]{2,1,0:T(8,128)S(1)}, u32[]{:S(2)}, u32[]{:S(2)}) %all-to-all-start) | async-done | bytes 294944 | tf_op jit(solution)/shard_map/all_to_all | solution.py:38
  20.9 6.0 %embed_project.1 = (bf16[2,400,128]{2,1,0:T(8,128)(2,1)}, bf16[2,400,128]{2,1,0:T(8,128)(2,1)}, bf16[2,400,128]{2,1,0:T(8,128)(2,1)}, bf16[2,400,128]{2,1,0:T(8,...) custom-call(s32[4]{0:T(128)} %pad_add_fusion.c_ref.refs_0_.where_ref, f32[8,72,128]{2,1,0:T(8,128)} %copy-done, ...), custom_call_target="tpu_custom_call" | custom-call | flops 805306368 | bytes 7340032 | tf_op jit(solution)/shard_map/embed_project/pallas_call | solution.py:250
  26.9 1.7 %collective-permute-start.3 = (bf16[2,400,128]{2,1,0:T(8,128)(2,1)}, bf16[2,400,128]{2,1,0:T(8,128)(2,1)S(1)}, u32[]{:S(2)}, u32[]{:S(2)}) collective-permute-start(bf16[2,400,128]{2,1,0:T(8,128)(2,1)} %get-tuple-element.75), channel_id=1, source_target_pairs={{0,2},{2,4},{4,6},{6,0},{1,3},{3,5},{5,7},{7,1},{8,10},{10,12},{12... | collective-permute-start | bytes 614408 | tf_op jit(solution)/shard_map/ppermute | solution.py:616
  28.6 3.3 %collective-permute-start.4 = (bf16[2,400,128]{2,1,0:T(8,128)(2,1)}, bf16[2,400,128]{2,1,0:T(8,128)(2,1)S(1)}, u32[]{:S(2)}, u32[]{:S(2)}) collective-permute-start(bf16[2,400,128]{2,1,0:T(8,128)(2,1)} %get-tuple-element.76), channel_id=1, source_target_pairs={{0,4},{2,6},{4,0},{6,2},{1,5},{3,7},{5,1},{7,3},{8,12},{10,14},{12... | collective-permute-start | bytes 614408 | tf_op jit(solution)/shard_map/ppermute | solution.py:616
  32.7 1.9 %collective-permute-done.3.refs_2_ = bf16[2,400,128]{2,1,0:T(8,128)(2,1)S(1)} collective-permute-done((bf16[2,400,128]{2,1,0:T(8,128)(2,1)}, bf16[2,400,128]{2,1,0:T(8,128)(2,1)S(1)}, u32[]{:S(2)}, u32[]{:S(2)}) %collective-permute-start.3) | collective-permute-done | bytes 204832 | tf_op jit(solution)/shard_map/ppermute | solution.py:616
  34.6 3.5 %collective-permute-start.8 = (f32[4,64,128]{2,1,0:T(8,128)}, f32[4,64,128]{2,1,0:T(8,128)S(1)}, u32[]{:S(2)}, u32[]{:S(2)}) collective-permute-start(f32[4,64,128]{2,1,0:T(8,128)} %get-tuple-element.80), channel_id=1, source_target_pairs={{0,1},{1,0},{2,3},{3,2},{4,5},{5,4},{6,7},{7,6},{8,9},{9,8},{10,11... | collective-permute-start | bytes 393224 | tf_op jit(solution)/shard_map/ppermute | solution.py:34
  38.1 1.4 collective-permute-done.4.refs_3_
  39.6 1.0 fusion
  40.6 2.6 %collective-permute-start.7 = (bf16[400,128]{1,0:T(8,128)(2,1)S(1)}, bf16[400,128]{1,0:T(8,128)(2,1)S(1)}, u32[]{:S(2)}, u32[]{:S(2)}) collective-permute-start(bf16[400,128]{1,0:T(8,128)(2,1)S(1)} %fusion), channel_id=1, source_target_pairs={{0,8},{8,0},{1,9},{9,1},{2,10},{10,2},{3,11},{11,3},{4,12},{12,4},... | collective-permute-start | bytes 307208 | tf_op jit(solution)/shard_map/ppermute | solution.py:34
  43.1 2.5 %collective-permute-done.7.refs_5_ = bf16[400,128]{1,0:T(8,128)(2,1)S(1)} collective-permute-done((bf16[400,128]{1,0:T(8,128)(2,1)S(1)}, bf16[400,128]{1,0:T(8,128)(2,1)S(1)}, u32[]{:S(2)}, u32[]{:S(2)}) %collective-permute-start.7) | collective-permute-done | bytes 102432 | tf_op jit(solution)/shard_map/ppermute | solution.py:34
  45.7 1.0 copy-done.1
  47.5 1.2 mix.2
  48.7 9.5 %all_to_all.25.a_ref = bf16[8,128,128]{2,1,0:T(8,128)(2,1)} all-to-all(bf16[8,128,128]{2,1,0:T(8,128)(2,1)S(1)} %get-tuple-element.82), channel_id=1, replica_groups=mesh['y'=4,'xl'=2,'xh'=2,'z'=4,'c'=2] {'y','xl'}, dimensions={0} | all-to-all | bytes 524288 | tf_op jit(solution)/shard_map/all_to_all | solution.py:38
  58.8 3.0 %project_out.2 = (bf16[2,128,128]{2,1,0:T(8,128)(2,1)}, bf16[2,128,128]{2,1,0:T(8,128)(2,1)}, bf16[2,128,128]{2,1,0:T(8,128)(2,1)}, bf16[2,128,128]{2,1,0:T(8,128)(2,1)}) custom-call(s32[4]{0:T(128)} %pad_add_fusion.c_ref.refs_0_.where_ref, bf16[8,128,128]{2,1,0:T(8,128)(2,1)} %all_to_all.25.a_ref, bf16[2,1024,512]{2,1,0:T(8,128)(2,1)} %bitcast.20, ...), custom_call_target="tpu_custom_call" | custom-call | flops 268435456 | bytes 2621440 | tf_op jit(solution)/shard_map/project_out/pallas_call | solution.py:383
  61.8 2.8 %collective-permute-start.10 = (bf16[2,128,128]{2,1,0:T(8,128)(2,1)}, bf16[2,128,128]{2,1,0:T(8,128)(2,1)S(1)}, u32[]{:S(2)}, u32[]{:S(2)}) collective-permute-start(bf16[2,128,128]{2,1,0:T(8,128)(2,1)} %get-tuple-element.87), channel_id=1, source_target_pairs={{0,2},{2,4},{4,6},{6,0},{1,3},{3,5},{5,7},{7,1},{8,10},{10,12},{12... | collective-permute-start | bytes 196616 | tf_op jit(solution)/shard_map/ppermute | solution.py:616
  64.5 1.5 collective-permute-start.11
  66.0 1.0 collective-permute-start.12
  67.0 2.4 %collective-permute-done.11.refs_2_ = bf16[2,128,128]{2,1,0:T(8,128)(2,1)S(1)} collective-permute-done((bf16[2,128,128]{2,1,0:T(8,128)(2,1)}, bf16[2,128,128]{2,1,0:T(8,128)(2,1)S(1)}, u32[]{:S(2)}, u32[]{:S(2)}) %collective-permute-start.11) | collective-permute-done | bytes 65568 | tf_op jit(solution)/shard_map/ppermute | solution.py:616
  70.4 2.6 %collective-permute-start.14 = (bf16[128,128]{1,0:T(8,128)(2,1)S(1)}, bf16[128,128]{1,0:T(8,128)(2,1)S(1)}, u32[]{:S(2)}, u32[]{:S(2)}) collective-permute-start(bf16[128,128]{1,0:T(8,128)(2,1)S(1)} %fusion.2), channel_id=1, source_target_pairs={{0,8},{8,0},{1,9},{9,1},{2,10},{10,2},{3,11},{11,3},{4,12},{12,4},... | collective-permute-start | bytes 98312 | tf_op jit(solution)/shard_map/ppermute | solution.py:34
  73.0 1.8 %collective-permute-done.14.refs_4_ = bf16[128,128]{1,0:T(8,128)(2,1)S(1)} collective-permute-done((bf16[128,128]{1,0:T(8,128)(2,1)S(1)}, bf16[128,128]{1,0:T(8,128)(2,1)S(1)}, u32[]{:S(2)}, u32[]{:S(2)}) %collective-permute-start.14) | collective-permute-done | bytes 32800 | tf_op jit(solution)/shard_map/ppermute | solution.py:34
  76.2 9.2 %all_to_all.26.a_ref = bf16[8,128,128]{2,1,0:T(8,128)(2,1)} all-to-all(bf16[8,128,128]{2,1,0:T(8,128)(2,1)S(1)} %residual.1.refs_5_), channel_id=1, replica_groups=mesh['y'=4,'xl'=2,'xh'=2,'z'=4,'c'=2] {'y','xl'}, dimensions={0} | all-to-all | bytes 524288 | tf_op jit(solution)/shard_map/all_to_all | solution.py:38
  86.0 5.3 %norm_project.1 = (bf16[2,400,128]{2,1,0:T(8,128)(2,1)}, bf16[2,400,128]{2,1,0:T(8,128)(2,1)}, bf16[2,400,128]{2,1,0:T(8,128)(2,1)}, bf16[2,400,128]{2,1,0:T(8,128)(2,1)}) custom-call(s32[4]{0:T(128)} %pad_add_fusion.c_ref.refs_0_.where_ref, bf16[8,128,128]{2,1,0:T(8,128)(2,1)} %all_to_all.26.a_ref, f32[2,512]{1,0:T(2,128)} %g_own.3, f32[2,512]{1,0:T(2,128)} %copy-done.18, ...), custom_call_target="tpu_custom_call" | custom-call | flops 805306368 | bytes 7340032 | tf_op jit(solution)/shard_map/norm_project/pallas_call | solution.py:291
  92.2 2.3 %collective-permute-start.16 = (bf16[2,400,128]{2,1,0:T(8,128)(2,1)}, bf16[2,400,128]{2,1,0:T(8,128)(2,1)S(1)}, u32[]{:S(2)}, u32[]{:S(2)}) collective-permute-start(bf16[2,400,128]{2,1,0:T(8,128)(2,1)} %get-tuple-element.97), channel_id=1, source_target_pairs={{0,4},{2,6},{4,0},{6,2},{1,5},{3,7},{5,1},{7,3},{8,12},{10,14},{12... | collective-permute-start | bytes 614408 | tf_op jit(solution)/shard_map/ppermute | solution.py:616
  95.0 2.4 %collective-permute-done.15.refs_2_ = bf16[2,400,128]{2,1,0:T(8,128)(2,1)S(1)} collective-permute-done((bf16[2,400,128]{2,1,0:T(8,128)(2,1)}, bf16[2,400,128]{2,1,0:T(8,128)(2,1)S(1)}, u32[]{:S(2)}, u32[]{:S(2)}) %collective-permute-start.15) | collective-permute-done | bytes 204832 | tf_op jit(solution)/shard_map/ppermute | solution.py:616
  97.4 2.7 %collective-permute-done.16.refs_3_ = bf16[2,400,128]{2,1,0:T(8,128)(2,1)S(1)} collective-permute-done((bf16[2,400,128]{2,1,0:T(8,128)(2,1)}, bf16[2,400,128]{2,1,0:T(8,128)(2,1)S(1)}, u32[]{:S(2)}, u32[]{:S(2)}) %collective-permute-start.16) | collective-permute-done | bytes 204832 | tf_op jit(solution)/shard_map/ppermute | solution.py:616
  100.6 1.0 fusion.1
  101.5 2.7 %collective-permute-start.19 = (bf16[400,128]{1,0:T(8,128)(2,1)S(1)}, bf16[400,128]{1,0:T(8,128)(2,1)S(1)}, u32[]{:S(2)}, u32[]{:S(2)}) collective-permute-start(bf16[400,128]{1,0:T(8,128)(2,1)S(1)} %fusion.1), channel_id=1, source_target_pairs={{0,8},{8,0},{1,9},{9,1},{2,10},{10,2},{3,11},{11,3},{4,12},{12,4},... | collective-permute-start | bytes 307208 | tf_op jit(solution)/shard_map/ppermute | solution.py:34
  104.3 4.0 %collective-permute-done.19.refs_5_ = bf16[400,128]{1,0:T(8,128)(2,1)S(1)} collective-permute-done((bf16[400,128]{1,0:T(8,128)(2,1)S(1)}, bf16[400,128]{1,0:T(8,128)(2,1)S(1)}, u32[]{:S(2)}, u32[]{:S(2)}) %collective-permute-start.19) | collective-permute-done | bytes 102432 | tf_op jit(solution)/shard_map/ppermute | solution.py:34
  109.2 1.2 mix.3
  110.4 9.3 %all_to_all.27.a_ref = bf16[8,128,128]{2,1,0:T(8,128)(2,1)} all-to-all(bf16[8,128,128]{2,1,0:T(8,128)(2,1)S(1)} %get-tuple-element.101), channel_id=1, replica_groups=mesh['y'=4,'xl'=2,'xh'=2,'z'=4,'c'=2] {'y','xl'}, dimensions={0} | all-to-all | bytes 524288 | tf_op jit(solution)/shard_map/all_to_all | solution.py:38
  119.7 3.0 %project_out.3 = (bf16[2,128,128]{2,1,0:T(8,128)(2,1)}, bf16[2,128,128]{2,1,0:T(8,128)(2,1)}, bf16[2,128,128]{2,1,0:T(8,128)(2,1)}, bf16[2,128,128]{2,1,0:T(8,128)(2,1)}) custom-call(s32[4]{0:T(128)} %pad_add_fusion.c_ref.refs_0_.where_ref, bf16[8,128,128]{2,1,0:T(8,128)(2,1)} %all_to_all.27.a_ref, bf16[2,1024,512]{2,1,0:T(8,128)(2,1)} %bitcast.21, ...), custom_call_target="tpu_custom_call" | custom-call | flops 268435456 | bytes 2621440 | tf_op jit(solution)/shard_map/project_out/pallas_call | solution.py:383
  123.2 2.9 %collective-permute-start.21 = (bf16[2,128,128]{2,1,0:T(8,128)(2,1)}, bf16[2,128,128]{2,1,0:T(8,128)(2,1)S(1)}, u32[]{:S(2)}, u32[]{:S(2)}) collective-permute-start(bf16[2,128,128]{2,1,0:T(8,128)(2,1)} %get-tuple-element.106), channel_id=1, source_target_pairs={{0,4},{2,6},{4,0},{6,2},{1,5},{3,7},{5,1},{7,3},{8,12},{10,14},{12... | collective-permute-start | bytes 196616 | tf_op jit(solution)/shard_map/ppermute | solution.py:616
  127.2 1.5 collective-permute-done.21.refs_2_
  128.7 1.2 collective-permute-done.22.refs_3_
  130.7 1.1 collective-permute-done.23.oth_ref
  131.8 2.1 %collective-permute-start.24 = (bf16[128,128]{1,0:T(8,128)(2,1)S(1)}, bf16[128,128]{1,0:T(8,128)(2,1)S(1)}, u32[]{:S(2)}, u32[]{:S(2)}) collective-permute-start(bf16[128,128]{1,0:T(8,128)(2,1)S(1)} %fusion.3), channel_id=1, source_target_pairs={{0,8},{8,0},{1,9},{9,1},{2,10},{10,2},{3,11},{11,3},{4,12},{12,4},... | collective-permute-start | bytes 98312 | tf_op jit(solution)/shard_map/ppermute | solution.py:34
  133.8 2.2 %collective-permute-done.24.refs_4_ = bf16[128,128]{1,0:T(8,128)(2,1)S(1)} collective-permute-done((bf16[128,128]{1,0:T(8,128)(2,1)S(1)}, bf16[128,128]{1,0:T(8,128)(2,1)S(1)}, u32[]{:S(2)}, u32[]{:S(2)}) %collective-permute-start.24) | collective-permute-done | bytes 32800 | tf_op jit(solution)/shard_map/ppermute | solution.py:34
  137.6 15.8 %collective-permute-start.25 = (bf16[2,128,128]{2,1,0:T(8,128)(2,1)S(1)}, bf16[2,128,128]{2,1,0:T(8,128)(2,1)S(1)}, u32[]{:S(2)}, u32[]{:S(2)}) collective-permute-start(bf16[2,128,128]{2,1,0:T(8,128)(2,1)S(1)} %get-tuple-element.113), channel_id=1, source_target_pairs={{0,1},{1,0},{2,3},{3,2},{4,5},{5,4},{6,7},{7,6},{8,9},{9,8},{10,11... | collective-permute-start | bytes 196616 | tf_op jit(solution)/shard_map/ppermute | solution.py:34
  154.4 1.2 arrange.1
  155.6 3.4 %all-to-all-start.4 = ((bf16[8,64,128]{2,1,0:T(8,128)(2,1)}), bf16[8,64,128]{2,1,0:T(8,128)(2,1)S(1)}, u32[]{:S(2)}, u32[]{:S(2)}) async-start(bf16[8,64,128]{2,1,0:T(8,128)(2,1)} %arrange.1), calls=%async_computation.4 | async-start | bytes 262144 | tf_op jit(solution)/shard_map/all_to_all | solution.py:38
  159.0 4.5 %reorder.1.fir_ref = bf16[127,16,512]{2,1,0:T(8,128)(2,1)} custom-call(s32[4]{0:T(128)} %pad_add_fusion.c_ref.refs_0_.where_ref, s32[2,128]{1,0:T(2,128)} %par_ref.5, bf16[127,16,512]{2,1,0:T(8,128)(2,1)} %bitcast.23, bf16[48,16,512]{2,1,0:T(8,128)(2,1)} %copy-done.13, bf16[29,16,512]{2,1,0:T(8,128)(2,1)} %copy-done.16, ...), custom_call_target="tpu_custom_call" | custom-call | flops 536870912 | bytes 6291456 | tf_op jit(solution)/shard_map/reorder/pallas_call | solution.py:524
  163.5 1.1 all-to-all-done.4.r_ref
  165.2 2.8 %final.1 = (bf16[2,16,512]{2,1,0:T(8,128)(2,1)}, bf16[127,16,512]{2,1,0:T(8,128)(2,1)}, f32[16,16,512]{2,1,0:T(8,128)}) custom-call(s32[4]{0:T(128)} %pad_add_fusion.c_ref.refs_0_.where_ref, s32[2,128]{1,0:T(2,128)} %par_ref.5, bf16[8,64,128]{2,1,0:T(8,128)(2,1)} %copy-done.14, f32[16,512]{1,0:T(8,128)} %poles_ref.3, ...), custom_call_target="tpu_custom_call", output_to_operand_aliasing={{1}: (6, {})} | custom-call | tf_op jit(solution)/shard_map/final/pallas_call | solution.py:564
  (70 shorter events, 15.7 us)
Async XLA Ops:
  0.6 6.8 %collective-permute-start = (bf16[512,512]{1,0:T(8,128)(2,1)}, bf16[512,512]{1,0:T(8,128)(2,1)S(1)}, u32[]{:S(2)}, u32[]{:S(2)}) collective-permute-start(bf16[512,512]{1,0:T(8,128)(2,1)} %own_ref.2), channel_id=1, source_target_pairs={{0,1},{1,0},{2,3},{3,2},{4,5},{5,4},{6,7},{7,6},{8,9},{9,8},{10,11... | collective-permute-start | bytes 1572872 | tf_op jit(solution)/shard_map/ppermute | solution.py:34
  2.1 5.2 %collective-permute-start.1 = (f32[2,512]{1,0:T(2,128)}, f32[2,512]{1,0:T(2,128)S(1)}, u32[]{:S(2)}, u32[]{:S(2)}) collective-permute-start(f32[2,512]{1,0:T(2,128)} %g_own.3), channel_id=1, source_target_pairs={{0,1},{1,0},{2,3},{3,2},{4,5},{5,4},{6,7},{7,6},{8,9},{9,8},{10,11... | collective-permute-start | bytes 12296 | tf_op jit(solution)/shard_map/ppermute | solution.py:34
  7.4 13.3 %copy-start.18 = (f32[2,512]{1,0:T(2,128)}, f32[2,512]{1,0:T(2,128)S(1)}, u32[]{:S(2)}) copy-start(f32[2,512]{1,0:T(2,128)S(1)} %collective-permute-done.1.g_oth) | copy-start | bytes 12292
  7.4 7.6 %copy-start.15 = (bf16[512,512]{1,0:T(8,128)(2,1)}, bf16[512,512]{1,0:T(8,128)(2,1)S(1)}, u32[]{:S(2)}) copy-start(bf16[512,512]{1,0:T(8,128)(2,1)S(1)} %collective-permute-done.oth_ref) | copy-start | bytes 1572868
  7.4 13.3 %collective-permute-start.2 = (bf16[2,3072,512]{2,1,0:T(8,128)(2,1)}, bf16[2,3072,512]{2,1,0:T(8,128)(2,1)}, u32[]{:S(2)}, u32[]{:S(2)}) collective-permute-start(bf16[2,3072,512]{2,1,0:T(8,128)(2,1)} %bitcast.16), channel_id=1, source_target_pairs={{0,1},{1,0},{2,3},{3,2},{4,5},{5,4},{6,7},{7,6},{8,9},{9,8},{10,11... | collective-permute-start | bytes 18874376 | tf_op jit(solution)/shard_map/ppermute | solution.py:34
  7.9 50.9 %collective-permute-start.9 = (bf16[2,1024,512]{2,1,0:T(8,128)(2,1)}, bf16[2,1024,512]{2,1,0:T(8,128)(2,1)}, u32[]{:S(2)}, u32[]{:S(2)}) collective-permute-start(bf16[2,1024,512]{2,1,0:T(8,128)(2,1)} %bitcast.19), channel_id=1, source_target_pairs={{0,1},{1,0},{2,3},{3,2},{4,5},{5,4},{6,7},{7,6},{8,9},{9,8},{10,11... | collective-permute-start | bytes 6291464 | tf_op jit(solution)/shard_map/ppermute | solution.py:34
  8.0 12.2 %all-to-all-start = ((f32[8,72,128]{2,1,0:T(8,128)}), f32[8,72,128]{2,1,0:T(8,128)S(1)}, u32[]{:S(2)}, u32[]{:S(2)}) async-start(f32[8,72,128]{2,1,0:T(8,128)} %get-tuple-element.67), calls=%async_computation | async-start | bytes 589824 | tf_op jit(solution)/shard_map/all_to_all | solution.py:38
  20.2 0.7 copy-start
  20.2 25.4 %copy-start.8 = (s32[4]{0:T(128)S(1)}, s32[4]{0:T(128)}, u32[]{:S(2)}) copy-start(s32[4]{0:T(128)} %pad_add_fusion.c_ref.refs_0_.where_ref) | copy-start | bytes 52
  20.2 25.4 %copy-start.12 = (s32[8,128]{1,0:T(8,128)S(1)}, s32[8,128]{1,0:T(8,128)}, u32[]{:S(2)}) copy-start(s32[8,128]{1,0:T(8,128)} %indices.1.refs_8_) | copy-start | bytes 12292
  20.2 20.3 %collective-permute-start.6 = (bf16[48,16,512]{2,1,0:T(8,128)(2,1)}, bf16[48,16,512]{2,1,0:T(8,128)(2,1)S(1)}, u32[]{:S(2)}, u32[]{:S(2)}) collective-permute-start(bf16[48,16,512]{2,1,0:T(8,128)(2,1)} %get-tuple-element.78), channel_id=1, source_target_pairs={{0,16},{16,0},{1,17},{17,1},{2,18},{18,2},{3,19},{19,3},{4,20},{20... | collective-permute-start | bytes 2359304 | tf_op jit(solution)/shard_map/ppermute | solution.py:34
  26.9 7.7 %collective-permute-start.3 = (bf16[2,400,128]{2,1,0:T(8,128)(2,1)}, bf16[2,400,128]{2,1,0:T(8,128)(2,1)S(1)}, u32[]{:S(2)}, u32[]{:S(2)}) collective-permute-start(bf16[2,400,128]{2,1,0:T(8,128)(2,1)} %get-tuple-element.75), channel_id=1, source_target_pairs={{0,2},{2,4},{4,6},{6,0},{1,3},{3,5},{5,7},{7,1},{8,10},{10,12},{12... | collective-permute-start | bytes 614408 | tf_op jit(solution)/shard_map/ppermute | solution.py:616
  28.6 11.0 %collective-permute-start.4 = (bf16[2,400,128]{2,1,0:T(8,128)(2,1)}, bf16[2,400,128]{2,1,0:T(8,128)(2,1)S(1)}, u32[]{:S(2)}, u32[]{:S(2)}) collective-permute-start(bf16[2,400,128]{2,1,0:T(8,128)(2,1)} %get-tuple-element.76), channel_id=1, source_target_pairs={{0,4},{2,6},{4,0},{6,2},{1,5},{3,7},{5,1},{7,3},{8,12},{10,14},{12... | collective-permute-start | bytes 614408 | tf_op jit(solution)/shard_map/ppermute | solution.py:616
  31.9 7.6 %collective-permute-start.5 = (bf16[2,400,128]{2,1,0:T(8,128)(2,1)}, bf16[2,400,128]{2,1,0:T(8,128)(2,1)S(1)}, u32[]{:S(2)}, u32[]{:S(2)}) collective-permute-start(bf16[2,400,128]{2,1,0:T(8,128)(2,1)} %get-tuple-element.77), channel_id=1, source_target_pairs={{0,6},{2,0},{4,2},{6,4},{1,7},{3,1},{5,3},{7,5},{8,14},{10,8},{12,... | collective-permute-start | bytes 614408 | tf_op jit(solution)/shard_map/ppermute | solution.py:616
  34.6 8.5 %collective-permute-start.8 = (f32[4,64,128]{2,1,0:T(8,128)}, f32[4,64,128]{2,1,0:T(8,128)S(1)}, u32[]{:S(2)}, u32[]{:S(2)}) collective-permute-start(f32[4,64,128]{2,1,0:T(8,128)} %get-tuple-element.80), channel_id=1, source_target_pairs={{0,1},{1,0},{2,3},{3,2},{4,5},{5,4},{6,7},{7,6},{8,9},{9,8},{10,11... | collective-permute-start | bytes 393224 | tf_op jit(solution)/shard_map/ppermute | solution.py:34
  40.5 17.7 %copy-start.13 = (bf16[48,16,512]{2,1,0:T(8,128)(2,1)}, bf16[48,16,512]{2,1,0:T(8,128)(2,1)S(1)}, u32[]{:S(2)}) copy-start(bf16[48,16,512]{2,1,0:T(8,128)(2,1)S(1)} %collective-permute-done.6.refs_0_) | copy-start | bytes 2359300
  40.6 5.1 %collective-permute-start.7 = (bf16[400,128]{1,0:T(8,128)(2,1)S(1)}, bf16[400,128]{1,0:T(8,128)(2,1)S(1)}, u32[]{:S(2)}, u32[]{:S(2)}) collective-permute-start(bf16[400,128]{1,0:T(8,128)(2,1)S(1)} %fusion), channel_id=1, source_target_pairs={{0,8},{8,0},{1,9},{9,1},{2,10},{10,2},{3,11},{11,3},{4,12},{12,4},... | collective-permute-start | bytes 307208 | tf_op jit(solution)/shard_map/ppermute | solution.py:34
  45.7 1.0 copy-start.1
  46.6 0.9 copy-start.3
  58.2 16.6 %copy-start.5 = (bf16[2,512,128]{2,1,0:T(8,128)(2,1)S(1)}, bf16[2,512,128]{2,1,0:T(8,128)(2,1)}, u32[]{:S(2)}) copy-start(bf16[2,512,128]{2,1,0:T(8,128)(2,1)} %get-tuple-element.92.refs_5_) | copy-start | bytes 786436
  58.2 16.6 %copy-start.9 = (s32[4]{0:T(128)S(1)}, s32[4]{0:T(128)}, u32[]{:S(2)}) copy-start(s32[4]{0:T(128)} %pad_add_fusion.c_ref.refs_0_.where_ref) | copy-start | bytes 52
  58.2 12.2 %collective-permute-start.13 = (bf16[29,16,512]{2,1,0:T(8,128)(2,1)}, bf16[29,16,512]{2,1,0:T(8,128)(2,1)S(1)}, u32[]{:S(2)}, u32[]{:S(2)}) collective-permute-start(bf16[29,16,512]{2,1,0:T(8,128)(2,1)} %get-tuple-element.90), channel_id=1, source_target_pairs={{0,16},{16,0},{1,17},{17,1},{2,18},{18,2},{3,19},{19,3},{4,20},{20... | collective-permute-start | bytes 1425416 | tf_op jit(solution)/shard_map/ppermute | solution.py:34
  61.8 5.2 %collective-permute-start.10 = (bf16[2,128,128]{2,1,0:T(8,128)(2,1)}, bf16[2,128,128]{2,1,0:T(8,128)(2,1)S(1)}, u32[]{:S(2)}, u32[]{:S(2)}) collective-permute-start(bf16[2,128,128]{2,1,0:T(8,128)(2,1)} %get-tuple-element.87), channel_id=1, source_target_pairs={{0,2},{2,4},{4,6},{6,0},{1,3},{3,5},{5,7},{7,1},{8,10},{10,12},{12... | collective-permute-start | bytes 196616 | tf_op jit(solution)/shard_map/ppermute | solution.py:616
  64.5 4.8 %collective-permute-start.11 = (bf16[2,128,128]{2,1,0:T(8,128)(2,1)}, bf16[2,128,128]{2,1,0:T(8,128)(2,1)S(1)}, u32[]{:S(2)}, u32[]{:S(2)}) collective-permute-start(bf16[2,128,128]{2,1,0:T(8,128)(2,1)} %get-tuple-element.88), channel_id=1, source_target_pairs={{0,4},{2,6},{4,0},{6,2},{1,5},{3,7},{5,1},{7,3},{8,12},{10,14},{12... | collective-permute-start | bytes 196616 | tf_op jit(solution)/shard_map/ppermute | solution.py:616
  66.0 3.6 %collective-permute-start.12 = (bf16[2,128,128]{2,1,0:T(8,128)(2,1)}, bf16[2,128,128]{2,1,0:T(8,128)(2,1)S(1)}, u32[]{:S(2)}, u32[]{:S(2)}) collective-permute-start(bf16[2,128,128]{2,1,0:T(8,128)(2,1)} %get-tuple-element.89), channel_id=1, source_target_pairs={{0,6},{2,0},{4,2},{6,4},{1,7},{3,1},{5,3},{7,5},{8,14},{10,8},{12,... | collective-permute-start | bytes 196616 | tf_op jit(solution)/shard_map/ppermute | solution.py:616
  70.4 20.9 %copy-start.16 = (bf16[29,16,512]{2,1,0:T(8,128)(2,1)}, bf16[29,16,512]{2,1,0:T(8,128)(2,1)S(1)}, u32[]{:S(2)}) copy-start(bf16[29,16,512]{2,1,0:T(8,128)(2,1)S(1)} %collective-permute-done.13.refs_1_) | copy-start | bytes 1425412
  70.4 4.3 %collective-permute-start.14 = (bf16[128,128]{1,0:T(8,128)(2,1)S(1)}, bf16[128,128]{1,0:T(8,128)(2,1)S(1)}, u32[]{:S(2)}, u32[]{:S(2)}) collective-permute-start(bf16[128,128]{1,0:T(8,128)(2,1)S(1)} %fusion.2), channel_id=1, source_target_pairs={{0,8},{8,0},{1,9},{9,1},{2,10},{10,2},{3,11},{11,3},{4,12},{12,4},... | collective-permute-start | bytes 98312 | tf_op jit(solution)/shard_map/ppermute | solution.py:34
  74.8 0.8 copy-start.7
  85.4 22.9 %copy-start.2 = (f32[8,72,128]{2,1,0:T(8,128)S(1)}, f32[8,72,128]{2,1,0:T(8,128)}, u32[]{:S(2)}) copy-start(f32[8,72,128]{2,1,0:T(8,128)} %copy-done) | copy-start | bytes 884740
  85.4 22.9 %copy-start.10 = (s32[4]{0:T(128)S(1)}, s32[4]{0:T(128)}, u32[]{:S(2)}) copy-start(s32[4]{0:T(128)} %pad_add_fusion.c_ref.refs_0_.where_ref) | copy-start | bytes 52
  85.4 16.1 %collective-permute-start.18 = (bf16[48,16,512]{2,1,0:T(8,128)(2,1)}, bf16[48,16,512]{2,1,0:T(8,128)(2,1)}, u32[]{:S(2)}, u32[]{:S(2)}) collective-permute-start(bf16[48,16,512]{2,1,0:T(8,128)(2,1)} %get-tuple-element.99), channel_id=1, source_target_pairs={{0,16},{16,0},{1,17},{17,1},{2,18},{18,2},{3,19},{19,3},{4,20},{20... | collective-permute-start | bytes 2359304 | tf_op jit(solution)/shard_map/ppermute | solution.py:34
  91.3 6.1 %collective-permute-start.15 = (bf16[2,400,128]{2,1,0:T(8,128)(2,1)}, bf16[2,400,128]{2,1,0:T(8,128)(2,1)S(1)}, u32[]{:S(2)}, u32[]{:S(2)}) collective-permute-start(bf16[2,400,128]{2,1,0:T(8,128)(2,1)} %get-tuple-element.96), channel_id=1, source_target_pairs={{0,2},{2,4},{4,6},{6,0},{1,3},{3,5},{5,7},{7,1},{8,10},{10,12},{12... | collective-permute-start | bytes 614408 | tf_op jit(solution)/shard_map/ppermute | solution.py:616
  92.2 7.8 %collective-permute-start.16 = (bf16[2,400,128]{2,1,0:T(8,128)(2,1)}, bf16[2,400,128]{2,1,0:T(8,128)(2,1)S(1)}, u32[]{:S(2)}, u32[]{:S(2)}) collective-permute-start(bf16[2,400,128]{2,1,0:T(8,128)(2,1)} %get-tuple-element.97), channel_id=1, source_target_pairs={{0,4},{2,6},{4,0},{6,2},{1,5},{3,7},{5,1},{7,3},{8,12},{10,14},{12... | collective-permute-start | bytes 614408 | tf_op jit(solution)/shard_map/ppermute | solution.py:616
  94.5 6.1 %collective-permute-start.17 = (bf16[2,400,128]{2,1,0:T(8,128)(2,1)}, bf16[2,400,128]{2,1,0:T(8,128)(2,1)S(1)}, u32[]{:S(2)}, u32[]{:S(2)}) collective-permute-start(bf16[2,400,128]{2,1,0:T(8,128)(2,1)} %get-tuple-element.98), channel_id=1, source_target_pairs={{0,6},{2,0},{4,2},{6,4},{1,7},{3,1},{5,3},{7,5},{8,14},{10,8},{12,... | collective-permute-start | bytes 614408 | tf_op jit(solution)/shard_map/ppermute | solution.py:616
  101.5 6.7 %collective-permute-start.19 = (bf16[400,128]{1,0:T(8,128)(2,1)S(1)}, bf16[400,128]{1,0:T(8,128)(2,1)S(1)}, u32[]{:S(2)}, u32[]{:S(2)}) collective-permute-start(bf16[400,128]{1,0:T(8,128)(2,1)S(1)} %fusion.1), channel_id=1, source_target_pairs={{0,8},{8,0},{1,9},{9,1},{2,10},{10,2},{3,11},{11,3},{4,12},{12,4},... | collective-permute-start | bytes 307208 | tf_op jit(solution)/shard_map/ppermute | solution.py:34
  108.3 0.9 copy-start.4
  119.7 6.5 %copy-start.19 = (bf16[16,16,512]{2,1,0:T(8,128)(2,1)S(1)}, bf16[16,16,512]{2,1,0:T(8,128)(2,1)}, u32[]{:S(2)}) copy-start(bf16[16,16,512]{2,1,0:T(8,128)(2,1)} %get-tuple-element.108) | copy-start | bytes 786436
  119.7 16.4 %copy-start.11 = (s32[4]{0:T(128)S(1)}, s32[4]{0:T(128)}, u32[]{:S(2)}) copy-start(s32[4]{0:T(128)} %pad_add_fusion.c_ref.refs_0_.where_ref) | copy-start | bytes 52
  122.7 4.5 %collective-permute-start.20 = (bf16[2,128,128]{2,1,0:T(8,128)(2,1)}, bf16[2,128,128]{2,1,0:T(8,128)(2,1)S(1)}, u32[]{:S(2)}, u32[]{:S(2)}) collective-permute-start(bf16[2,128,128]{2,1,0:T(8,128)(2,1)} %get-tuple-element.105), channel_id=1, source_target_pairs={{0,2},{2,4},{4,6},{6,0},{1,3},{3,5},{5,7},{7,1},{8,10},{10,12},{12... | collective-permute-start | bytes 196616 | tf_op jit(solution)/shard_map/ppermute | solution.py:616
  123.2 5.5 %collective-permute-start.21 = (bf16[2,128,128]{2,1,0:T(8,128)(2,1)}, bf16[2,128,128]{2,1,0:T(8,128)(2,1)S(1)}, u32[]{:S(2)}, u32[]{:S(2)}) collective-permute-start(bf16[2,128,128]{2,1,0:T(8,128)(2,1)} %get-tuple-element.106), channel_id=1, source_target_pairs={{0,4},{2,6},{4,0},{6,2},{1,5},{3,7},{5,1},{7,3},{8,12},{10,14},{12... | collective-permute-start | bytes 196616 | tf_op jit(solution)/shard_map/ppermute | solution.py:616
  126.2 3.7 %collective-permute-start.22 = (bf16[2,128,128]{2,1,0:T(8,128)(2,1)}, bf16[2,128,128]{2,1,0:T(8,128)(2,1)S(1)}, u32[]{:S(2)}, u32[]{:S(2)}) collective-permute-start(bf16[2,128,128]{2,1,0:T(8,128)(2,1)} %get-tuple-element.107), channel_id=1, source_target_pairs={{0,6},{2,0},{4,2},{6,4},{1,7},{3,1},{5,3},{7,5},{8,14},{10,8},{12,... | collective-permute-start | bytes 196616 | tf_op jit(solution)/shard_map/ppermute | solution.py:616
  126.2 5.6 %collective-permute-start.23 = (bf16[16,16,512]{2,1,0:T(8,128)(2,1)S(1)}, bf16[16,16,512]{2,1,0:T(8,128)(2,1)S(1)}, u32[]{:S(2)}, u32[]{:S(2)}) collective-permute-start(bf16[16,16,512]{2,1,0:T(8,128)(2,1)S(1)} %copy-done.19), channel_id=1, source_target_pairs={{0,16},{16,0},{1,17},{17,1},{2,18},{18,2},{3,19},{19,3},{4,20},{20... | collective-permute-start | bytes 786440 | tf_op jit(solution)/shard_map/ppermute | solution.py:34
  131.8 31.7 %copy-start.17 = (bf16[16,16,512]{2,1,0:T(8,128)(2,1)}, bf16[16,16,512]{2,1,0:T(8,128)(2,1)S(1)}, u32[]{:S(2)}) copy-start(bf16[16,16,512]{2,1,0:T(8,128)(2,1)S(1)} %collective-permute-done.23.oth_ref) | copy-start | bytes 786436
  131.8 4.3 %collective-permute-start.24 = (bf16[128,128]{1,0:T(8,128)(2,1)S(1)}, bf16[128,128]{1,0:T(8,128)(2,1)S(1)}, u32[]{:S(2)}, u32[]{:S(2)}) collective-permute-start(bf16[128,128]{1,0:T(8,128)(2,1)S(1)} %fusion.3), channel_id=1, source_target_pairs={{0,8},{8,0},{1,9},{9,1},{2,10},{10,2},{3,11},{11,3},{4,12},{12,4},... | collective-permute-start | bytes 98312 | tf_op jit(solution)/shard_map/ppermute | solution.py:34
  136.1 0.8 copy-start.6
  137.6 16.7 %collective-permute-start.25 = (bf16[2,128,128]{2,1,0:T(8,128)(2,1)S(1)}, bf16[2,128,128]{2,1,0:T(8,128)(2,1)S(1)}, u32[]{:S(2)}, u32[]{:S(2)}) collective-permute-start(bf16[2,128,128]{2,1,0:T(8,128)(2,1)S(1)} %get-tuple-element.113), channel_id=1, source_target_pairs={{0,1},{1,0},{2,3},{3,2},{4,5},{5,4},{6,7},{7,6},{8,9},{9,8},{10,11... | collective-permute-start | bytes 196616 | tf_op jit(solution)/shard_map/ppermute | solution.py:34
  155.6 8.9 %all-to-all-start.4 = ((bf16[8,64,128]{2,1,0:T(8,128)(2,1)}), bf16[8,64,128]{2,1,0:T(8,128)(2,1)S(1)}, u32[]{:S(2)}, u32[]{:S(2)}) async-start(bf16[8,64,128]{2,1,0:T(8,128)(2,1)} %arrange.1), calls=%async_computation.4 | async-start | bytes 262144 | tf_op jit(solution)/shard_map/all_to_all | solution.py:38
  164.5 0.7 copy-start.14

commit v4 on v3

--- a/solution.py
+++ b/solution.py
@@ -18,7 +18,7 @@
 HBM = pl.BlockSpec(memory_space=pltpu.HBM)
 LARGE = 62 * 1024 * 1024 + 512 * 1024
 SMALL = 8 * 1024 * 1024
-CHUNKS = (48, 29, 48)
+CHUNKS = (57, 22, 46)
 EXTRA = 16
 
 
@@ -39,7 +39,7 @@
 
 
 def sums_kernel(
-    c_ref, tok_ref, filt_ref, poles_ref, res_ref, state_ref, cache_ref, out_ref, *refs
+    tok_ref, filt_ref, poles_ref, res_ref, state_ref, cache_ref, out_ref, *refs
 ):
     pieces, (sent_ref, taps, rows, held, sems, sem_out) = refs[: len(CHUNKS)], refs[len(CHUNKS) :]
     copies = []
@@ -56,11 +56,16 @@
     )
     taps[128:136, :] = jnp.zeros((8, 512), F32)
     rows[64:128, :] = jnp.zeros((64, 512), F32)
-    rows[64:66, :] = taps[0:2, :]
     once = res_ref[...] * poles_ref[...]
     twice = once * poles_ref[...]
-    rows[66:67, :] = jnp.sum(res_ref[...], axis=0, keepdims=True)
-    rows[67:68, :] = jnp.sum(once, axis=0, keepdims=True)
+    gains = (
+        taps[0:1, :], taps[1:2, :],
+        jnp.sum(res_ref[...], axis=0, keepdims=True), jnp.sum(once, axis=0, keepdims=True),
+    )
+    for k, gain in enumerate(gains):
+        high = gain.astype(BF).astype(F32)
+        rows[64 + k : 65 + k, :] = high
+        rows[72 + k : 73 + k, :] = gain - high
     for b in range(16):
         state = state_ref[b]
         rows[32 + b : 33 + b, :] = jnp.sum(state * once, axis=0, keepdims=True)
@@ -91,29 +96,31 @@
     rows[0:16, :] = sums[0]
     rows[16:32, :] = sums[1]
     columns = rows[...].T
-    lane = lax.broadcasted_iota(I32, (8, 128), 1)
-    start = (c_ref[1] % 4) * 32
-    tok = jnp.zeros((8, 128), I32)
+    columns = columns.astype(BF)
+    lane = lax.broadcasted_iota(I32, (16, 128), 1)
+    start = ((lax.axis_index("y") & 1) * 2 + lax.axis_index("xl")) * 32
+    tok = jnp.zeros((16, 128), I32)
     for t in range(2):
         for b in range(16):
             tok = jnp.where(lane == start + 16 * t + b, tok_ref[t, b], tok)
-    tok = tok.astype(F32)
+    first = lax.broadcasted_iota(I32, (16, 128), 0) == 0
+    tok = jnp.where(first, tok >> 4, tok & 15).astype(F32).astype(BF)
     for i in range(8):
         out_ref[i, 0:64, :] = columns[64 * i : 64 * i + 64, :]
-        out_ref[i, 64:72, :] = tok
+        out_ref[i, 64:80, :] = tok
     for copy in outs:
         copy.wait()
 
 
-def make_sums(where, tokens, filters, poles, residues, state, cache):
+def make_sums(tokens, filters, poles, residues, state, cache):
     return pl.pallas_call(
         sums_kernel,
         grid=(1,),
         in_specs=[
-            SMEM, SMEM, whole(32, 128), whole(16, 512), whole(16, 512), whole(16, 16, 512), HBM,
-        ],
-        out_specs=[whole(8, 72, 128)] + [HBM] * len(CHUNKS) + [whole(16, 16, 512)],
-        out_shape=[jax.ShapeDtypeStruct((8, 72, 128), F32)]
+            SMEM, whole(32, 128), whole(16, 512), whole(16, 512), whole(16, 16, 512), HBM,
+        ],
+        out_specs=[whole(8, 80, 128)] + [HBM] * len(CHUNKS) + [whole(16, 16, 512)],
+        out_shape=[jax.ShapeDtypeStruct((8, 80, 128), BF)]
         + [jax.ShapeDtypeStruct((size, 16, 512), BF) for size in CHUNKS + (16,)],
         scratch_shapes=[
             pltpu.VMEM((136, 512), F32),
@@ -124,7 +131,7 @@
         ],
         compiler_params=params(),
         name="state_sums",
-    )(where, tokens, filters, poles, residues, state, cache)
+    )(tokens, filters, poles, residues, state, cache)
 
 
 def index_kernel(c_ref, par_ref, out_ref):
@@ -220,12 +227,13 @@
     @pl.when(pl.program_id(0) == 0)
     def _():
         c = c_ref[0]
-        tok = jnp.zeros((8, 128), F32)
+        tok = jnp.zeros((16, 128), F32)
         for q in range(4):
-            tok = tok + got_ref[c * 4 + q, 64:72, :]
+            tok = tok + got_ref[c * 4 + q, 64:80, :].astype(F32)
             send_ref[q] = got_ref[4 - c * 4 + q, 0:64, :]
         vocab = lax.broadcasted_iota(I32, (512, 128), 0)
-        onehot = (vocab == tok[0:1, :].astype(I32)).astype(BF)
+        tok = (tok[0:1, :] * 16.0 + tok[1:2, :] + 0.5).astype(I32)
+        onehot = (vocab == tok).astype(BF)
         halves = []
         for k, gain in enumerate((g_own, g_oth)):
             x = jnp.dot(tables[k], onehot, preferred_element_type=F32)
@@ -251,14 +259,14 @@
         embed_kernel,
         grid=(2,),
         in_specs=[
-            SMEM, whole(8, 72, 128), whole(2, 512, 512), whole(2, 512), whole(2, 512),
+            SMEM, whole(8, 80, 128), whole(2, 512, 512), whole(2, 512), whole(2, 512),
             *weights(0, 3072),
         ],
         out_specs=[*IN_SPECS, whole(2, 512, 128), whole(4, 64, 128)],
         out_shape=[
             *IN_SHAPE,
             jax.ShapeDtypeStruct((2, 512, 128), BF),
-            jax.ShapeDtypeStruct((4, 64, 128), F32),
+            jax.ShapeDtypeStruct((4, 64, 128), BF),
         ],
         scratch_shapes=IN_SCRATCH,
         compiler_params=params(),
@@ -335,12 +343,13 @@
         own = c == k
         acc = jnp.zeros((64, 128), F32)
         for q in range(4):
-            sums = jnp.where(own, t_own[c * 4 + q, 0:64, :], t_oth[q])
-            pick = (square + 128 * q == idx_ref[block : block + 1, :]).astype(F32)
-            acc = acc + jnp.dot(sums, pick, preferred_element_type=F32, precision=HIGH)
+            sums = jnp.where(own, t_own[c * 4 + q, 0:64, :].astype(F32), t_oth[q].astype(F32))
+            pick = (square + 128 * q == idx_ref[block : block + 1, :]).astype(BF)
+            acc = acc + jnp.dot(sums.astype(BF), pick, preferred_element_type=F32)
             if q == 0:
-                first.append(sums[:, 64 + 2 * block : 65 + 2 * block])
-                second.append(sums[:, 65 + 2 * block : 66 + 2 * block])
+                gain = lambda lane: sums[:, lane : lane + 1] + sums[:, lane + 8 : lane + 9]
+                first.append(gain(64 + 2 * block))
+                second.append(gain(65 + 2 * block))
         parts.append(acc)
     first, second = jnp.concatenate(first, axis=0), jnp.concatenate(second, axis=0)
     filtered = first * kv.astype(F32) + second * kv_before + jnp.concatenate(parts, axis=0)
@@ -354,7 +363,7 @@
         lambda *refs: mix_kernel(block, *refs),
         grid=(1,),
         in_specs=[
-            SMEM, *terms_specs(400), whole(8, 72, 128), whole(4, 64, 128), whole(8, 128)
+            SMEM, *terms_specs(400), whole(8, 80, 128), whole(4, 64, 128), whole(8, 128)
         ],
         out_specs=[whole(8, 128, 128), whole(128, 128)],
         out_shape=[
@@ -366,8 +375,7 @@
     )(where, *received, t_own, t_oth, idx)
 
 
-def out_kernel(c_ref, a_ref, w_own, w_oth, *refs):
-    *outs, rows, spread = refs
+def out_kernel(c_ref, a_ref, w_own, w_oth, out_ref, rows):
 
     @pl.when(pl.program_id(0) == 0)
     def _():
@@ -376,7 +384,8 @@
 
     acc = jnp.dot(w_own[0], rows[0], preferred_element_type=F32)
     acc = (acc + jnp.dot(w_oth[0], rows[1], preferred_element_type=F32)).astype(BF)
-    hand_out(acc, 128, c_ref, outs, spread)
+    for k in range(4):
+        out_ref[k] = acc[128 * k : 128 * k + 128, :]
 
 
 def project_out(block, where, rows, w_own, w_oth):
@@ -384,18 +393,24 @@
         out_kernel,
         grid=(2,),
         in_specs=[SMEM, whole(8, 128, 128), *weights(block, 1024)],
-        out_specs=[whole(2, 128, 128)] * 4,
-        out_shape=[jax.ShapeDtypeStruct((2, 128, 128), BF)] * 4,
-        scratch_shapes=[pltpu.VMEM((2, 512, 128), BF), pltpu.VMEM((512, 128), BF)],
+        out_specs=pl.BlockSpec((4, 128, 128), lambda g: (g, 0, 0)),
+        out_shape=jax.ShapeDtypeStruct((8, 128, 128), BF),
+        scratch_shapes=[pltpu.VMEM((2, 512, 128), BF)],
         compiler_params=params(),
         cost_estimate=COST_OUT,
         name="project_out",
     )(where, rows, w_own, w_oth)
 
 
-def residual_kernel(c_ref, *refs):
-    x_ref, out_ref = refs[5:]
-    outward = add_up(refs[:5]).astype(BF).astype(F32)
+def add_blocks(r_ref):
+    total = r_ref[0].astype(F32)
+    for g in range(1, 8):
+        total = total + r_ref[g].astype(F32)
+    return total.astype(BF).astype(F32)
+
+
+def residual_kernel(c_ref, r_ref, x_ref, out_ref):
+    outward = add_blocks(r_ref)
     start = pl.multiple_of(c_ref[1] * 64, 64)
     before = jnp.concatenate(
         [x_ref[c_ref[0] ^ k, pl.ds(start, 64), :] for k in range(2)], axis=0
@@ -409,17 +424,16 @@
     return pl.pallas_call(
         residual_kernel,
         grid=(1,),
-        in_specs=[SMEM, *terms_specs(128), whole(2, 512, 128)],
+        in_specs=[SMEM, whole(8, 128, 128), whole(2, 512, 128)],
         out_specs=whole(8, 128, 128),
         out_shape=jax.ShapeDtypeStruct((8, 128, 128), BF),
         compiler_params=params(SMALL),
         name="residual",
-    )(where, *received, embedded)
-
-
-def last_kernel(c_ref, *refs):
-    h_ref, kv0_ref, kv1_ref, keep_ref, send_ref = refs[5:]
-    outward = add_up(refs[:5]).astype(BF).astype(F32)
+    )(where, received, embedded)
+
+
+def last_kernel(c_ref, r_ref, h_ref, kv0_ref, kv1_ref, keep_ref, send_ref):
+    outward = add_blocks(r_ref)
     hidden = (h_ref[0].astype(F32) + outward).astype(BF).astype(F32).T
     first = c_ref[0] == 0
     kv0, kv1 = kv0_ref[...].astype(F32), kv1_ref[...].astype(F32)
@@ -439,14 +453,14 @@
         last_kernel,
         grid=(1,),
         in_specs=[
-            SMEM, *terms_specs(128), pl.BlockSpec((1, 128, 128), lambda g: (0, 0, 0)),
+            SMEM, whole(8, 128, 128), pl.BlockSpec((1, 128, 128), lambda g: (0, 0, 0)),
             whole(128, 128), whole(128, 128),
         ],
         out_specs=[whole(2, 128, 128)] * 2,
         out_shape=[jax.ShapeDtypeStruct((2, 128, 128), BF)] * 2,
         compiler_params=params(SMALL),
         name="last",
-    )(where, *received, hidden, kv0, kv1)
+    )(where, received, hidden, kv0, kv1)
 
 
 def arrange_kernel(c_ref, keep_ref, got_ref, out_ref):
@@ -594,7 +608,7 @@
     e_oth = swap(embed_table, "c")
     g_oth = swap(norm_gain, "c")
     sums, *pieces = make_sums(
-        where, tokens, fir_filters, mode_poles, residues, modal_state, cache
+        tokens, fir_filters, mode_poles, residues, modal_state, cache
     )
     w_in, w_out, e_oth, g_oth, sums = lax.optimization_barrier(
         (w_in, w_out, e_oth, g_oth, sums)
@@ -625,19 +639,18 @@
         where, send(got), tables, norm_gain, g_oth, w_in, w_in_oth
     )
     t_oth = swap(t_send, "c")
+    def gather(rows):
+        rows, moved[-1] = lax.optimization_barrier((exchange(send(rows), DP), moved[-1]))
+        return rows
+
     gated, kv0 = mix(0, where, scatter(partial), got, t_oth, idx)
-    partial = project_out(
-        0, where, send(exchange(gated, DP)), w_out, w_out_oth
-    )
-    hidden = residual(where, scatter(partial), embedded)
-    partial = project_in(
-        where, send(exchange(hidden, DP)), norm_gain, g_oth, w_in, w_in_oth
-    )
+    partial = project_out(0, where, gather(gated), w_out, w_out_oth)
+    hidden = residual(where, exchange(partial, XZ), embedded)
+    rows = send(exchange(hidden, DP))
+    partial = project_in(where, rows, norm_gain, g_oth, w_in, w_in_oth)
     gated, kv1 = mix(1, where, scatter(partial), got, t_oth, idx)
-    partial = project_out(
-        1, where, send(exchange(gated, DP)), w_out, w_out_oth
-    )
-    keep, crossing = last(where, scatter(partial), hidden, kv0, kv1)
+    partial = project_out(1, where, gather(gated), w_out, w_out_oth)
+    keep, crossing = last(where, exchange(partial, XZ), hidden, kv0, kv1)
     received = exchange(arrange(where, keep, swap(crossing, "c")), DP)
     *moved, state_oth = moved
     fir_before = reorder(where, parents, cache, moved)

time: 169 us -> 165 us (0.976)
  blocking collectives: 28 us -> 55.7 us
  starting transfers between devices: 60.3 us -> 41.9 us
  waiting for transfers between devices: 31.1 us -> 22.2 us
  local copies, waits for them, and re-layouts: 5.45 us -> 3.47 us
    all_to_all x3 -> x5, blocking collectives: 28 us -> 55.7 us  [exchange(): return lax.all_to_all(value, axes, 0, 0, tiled=True)]
    ppermute x12 -> x6, starting transfers between devices: 18.1 us -> 8.44 us  [scatter(): terms[s] = lax.ppermute(terms[s], 'z', [(z, (z + s) % 4) for z in range(4)])]
    ppermute x14 -> x12, starting transfers between devices: 33.6 us -> 24.9 us  [swap(): return lax.ppermute(value, axis, [(0, 1), (1, 0)])]
    ppermute x14 -> x12, waiting for transfers between devices: 12.6 us -> 7.11 us  [swap(): return lax.ppermute(value, axis, [(0, 1), (1, 0)])]
    unnamed x40 -> x32, local copies, waits for them, and re-layouts: 5.45 us -> 3.47 us
    all_to_all x2, waiting for transfers between devices: 3.8 us -> 1.88 us  [exchange(): return lax.all_to_all(value, axes, 0, 0, tiled=True)]
    add x4 -> x2, other arithmetic: 3.47 us -> 1.9 us  [scatter(): far = sum((term[1].astype(F32) for term in terms)).astype(BF)]
    ppermute x12 -> x6, waiting for transfers between devices: 14.8 us -> 13.2 us  [scatter(): terms[s] = lax.ppermute(terms[s], 'z', [(z, (z + s) % 4) for z in range(4)])]
  transfers between devices with their start and end apart: 28 -> 20, of which waited for: 18 -> 10; matrix products, arithmetic and copies ran while one was open for 2% -> 2% of each run, Pallas kernels for 17% -> 15%
where the time goes in v4:
time: 165 us; the launch traced here: 164 us
  blocking collectives  55.7 us (34%)
  starting transfers between devices  41.9 us (25%)
  Pallas kernels  37.4 us (23%)
  waiting for transfers between devices  22.2 us (13%)
  local copies, waits for them, and re-layouts  3.47 us (2%)
  other arithmetic  2.5 us (2%)
    all_to_all x5, blocking collectives, exchange(): return lax.all_to_all(value, axes, 0, 0, tiled=True)  55.7 us
    ppermute x12, starting transfers between devices, swap(): return lax.ppermute(value, axis, [(0, 1), (1, 0)])  24.9 us
    ppermute x6, waiting for transfers between devices, scatter(): terms[s] = lax.ppermute(terms[s], 'z', [(z, (z + s) % 4) for z in range(4)])  13.2 us
    all_to_all x2, starting transfers between devices, exchange(): return lax.all_to_all(value, axes, 0, 0, tiled=True)  8.57 us
    ppermute x6, starting transfers between devices, scatter(): terms[s] = lax.ppermute(terms[s], 'z', [(z, (z + s) % 4) for z in range(4)])  8.44 us
    ppermute x12, waiting for transfers between devices, swap(): return lax.ppermute(value, axis, [(0, 1), (1, 0)])  7.11 us
    pallas_call x1, Pallas kernels, project_embed(): pl.pallas_call(embed_kernel, grid=(2,), in_specs=[SMEM, whole(8, 80, 128)...  5.95 us
    pallas_call x2, Pallas kernels, project_out(): pl.pallas_call(out_kernel, grid=(2,), in_specs=[SMEM, whole(8, 128, 128),...  5.88 us
  transfers between devices with their start and end apart: 20, of which 10 were waited for; matrix products, arithmetic and copies ran while one was open for 2% of the time, Pallas kernels for 15%

profile of v4, /device:TPU:1, one launch (start us, length us, event | category | flops | bytes accessed | tf_op | source)
XLA Modules:
  0.0 164.0 jit_solution(18088124940900279018)
XLA Ops:
  0.6 1.5 collective-permute-start
  2.2 4.5 %state_sums.1 = (bf16[8,80,128]{2,1,0:T(8,128)(2,1)}, bf16[57,16,512]{2,1,0:T(8,128)(2,1)}, bf16[22,16,512]{2,1,0:T(8,128)(2,1)}, bf16[46,16,512]{2,1,0:T(8,128)(2,1)}, bf16[16,16,512]{2,1,0:T(8,128)(2,1)}) custom-call(s32[2,16]{1,0:T(2,128)} %tok_ref.1, f32[32,128]{1,0:T(8,128)} %filt_ref.1, f32[16,512]{1,0:T(8,128)} %poles_ref.3, f32[16,512]{1,0:T(8,128)} %res_ref.1, ...), custom_call_target="tpu_custom_call" | custom-call | tf_op jit(solution)/shard_map/state_sums/pallas_call | solution.py:116
  7.4 5.2 %all-to-all-start = ((bf16[8,80,128]{2,1,0:T(8,128)(2,1)}), bf16[8,80,128]{2,1,0:T(8,128)(2,1)S(1)}, u32[]{:S(2)}, u32[]{:S(2)}) async-start(bf16[8,80,128]{2,1,0:T(8,128)(2,1)} %get-tuple-element.59), calls=%async_computation | async-start | bytes 327680 | tf_op jit(solution)/shard_map/all_to_all | solution.py:38
  12.6 0.6 pad_add_fusion.c_ref.refs_0_.where_ref
  13.2 1.8 %indices.1.refs_8_ = s32[8,128]{1,0:T(8,128)} custom-call(s32[4]{0:T(128)} %pad_add_fusion.c_ref.refs_0_.where_ref, s32[2,128]{1,0:T(2,128)} %par_ref.5), custom_call_target="tpu_custom_call" | custom-call | tf_op jit(solution)/shard_map/indices/pallas_call | solution.py:160
  14.9 2.5 %turn.1.tables = bf16[2,512,512]{2,1,0:T(8,128)(2,1)} custom-call(bf16[512,512]{1,0:T(8,128)(2,1)} %own_ref.2, bf16[512,512]{1,0:T(8,128)(2,1)} %copy-done.14), custom_call_target="tpu_custom_call" | custom-call | tf_op jit(solution)/shard_map/turn/pallas_call | solution.py:177
  17.4 0.8 all-to-all-done.got_ref.refs_6_
  18.3 0.7 collective-permute-start.6
  19.0 6.0 %embed_project.1 = (bf16[2,400,128]{2,1,0:T(8,128)(2,1)}, bf16[2,400,128]{2,1,0:T(8,128)(2,1)}, bf16[2,400,128]{2,1,0:T(8,128)(2,1)}, bf16[2,400,128]{2,1,0:T(8,...) custom-call(s32[4]{0:T(128)} %pad_add_fusion.c_ref.refs_0_.where_ref, bf16[8,80,128]{2,1,0:T(8,128)(2,1)} %copy-done, ...), custom_call_target="tpu_custom_call" | custom-call | flops 805306368 | bytes 7340032 | tf_op jit(solution)/shard_map/embed_project/pallas_call | solution.py:258
  25.0 1.7 %collective-permute-start.3 = (bf16[2,400,128]{2,1,0:T(8,128)(2,1)}, bf16[2,400,128]{2,1,0:T(8,128)(2,1)S(1)}, u32[]{:S(2)}, u32[]{:S(2)}) collective-permute-start(bf16[2,400,128]{2,1,0:T(8,128)(2,1)} %get-tuple-element.67), channel_id=1, source_target_pairs={{0,2},{2,4},{4,6},{6,0},{1,3},{3,5},{5,7},{7,1},{8,10},{10,12},{12... | collective-permute-start | bytes 614408 | tf_op jit(solution)/shard_map/ppermute | solution.py:630
  26.6 3.3 %collective-permute-start.4 = (bf16[2,400,128]{2,1,0:T(8,128)(2,1)}, bf16[2,400,128]{2,1,0:T(8,128)(2,1)S(1)}, u32[]{:S(2)}, u32[]{:S(2)}) collective-permute-start(bf16[2,400,128]{2,1,0:T(8,128)(2,1)} %get-tuple-element.68), channel_id=1, source_target_pairs={{0,4},{2,6},{4,0},{6,2},{1,5},{3,7},{5,1},{7,3},{8,12},{10,14},{12... | collective-permute-start | bytes 614408 | tf_op jit(solution)/shard_map/ppermute | solution.py:630
  30.0 0.7 collective-permute-start.5
  30.7 1.8 %collective-permute-done.3.refs_2_ = bf16[2,400,128]{2,1,0:T(8,128)(2,1)S(1)} collective-permute-done((bf16[2,400,128]{2,1,0:T(8,128)(2,1)}, bf16[2,400,128]{2,1,0:T(8,128)(2,1)S(1)}, u32[]{:S(2)}, u32[]{:S(2)}) %collective-permute-start.3) | collective-permute-done | bytes 204832 | tf_op jit(solution)/shard_map/ppermute | solution.py:630
  32.5 5.0 %collective-permute-done.4.refs_3_ = bf16[2,400,128]{2,1,0:T(8,128)(2,1)S(1)} collective-permute-done((bf16[2,400,128]{2,1,0:T(8,128)(2,1)}, bf16[2,400,128]{2,1,0:T(8,128)(2,1)S(1)}, u32[]{:S(2)}, u32[]{:S(2)}) %collective-permute-start.4) | collective-permute-done | bytes 204832 | tf_op jit(solution)/shard_map/ppermute | solution.py:630
  37.5 1.0 fusion
  38.8 2.5 %collective-permute-start.7 = (bf16[400,128]{1,0:T(8,128)(2,1)S(1)}, bf16[400,128]{1,0:T(8,128)(2,1)S(1)}, u32[]{:S(2)}, u32[]{:S(2)}) collective-permute-start(bf16[400,128]{1,0:T(8,128)(2,1)S(1)} %fusion), channel_id=1, source_target_pairs={{0,8},{8,0},{1,9},{9,1},{2,10},{10,2},{3,11},{11,3},{4,12},{12,4},... | collective-permute-start | bytes 307208 | tf_op jit(solution)/shard_map/ppermute | solution.py:34
  41.3 3.1 %collective-permute-start.8 = (bf16[4,64,128]{2,1,0:T(8,128)(2,1)}, bf16[4,64,128]{2,1,0:T(8,128)(2,1)S(1)}, u32[]{:S(2)}, u32[]{:S(2)}) collective-permute-start(bf16[4,64,128]{2,1,0:T(8,128)(2,1)} %get-tuple-element.72), channel_id=1, source_target_pairs={{0,1},{1,0},{2,3},{3,2},{4,5},{5,4},{6,7},{7,6},{8,9},{9,8},{10,11... | collective-permute-start | bytes 196616 | tf_op jit(solution)/shard_map/ppermute | solution.py:34
  44.4 1.1 collective-permute-done.8.refs_7_
  45.5 0.9 copy-done.1
  46.4 0.9 copy-done.3
  47.3 0.8 mix.2
  48.4 12.5 %all_to_all.35.a_ref = bf16[8,128,128]{2,1,0:T(8,128)(2,1)} all-to-all(bf16[8,128,128]{2,1,0:T(8,128)(2,1)S(1)} %get-tuple-element.76), channel_id=1, replica_groups=mesh['y'=4,'xl'=2,'xh'=2,'z'=4,'c'=2] {'y','xl'}, dimensions={0} | all-to-all | bytes 524288 | tf_op jit(solution)/shard_map/all_to_all | solution.py:38
  60.9 3.0 %project_out.2 = bf16[8,128,128]{2,1,0:T(8,128)(2,1)} custom-call(s32[4]{0:T(128)} %pad_add_fusion.c_ref.refs_0_.where_ref, bf16[8,128,128]{2,1,0:T(8,128)(2,1)} %all_to_all.35.a_ref, bf16[2,1024,512]{2,1,0:T(8,128)(2,1)} %bitcast.16, bf16[2,1024,512]{2,1,0:T(8,128)(2,1)} %collective-permute-done.10.w_oth), custom_call_target="tpu_custom_call" | custom-call | flops 268435456 | bytes 2621440 | tf_op jit(solution)/shard_map/project_out/pallas_call | solution.py:392
  63.9 13.5 %all_to_all.36.r_ref = bf16[8,128,128]{2,1,0:T(8,128)(2,1)S(1)} all-to-all(bf16[8,128,128]{2,1,0:T(8,128)(2,1)} %project_out.2), channel_id=1, replica_groups=mesh['y'=4,'xl'=2,'xh'=2,'z'=4,'c'=2] {'xh','z'}, dimensions={0} | all-to-all | bytes 524288 | tf_op jit(solution)/shard_map/all_to_all | solution.py:38
  77.4 0.6 residual.1.h_ref
  78.0 9.2 %all_to_all.37.a_ref = bf16[8,128,128]{2,1,0:T(8,128)(2,1)} all-to-all(bf16[8,128,128]{2,1,0:T(8,128)(2,1)S(1)} %residual.1.h_ref), channel_id=1, replica_groups=mesh['y'=4,'xl'=2,'xh'=2,'z'=4,'c'=2] {'y','xl'}, dimensions={0} | all-to-all | bytes 524288 | tf_op jit(solution)/shard_map/all_to_all | solution.py:38
  87.8 5.3 %norm_project.1 = (bf16[2,400,128]{2,1,0:T(8,128)(2,1)}, bf16[2,400,128]{2,1,0:T(8,128)(2,1)}, bf16[2,400,128]{2,1,0:T(8,128)(2,1)}, bf16[2,400,128]{2,1,0:T(8,128)(2,1)}) custom-call(s32[4]{0:T(128)} %pad_add_fusion.c_ref.refs_0_.where_ref, bf16[8,128,128]{2,1,0:T(8,128)(2,1)} %all_to_all.37.a_ref, f32[2,512]{1,0:T(2,128)} %g_own.3, f32[2,512]{1,0:T(2,128)} %copy-done.15, ...), custom_call_target="tpu_custom_call" | custom-call | flops 805306368 | bytes 7340032 | tf_op jit(solution)/shard_map/norm_project/pallas_call | solution.py:299
  93.1 1.9 %collective-permute-start.12 = (bf16[2,400,128]{2,1,0:T(8,128)(2,1)}, bf16[2,400,128]{2,1,0:T(8,128)(2,1)S(1)}, u32[]{:S(2)}, u32[]{:S(2)}) collective-permute-start(bf16[2,400,128]{2,1,0:T(8,128)(2,1)} %get-tuple-element.85), channel_id=1, source_target_pairs={{0,4},{2,6},{4,0},{6,2},{1,5},{3,7},{5,1},{7,3},{8,12},{10,14},{12... | collective-permute-start | bytes 614408 | tf_op jit(solution)/shard_map/ppermute | solution.py:630
  95.0 0.9 collective-permute-start.13
  95.8 5.5 %collective-permute-done.11.refs_2_ = bf16[2,400,128]{2,1,0:T(8,128)(2,1)S(1)} collective-permute-done((bf16[2,400,128]{2,1,0:T(8,128)(2,1)}, bf16[2,400,128]{2,1,0:T(8,128)(2,1)S(1)}, u32[]{:S(2)}, u32[]{:S(2)}) %collective-permute-start.11) | collective-permute-done | bytes 204832 | tf_op jit(solution)/shard_map/ppermute | solution.py:630
  101.3 0.9 collective-permute-done.13.refs_4_
  102.3 1.0 fusion.1
  103.7 4.7 %collective-permute-done.15.refs_5_ = bf16[400,128]{1,0:T(8,128)(2,1)S(1)} collective-permute-done((bf16[400,128]{1,0:T(8,128)(2,1)S(1)}, bf16[400,128]{1,0:T(8,128)(2,1)S(1)}, u32[]{:S(2)}, u32[]{:S(2)}) %collective-permute-start.15) | collective-permute-done | bytes 102432 | tf_op jit(solution)/shard_map/ppermute | solution.py:34
  108.3 0.9 copy-done.4
  109.3 0.8 mix.3
  110.1 1.3 collective-permute-start.16
  111.4 9.2 %all_to_all.38.a_ref = bf16[8,128,128]{2,1,0:T(8,128)(2,1)} all-to-all(bf16[8,128,128]{2,1,0:T(8,128)(2,1)S(1)} %get-tuple-element.91), channel_id=1, replica_groups=mesh['y'=4,'xl'=2,'xh'=2,'z'=4,'c'=2] {'y','xl'}, dimensions={0} | all-to-all | bytes 524288 | tf_op jit(solution)/shard_map/all_to_all | solution.py:38
  120.6 2.9 %project_out.3 = bf16[8,128,128]{2,1,0:T(8,128)(2,1)} custom-call(s32[4]{0:T(128)} %pad_add_fusion.c_ref.refs_0_.where_ref, bf16[8,128,128]{2,1,0:T(8,128)(2,1)} %all_to_all.38.a_ref, bf16[2,1024,512]{2,1,0:T(8,128)(2,1)} %bitcast.17, bf16[2,1024,512]{2,1,0:T(8,128)(2,1)} %collective-permute-done.10.w_oth), custom_call_target="tpu_custom_call" | custom-call | flops 268435456 | bytes 2621440 | tf_op jit(solution)/shard_map/project_out/pallas_call | solution.py:392
  123.5 11.2 %all_to_all.39.r_ref = bf16[8,128,128]{2,1,0:T(8,128)(2,1)S(1)} all-to-all(bf16[8,128,128]{2,1,0:T(8,128)(2,1)} %project_out.3), channel_id=1, replica_groups=mesh['y'=4,'xl'=2,'xh'=2,'z'=4,'c'=2] {'xh','z'}, dimensions={0} | all-to-all | bytes 524288 | tf_op jit(solution)/shard_map/all_to_all | solution.py:38
  134.7 0.7 last.1
  135.5 14.0 %collective-permute-start.17 = (bf16[2,128,128]{2,1,0:T(8,128)(2,1)S(1)}, bf16[2,128,128]{2,1,0:T(8,128)(2,1)S(1)}, u32[]{:S(2)}, u32[]{:S(2)}) collective-permute-start(bf16[2,128,128]{2,1,0:T(8,128)(2,1)S(1)} %get-tuple-element.97), channel_id=1, source_target_pairs={{0,1},{1,0},{2,3},{3,2},{4,5},{5,4},{6,7},{7,6},{8,9},{9,8},{10,11... | collective-permute-start | bytes 196616 | tf_op jit(solution)/shard_map/ppermute | solution.py:34
  149.4 0.9 collective-permute-done.17.got_ref
  150.3 1.2 arrange.1
  151.6 3.4 %all-to-all-start.6 = ((bf16[8,64,128]{2,1,0:T(8,128)(2,1)}), bf16[8,64,128]{2,1,0:T(8,128)(2,1)S(1)}, u32[]{:S(2)}, u32[]{:S(2)}) async-start(bf16[8,64,128]{2,1,0:T(8,128)(2,1)} %arrange.1), calls=%async_computation.6 | async-start | bytes 262144 | tf_op jit(solution)/shard_map/all_to_all | solution.py:38
  154.9 4.5 %reorder.1.fir_ref = bf16[127,16,512]{2,1,0:T(8,128)(2,1)} custom-call(s32[4]{0:T(128)} %pad_add_fusion.c_ref.refs_0_.where_ref, s32[2,128]{1,0:T(2,128)} %par_ref.5, bf16[127,16,512]{2,1,0:T(8,128)(2,1)} %bitcast.19, bf16[57,16,512]{2,1,0:T(8,128)(2,1)} %copy-done.11, bf16[22,16,512]{2,1,0:T(8,128)(2,1)} %collective-permute-done.9.refs_1_, ...), custom_call_target="tpu_custom_call" | custom-call | flops 536870912 | bytes 6291456 | tf_op jit(solution)/shard_map/reorder/pallas_call | solution.py:538
  159.4 1.1 all-to-all-done.6.r_ref
  160.5 0.6 copy-done.13
  161.1 2.8 %final.1 = (bf16[2,16,512]{2,1,0:T(8,128)(2,1)}, bf16[127,16,512]{2,1,0:T(8,128)(2,1)}, f32[16,16,512]{2,1,0:T(8,128)}) custom-call(s32[4]{0:T(128)} %pad_add_fusion.c_ref.refs_0_.where_ref, s32[2,128]{1,0:T(2,128)} %par_ref.5, bf16[8,64,128]{2,1,0:T(8,128)(2,1)} %copy-done.13, f32[16,512]{1,0:T(8,128)} %poles_ref.3, ...), custom_call_target="tpu_custom_call", output_to_operand_aliasing={{1}: (6, {})} | custom-call | tf_op jit(solution)/shard_map/final/pallas_call | solution.py:578
  (46 shorter events, 2.4 us)
Async XLA Ops:
  0.6 6.1 %collective-permute-start = (bf16[512,512]{1,0:T(8,128)(2,1)}, bf16[512,512]{1,0:T(8,128)(2,1)S(1)}, u32[]{:S(2)}, u32[]{:S(2)}) collective-permute-start(bf16[512,512]{1,0:T(8,128)(2,1)} %own_ref.2), channel_id=1, source_target_pairs={{0,1},{1,0},{2,3},{3,2},{4,5},{5,4},{6,7},{7,6},{8,9},{9,8},{10,11... | collective-permute-start | bytes 1572872 | tf_op jit(solution)/shard_map/ppermute | solution.py:34
  2.1 4.6 %collective-permute-start.1 = (f32[2,512]{1,0:T(2,128)}, f32[2,512]{1,0:T(2,128)S(1)}, u32[]{:S(2)}, u32[]{:S(2)}) collective-permute-start(f32[2,512]{1,0:T(2,128)} %g_own.3), channel_id=1, source_target_pairs={{0,1},{1,0},{2,3},{3,2},{4,5},{5,4},{6,7},{7,6},{8,9},{9,8},{10,11... | collective-permute-start | bytes 12296 | tf_op jit(solution)/shard_map/ppermute | solution.py:34
  6.7 12.3 %copy-start.15 = (f32[2,512]{1,0:T(2,128)}, f32[2,512]{1,0:T(2,128)S(1)}, u32[]{:S(2)}) copy-start(f32[2,512]{1,0:T(2,128)S(1)} %collective-permute-done.1.g_oth) | copy-start | bytes 12292
  6.8 8.2 %copy-start.14 = (bf16[512,512]{1,0:T(8,128)(2,1)}, bf16[512,512]{1,0:T(8,128)(2,1)S(1)}, u32[]{:S(2)}) copy-start(bf16[512,512]{1,0:T(8,128)(2,1)S(1)} %collective-permute-done.oth_ref) | copy-start | bytes 1572868
  6.8 12.2 %collective-permute-start.2 = (bf16[2,3072,512]{2,1,0:T(8,128)(2,1)}, bf16[2,3072,512]{2,1,0:T(8,128)(2,1)}, u32[]{:S(2)}, u32[]{:S(2)}) collective-permute-start(bf16[2,3072,512]{2,1,0:T(8,128)(2,1)} %bitcast.12), channel_id=1, source_target_pairs={{0,1},{1,0},{2,3},{3,2},{4,5},{5,4},{6,7},{7,6},{8,9},{9,8},{10,11... | collective-permute-start | bytes 18874376 | tf_op jit(solution)/shard_map/ppermute | solution.py:34
  7.3 53.6 %collective-permute-start.10 = (bf16[2,1024,512]{2,1,0:T(8,128)(2,1)}, bf16[2,1024,512]{2,1,0:T(8,128)(2,1)}, u32[]{:S(2)}, u32[]{:S(2)}) collective-permute-start(bf16[2,1024,512]{2,1,0:T(8,128)(2,1)} %bitcast.15), channel_id=1, source_target_pairs={{0,1},{1,0},{2,3},{3,2},{4,5},{5,4},{6,7},{7,6},{8,9},{9,8},{10,11... | collective-permute-start | bytes 6291464 | tf_op jit(solution)/shard_map/ppermute | solution.py:34
  7.4 10.9 %all-to-all-start = ((bf16[8,80,128]{2,1,0:T(8,128)(2,1)}), bf16[8,80,128]{2,1,0:T(8,128)(2,1)S(1)}, u32[]{:S(2)}, u32[]{:S(2)}) async-start(bf16[8,80,128]{2,1,0:T(8,128)(2,1)} %get-tuple-element.59), calls=%async_computation | async-start | bytes 327680 | tf_op jit(solution)/shard_map/all_to_all | solution.py:38
  18.3 0.7 copy-start
  18.3 27.2 %copy-start.6 = (s32[4]{0:T(128)S(1)}, s32[4]{0:T(128)}, u32[]{:S(2)}) copy-start(s32[4]{0:T(128)} %pad_add_fusion.c_ref.refs_0_.where_ref) | copy-start | bytes 52
  18.3 27.2 %copy-start.10 = (s32[8,128]{1,0:T(8,128)S(1)}, s32[8,128]{1,0:T(8,128)}, u32[]{:S(2)}) copy-start(s32[8,128]{1,0:T(8,128)} %indices.1.refs_8_) | copy-start | bytes 12292
  18.3 20.6 %collective-permute-start.6 = (bf16[57,16,512]{2,1,0:T(8,128)(2,1)}, bf16[57,16,512]{2,1,0:T(8,128)(2,1)S(1)}, u32[]{:S(2)}, u32[]{:S(2)}) collective-permute-start(bf16[57,16,512]{2,1,0:T(8,128)(2,1)} %get-tuple-element.70), channel_id=1, source_target_pairs={{0,16},{16,0},{1,17},{17,1},{2,18},{18,2},{3,19},{19,3},{4,20},{20... | collective-permute-start | bytes 2801672 | tf_op jit(solution)/shard_map/ppermute | solution.py:34
  25.0 7.5 %collective-permute-start.3 = (bf16[2,400,128]{2,1,0:T(8,128)(2,1)}, bf16[2,400,128]{2,1,0:T(8,128)(2,1)S(1)}, u32[]{:S(2)}, u32[]{:S(2)}) collective-permute-start(bf16[2,400,128]{2,1,0:T(8,128)(2,1)} %get-tuple-element.67), channel_id=1, source_target_pairs={{0,2},{2,4},{4,6},{6,0},{1,3},{3,5},{5,7},{7,1},{8,10},{10,12},{12... | collective-permute-start | bytes 614408 | tf_op jit(solution)/shard_map/ppermute | solution.py:630
  26.6 10.9 %collective-permute-start.4 = (bf16[2,400,128]{2,1,0:T(8,128)(2,1)}, bf16[2,400,128]{2,1,0:T(8,128)(2,1)S(1)}, u32[]{:S(2)}, u32[]{:S(2)}) collective-permute-start(bf16[2,400,128]{2,1,0:T(8,128)(2,1)} %get-tuple-element.68), channel_id=1, source_target_pairs={{0,4},{2,6},{4,0},{6,2},{1,5},{3,7},{5,1},{7,3},{8,12},{10,14},{12... | collective-permute-start | bytes 614408 | tf_op jit(solution)/shard_map/ppermute | solution.py:630
  30.0 7.5 %collective-permute-start.5 = (bf16[2,400,128]{2,1,0:T(8,128)(2,1)}, bf16[2,400,128]{2,1,0:T(8,128)(2,1)S(1)}, u32[]{:S(2)}, u32[]{:S(2)}) collective-permute-start(bf16[2,400,128]{2,1,0:T(8,128)(2,1)} %get-tuple-element.69), channel_id=1, source_target_pairs={{0,6},{2,0},{4,2},{6,4},{1,7},{3,1},{5,3},{7,5},{8,14},{10,8},{12,... | collective-permute-start | bytes 614408 | tf_op jit(solution)/shard_map/ppermute | solution.py:630
  38.8 9.6 %copy-start.11 = (bf16[57,16,512]{2,1,0:T(8,128)(2,1)}, bf16[57,16,512]{2,1,0:T(8,128)(2,1)S(1)}, u32[]{:S(2)}) copy-start(bf16[57,16,512]{2,1,0:T(8,128)(2,1)S(1)} %collective-permute-done.6.refs_0_) | copy-start | bytes 2801668
  38.8 6.7 %collective-permute-start.7 = (bf16[400,128]{1,0:T(8,128)(2,1)S(1)}, bf16[400,128]{1,0:T(8,128)(2,1)S(1)}, u32[]{:S(2)}, u32[]{:S(2)}) collective-permute-start(bf16[400,128]{1,0:T(8,128)(2,1)S(1)} %fusion), channel_id=1, source_target_pairs={{0,8},{8,0},{1,9},{9,1},{2,10},{10,2},{3,11},{11,3},{4,12},{12,4},... | collective-permute-start | bytes 307208 | tf_op jit(solution)/shard_map/ppermute | solution.py:34
  41.3 4.2 %collective-permute-start.8 = (bf16[4,64,128]{2,1,0:T(8,128)(2,1)}, bf16[4,64,128]{2,1,0:T(8,128)(2,1)S(1)}, u32[]{:S(2)}, u32[]{:S(2)}) collective-permute-start(bf16[4,64,128]{2,1,0:T(8,128)(2,1)} %get-tuple-element.72), channel_id=1, source_target_pairs={{0,1},{1,0},{2,3},{3,2},{4,5},{5,4},{6,7},{7,6},{8,9},{9,8},{10,11... | collective-permute-start | bytes 196616 | tf_op jit(solution)/shard_map/ppermute | solution.py:34
  45.5 0.9 copy-start.1
  46.4 0.9 copy-start.3
  48.2 12.7 %collective-permute-start.9 = (bf16[22,16,512]{2,1,0:T(8,128)(2,1)}, bf16[22,16,512]{2,1,0:T(8,128)(2,1)}, u32[]{:S(2)}, u32[]{:S(2)}) collective-permute-start(bf16[22,16,512]{2,1,0:T(8,128)(2,1)} %get-tuple-element.77), channel_id=1, source_target_pairs={{0,16},{16,0},{1,17},{17,1},{2,18},{18,2},{3,19},{19,3},{4,20},{20... | collective-permute-start | bytes 1081352 | tf_op jit(solution)/shard_map/ppermute | solution.py:34
  60.9 16.5 %copy-start.5 = (bf16[2,512,128]{2,1,0:T(8,128)(2,1)S(1)}, bf16[2,512,128]{2,1,0:T(8,128)(2,1)}, u32[]{:S(2)}) copy-start(bf16[2,512,128]{2,1,0:T(8,128)(2,1)} %get-tuple-element.80.x_ref) | copy-start | bytes 786436
  60.9 16.5 %copy-start.7 = (s32[4]{0:T(128)S(1)}, s32[4]{0:T(128)}, u32[]{:S(2)}) copy-start(s32[4]{0:T(128)} %pad_add_fusion.c_ref.refs_0_.where_ref) | copy-start | bytes 52
  87.2 21.1 %copy-start.2 = (bf16[8,80,128]{2,1,0:T(8,128)(2,1)S(1)}, bf16[8,80,128]{2,1,0:T(8,128)(2,1)}, u32[]{:S(2)}) copy-start(bf16[8,80,128]{2,1,0:T(8,128)(2,1)} %copy-done) | copy-start | bytes 491524
  87.2 21.1 %copy-start.8 = (s32[4]{0:T(128)S(1)}, s32[4]{0:T(128)}, u32[]{:S(2)}) copy-start(s32[4]{0:T(128)} %pad_add_fusion.c_ref.refs_0_.where_ref) | copy-start | bytes 52
  87.2 16.0 %collective-permute-start.14 = (bf16[46,16,512]{2,1,0:T(8,128)(2,1)}, bf16[46,16,512]{2,1,0:T(8,128)(2,1)S(1)}, u32[]{:S(2)}, u32[]{:S(2)}) collective-permute-start(bf16[46,16,512]{2,1,0:T(8,128)(2,1)} %get-tuple-element.87), channel_id=1, source_target_pairs={{0,16},{16,0},{1,17},{17,1},{2,18},{18,2},{3,19},{19,3},{4,20},{20... | collective-permute-start | bytes 2261000 | tf_op jit(solution)/shard_map/ppermute | solution.py:34
  93.1 8.2 %collective-permute-start.11 = (bf16[2,400,128]{2,1,0:T(8,128)(2,1)}, bf16[2,400,128]{2,1,0:T(8,128)(2,1)S(1)}, u32[]{:S(2)}, u32[]{:S(2)}) collective-permute-start(bf16[2,400,128]{2,1,0:T(8,128)(2,1)} %get-tuple-element.84), channel_id=1, source_target_pairs={{0,2},{2,4},{4,6},{6,0},{1,3},{3,5},{5,7},{7,1},{8,10},{10,12},{12... | collective-permute-start | bytes 614408 | tf_op jit(solution)/shard_map/ppermute | solution.py:630
  93.1 8.2 %collective-permute-start.12 = (bf16[2,400,128]{2,1,0:T(8,128)(2,1)}, bf16[2,400,128]{2,1,0:T(8,128)(2,1)S(1)}, u32[]{:S(2)}, u32[]{:S(2)}) collective-permute-start(bf16[2,400,128]{2,1,0:T(8,128)(2,1)} %get-tuple-element.85), channel_id=1, source_target_pairs={{0,4},{2,6},{4,0},{6,2},{1,5},{3,7},{5,1},{7,3},{8,12},{10,14},{12... | collective-permute-start | bytes 614408 | tf_op jit(solution)/shard_map/ppermute | solution.py:630
  95.0 7.3 %collective-permute-start.13 = (bf16[2,400,128]{2,1,0:T(8,128)(2,1)}, bf16[2,400,128]{2,1,0:T(8,128)(2,1)S(1)}, u32[]{:S(2)}, u32[]{:S(2)}) collective-permute-start(bf16[2,400,128]{2,1,0:T(8,128)(2,1)} %get-tuple-element.86), channel_id=1, source_target_pairs={{0,6},{2,0},{4,2},{6,4},{1,7},{3,1},{5,3},{7,5},{8,14},{10,8},{12,... | collective-permute-start | bytes 614408 | tf_op jit(solution)/shard_map/ppermute | solution.py:630
  103.2 20.3 %copy-start.12 = (bf16[46,16,512]{2,1,0:T(8,128)(2,1)}, bf16[46,16,512]{2,1,0:T(8,128)(2,1)S(1)}, u32[]{:S(2)}) copy-start(bf16[46,16,512]{2,1,0:T(8,128)(2,1)S(1)} %collective-permute-done.14.refs_2_) | copy-start | bytes 2260996
  103.2 5.1 %collective-permute-start.15 = (bf16[400,128]{1,0:T(8,128)(2,1)S(1)}, bf16[400,128]{1,0:T(8,128)(2,1)S(1)}, u32[]{:S(2)}, u32[]{:S(2)}) collective-permute-start(bf16[400,128]{1,0:T(8,128)(2,1)S(1)} %fusion.1), channel_id=1, source_target_pairs={{0,8},{8,0},{1,9},{9,1},{2,10},{10,2},{3,11},{11,3},{4,12},{12,4},... | collective-permute-start | bytes 307208 | tf_op jit(solution)/shard_map/ppermute | solution.py:34
  108.3 0.9 copy-start.4
  110.1 10.5 %collective-permute-start.16 = (bf16[16,16,512]{2,1,0:T(8,128)(2,1)}, bf16[16,16,512]{2,1,0:T(8,128)(2,1)}, u32[]{:S(2)}, u32[]{:S(2)}) collective-permute-start(bf16[16,16,512]{2,1,0:T(8,128)(2,1)} %get-tuple-element.92), channel_id=1, source_target_pairs={{0,16},{16,0},{1,17},{17,1},{2,18},{18,2},{3,19},{19,3},{4,20},{20... | collective-permute-start | bytes 786440 | tf_op jit(solution)/shard_map/ppermute | solution.py:34
  120.6 14.2 %copy-start.9 = (s32[4]{0:T(128)S(1)}, s32[4]{0:T(128)}, u32[]{:S(2)}) copy-start(s32[4]{0:T(128)} %pad_add_fusion.c_ref.refs_0_.where_ref) | copy-start | bytes 52
  135.5 14.9 %collective-permute-start.17 = (bf16[2,128,128]{2,1,0:T(8,128)(2,1)S(1)}, bf16[2,128,128]{2,1,0:T(8,128)(2,1)S(1)}, u32[]{:S(2)}, u32[]{:S(2)}) collective-permute-start(bf16[2,128,128]{2,1,0:T(8,128)(2,1)S(1)} %get-tuple-element.97), channel_id=1, source_target_pairs={{0,1},{1,0},{2,3},{3,2},{4,5},{5,4},{6,7},{7,6},{8,9},{9,8},{10,11... | collective-permute-start | bytes 196616 | tf_op jit(solution)/shard_map/ppermute | solution.py:34
  151.6 8.9 %all-to-all-start.6 = ((bf16[8,64,128]{2,1,0:T(8,128)(2,1)}), bf16[8,64,128]{2,1,0:T(8,128)(2,1)S(1)}, u32[]{:S(2)}, u32[]{:S(2)}) async-start(bf16[8,64,128]{2,1,0:T(8,128)(2,1)} %arrange.1), calls=%async_computation.6 | async-start | bytes 262144 | tf_op jit(solution)/shard_map/all_to_all | solution.py:38
  160.5 0.6 copy-start.13

commit v5 on v4

--- a/solution.py
+++ b/solution.py
@@ -590,7 +590,7 @@
         ],
         scratch_shapes=[pltpu.VMEM((2, 16, 512), BF), pltpu.SemaphoreType.DMA],
         input_output_aliases={6: 1},
-        compiler_params=params(),
+        compiler_params=params(SMALL),
         name="final",
     )(where, parents, received, poles, own, oth, fir)
 

time: 165 us -> 164 us (level)
    unnamed x32 -> x38, local copies, waits for them, and re-layouts: 3.47 us -> 3.29 us
  transfers between devices with their start and end apart: 20 -> 20, of which waited for: 10 -> 10; matrix products, arithmetic and copies ran while one was open for 2% -> 2% of each run, Pallas kernels for 15% -> 16%
where the time goes in v5:
time: 164 us; the launch traced here: 163 us
  blocking collectives  55.8 us (34%)
  starting transfers between devices  42 us (26%)
  Pallas kernels  36.9 us (22%)
  waiting for transfers between devices  21.4 us (13%)
  local copies, waits for them, and re-layouts  3.29 us (2%)
  other arithmetic  2.57 us (2%)
    all_to_all x5, blocking collectives, exchange(): return lax.all_to_all(value, axes, 0, 0, tiled=True)  55.8 us
    ppermute x12, starting transfers between devices, swap(): return lax.ppermute(value, axis, [(0, 1), (1, 0)])  25 us
    ppermute x6, waiting for transfers between devices, scatter(): terms[s] = lax.ppermute(terms[s], 'z', [(z, (z + s) % 4) for z in range(4)])  13.3 us
    all_to_all x2, starting transfers between devices, exchange(): return lax.all_to_all(value, axes, 0, 0, tiled=True)  8.57 us
    ppermute x6, starting transfers between devices, scatter(): terms[s] = lax.ppermute(terms[s], 'z', [(z, (z + s) % 4) for z in range(4)])  8.46 us
    ppermute x12, waiting for transfers between devices, swap(): return lax.ppermute(value, axis, [(0, 1), (1, 0)])  6.5 us
    pallas_call x1, Pallas kernels, project_embed(): pl.pallas_call(embed_kernel, grid=(2,), in_specs=[SMEM, whole(8, 80, 128)...  5.93 us
    pallas_call x2, Pallas kernels, project_out(): pl.pallas_call(out_kernel, grid=(2,), in_specs=[SMEM, whole(8, 128, 128),...  5.88 us
  transfers between devices with their start and end apart: 20, of which 10 were waited for; matrix products, arithmetic and copies ran while one was open for 2% of the time, Pallas kernels for 16%

profile of v5, /device:TPU:1, one launch (start us, length us, event | category | flops | bytes accessed | tf_op | source)
XLA Modules:
  0.0 162.7 jit_solution(9472478988948633407)
XLA Ops:
  0.6 1.5 collective-permute-start
  2.2 4.5 %state_sums.1 = (bf16[8,80,128]{2,1,0:T(8,128)(2,1)}, bf16[57,16,512]{2,1,0:T(8,128)(2,1)}, bf16[22,16,512]{2,1,0:T(8,128)(2,1)}, bf16[46,16,512]{2,1,0:T(8,128)(2,1)}, bf16[16,16,512]{2,1,0:T(8,128)(2,1)}) custom-call(s32[2,16]{1,0:T(2,128)} %tok_ref.1, f32[32,128]{1,0:T(8,128)} %filt_ref.1, f32[16,512]{1,0:T(8,128)} %poles_ref.3, f32[16,512]{1,0:T(8,128)} %res_ref.1, ...), custom_call_target="tpu_custom_call" | custom-call | tf_op jit(solution)/shard_map/state_sums/pallas_call | solution.py:116
  7.3 5.2 %all-to-all-start = ((bf16[8,80,128]{2,1,0:T(8,128)(2,1)}), bf16[8,80,128]{2,1,0:T(8,128)(2,1)S(1)}, u32[]{:S(2)}, u32[]{:S(2)}) async-start(bf16[8,80,128]{2,1,0:T(8,128)(2,1)} %get-tuple-element.59), calls=%async_computation | async-start | bytes 327680 | tf_op jit(solution)/shard_map/all_to_all | solution.py:38
  12.6 0.7 pad_add_fusion.c_ref.refs_0_.where_ref
  13.2 1.8 %indices.1.refs_8_ = s32[8,128]{1,0:T(8,128)} custom-call(s32[4]{0:T(128)} %pad_add_fusion.c_ref.refs_0_.where_ref, s32[2,128]{1,0:T(2,128)} %par_ref.5), custom_call_target="tpu_custom_call" | custom-call | tf_op jit(solution)/shard_map/indices/pallas_call | solution.py:160
  15.0 2.5 %turn.1.tables = bf16[2,512,512]{2,1,0:T(8,128)(2,1)} custom-call(bf16[512,512]{1,0:T(8,128)(2,1)} %own_ref.2, bf16[512,512]{1,0:T(8,128)(2,1)} %copy-done.17), custom_call_target="tpu_custom_call" | custom-call | tf_op jit(solution)/shard_map/turn/pallas_call | solution.py:177
  17.5 0.7 all-to-all-done.got_ref.refs_6_
  18.2 0.8 collective-permute-start.6
  19.1 5.9 %embed_project.1 = (bf16[2,400,128]{2,1,0:T(8,128)(2,1)}, bf16[2,400,128]{2,1,0:T(8,128)(2,1)}, bf16[2,400,128]{2,1,0:T(8,128)(2,1)}, bf16[2,400,128]{2,1,0:T(8,...) custom-call(s32[4]{0:T(128)} %pad_add_fusion.c_ref.refs_0_.where_ref, bf16[8,80,128]{2,1,0:T(8,128)(2,1)} %copy-done, ...), custom_call_target="tpu_custom_call" | custom-call | flops 805306368 | bytes 7340032 | tf_op jit(solution)/shard_map/embed_project/pallas_call | solution.py:258
  25.0 1.7 %collective-permute-start.3 = (bf16[2,400,128]{2,1,0:T(8,128)(2,1)}, bf16[2,400,128]{2,1,0:T(8,128)(2,1)S(1)}, u32[]{:S(2)}, u32[]{:S(2)}) collective-permute-start(bf16[2,400,128]{2,1,0:T(8,128)(2,1)} %get-tuple-element.67), channel_id=1, source_target_pairs={{0,2},{2,4},{4,6},{6,0},{1,3},{3,5},{5,7},{7,1},{8,10},{10,12},{12... | collective-permute-start | bytes 614408 | tf_op jit(solution)/shard_map/ppermute | solution.py:630
  26.7 3.3 %collective-permute-start.4 = (bf16[2,400,128]{2,1,0:T(8,128)(2,1)}, bf16[2,400,128]{2,1,0:T(8,128)(2,1)S(1)}, u32[]{:S(2)}, u32[]{:S(2)}) collective-permute-start(bf16[2,400,128]{2,1,0:T(8,128)(2,1)} %get-tuple-element.68), channel_id=1, source_target_pairs={{0,4},{2,6},{4,0},{6,2},{1,5},{3,7},{5,1},{7,3},{8,12},{10,14},{12... | collective-permute-start | bytes 614408 | tf_op jit(solution)/shard_map/ppermute | solution.py:630
  30.0 0.7 collective-permute-start.5
  30.7 1.9 %collective-permute-done.3.refs_2_ = bf16[2,400,128]{2,1,0:T(8,128)(2,1)S(1)} collective-permute-done((bf16[2,400,128]{2,1,0:T(8,128)(2,1)}, bf16[2,400,128]{2,1,0:T(8,128)(2,1)S(1)}, u32[]{:S(2)}, u32[]{:S(2)}) %collective-permute-start.3) | collective-permute-done | bytes 204832 | tf_op jit(solution)/shard_map/ppermute | solution.py:630
  32.6 5.0 %collective-permute-done.4.refs_3_ = bf16[2,400,128]{2,1,0:T(8,128)(2,1)S(1)} collective-permute-done((bf16[2,400,128]{2,1,0:T(8,128)(2,1)}, bf16[2,400,128]{2,1,0:T(8,128)(2,1)S(1)}, u32[]{:S(2)}, u32[]{:S(2)}) %collective-permute-start.4) | collective-permute-done | bytes 204832 | tf_op jit(solution)/shard_map/ppermute | solution.py:630
  37.6 1.0 fusion
  38.8 2.5 %collective-permute-start.7 = (bf16[400,128]{1,0:T(8,128)(2,1)S(1)}, bf16[400,128]{1,0:T(8,128)(2,1)S(1)}, u32[]{:S(2)}, u32[]{:S(2)}) collective-permute-start(bf16[400,128]{1,0:T(8,128)(2,1)S(1)} %fusion), channel_id=1, source_target_pairs={{0,8},{8,0},{1,9},{9,1},{2,10},{10,2},{3,11},{11,3},{4,12},{12,4},... | collective-permute-start | bytes 307208 | tf_op jit(solution)/shard_map/ppermute | solution.py:34
  41.3 3.2 %collective-permute-start.8 = (bf16[4,64,128]{2,1,0:T(8,128)(2,1)}, bf16[4,64,128]{2,1,0:T(8,128)(2,1)S(1)}, u32[]{:S(2)}, u32[]{:S(2)}) collective-permute-start(bf16[4,64,128]{2,1,0:T(8,128)(2,1)} %get-tuple-element.72), channel_id=1, source_target_pairs={{0,1},{1,0},{2,3},{3,2},{4,5},{5,4},{6,7},{7,6},{8,9},{9,8},{10,11... | collective-permute-start | bytes 196616 | tf_op jit(solution)/shard_map/ppermute | solution.py:34
  44.4 1.1 collective-permute-done.8.refs_7_
  45.6 0.9 copy-done.1
  46.5 0.9 copy-done.4
  47.4 0.8 mix.2
  48.4 12.6 %all_to_all.35.a_ref = bf16[8,128,128]{2,1,0:T(8,128)(2,1)} all-to-all(bf16[8,128,128]{2,1,0:T(8,128)(2,1)S(1)} %get-tuple-element.76), channel_id=1, replica_groups=mesh['y'=4,'xl'=2,'xh'=2,'z'=4,'c'=2] {'y','xl'}, dimensions={0} | all-to-all | bytes 524288 | tf_op jit(solution)/shard_map/all_to_all | solution.py:38
  61.0 3.0 %project_out.2 = bf16[8,128,128]{2,1,0:T(8,128)(2,1)} custom-call(s32[4]{0:T(128)} %pad_add_fusion.c_ref.refs_0_.where_ref, bf16[8,128,128]{2,1,0:T(8,128)(2,1)} %all_to_all.35.a_ref, bf16[2,1024,512]{2,1,0:T(8,128)(2,1)} %bitcast.16, bf16[2,1024,512]{2,1,0:T(8,128)(2,1)} %collective-permute-done.10.w_oth), custom_call_target="tpu_custom_call" | custom-call | flops 268435456 | bytes 2621440 | tf_op jit(solution)/shard_map/project_out/pallas_call | solution.py:392
  63.9 13.5 %all_to_all.36.r_ref = bf16[8,128,128]{2,1,0:T(8,128)(2,1)S(1)} all-to-all(bf16[8,128,128]{2,1,0:T(8,128)(2,1)} %project_out.2), channel_id=1, replica_groups=mesh['y'=4,'xl'=2,'xh'=2,'z'=4,'c'=2] {'xh','z'}, dimensions={0} | all-to-all | bytes 524288 | tf_op jit(solution)/shard_map/all_to_all | solution.py:38
  77.5 0.6 residual.1.h_ref
  78.1 9.2 %all_to_all.37.a_ref = bf16[8,128,128]{2,1,0:T(8,128)(2,1)} all-to-all(bf16[8,128,128]{2,1,0:T(8,128)(2,1)S(1)} %residual.1.h_ref), channel_id=1, replica_groups=mesh['y'=4,'xl'=2,'xh'=2,'z'=4,'c'=2] {'y','xl'}, dimensions={0} | all-to-all | bytes 524288 | tf_op jit(solution)/shard_map/all_to_all | solution.py:38
  87.3 0.6 collective-permute-start.14
  87.9 5.3 %norm_project.1 = (bf16[2,400,128]{2,1,0:T(8,128)(2,1)}, bf16[2,400,128]{2,1,0:T(8,128)(2,1)}, bf16[2,400,128]{2,1,0:T(8,128)(2,1)}, bf16[2,400,128]{2,1,0:T(8,128)(2,1)}) custom-call(s32[4]{0:T(128)} %pad_add_fusion.c_ref.refs_0_.where_ref, bf16[8,128,128]{2,1,0:T(8,128)(2,1)} %all_to_all.37.a_ref, f32[2,512]{1,0:T(2,128)} %g_own.3, f32[2,512]{1,0:T(2,128)} %copy-done.18, ...), custom_call_target="tpu_custom_call" | custom-call | flops 805306368 | bytes 7340032 | tf_op jit(solution)/shard_map/norm_project/pallas_call | solution.py:299
  93.2 1.9 %collective-permute-start.12 = (bf16[2,400,128]{2,1,0:T(8,128)(2,1)}, bf16[2,400,128]{2,1,0:T(8,128)(2,1)S(1)}, u32[]{:S(2)}, u32[]{:S(2)}) collective-permute-start(bf16[2,400,128]{2,1,0:T(8,128)(2,1)} %get-tuple-element.85), channel_id=1, source_target_pairs={{0,4},{2,6},{4,0},{6,2},{1,5},{3,7},{5,1},{7,3},{8,12},{10,14},{12... | collective-permute-start | bytes 614408 | tf_op jit(solution)/shard_map/ppermute | solution.py:630
  95.0 0.9 collective-permute-start.13
  95.9 5.5 %collective-permute-done.11.refs_2_ = bf16[2,400,128]{2,1,0:T(8,128)(2,1)S(1)} collective-permute-done((bf16[2,400,128]{2,1,0:T(8,128)(2,1)}, bf16[2,400,128]{2,1,0:T(8,128)(2,1)S(1)}, u32[]{:S(2)}, u32[]{:S(2)}) %collective-permute-start.11) | collective-permute-done | bytes 204832 | tf_op jit(solution)/shard_map/ppermute | solution.py:630
  101.4 0.9 collective-permute-done.13.refs_4_
  102.3 1.0 fusion.1
  104.1 4.2 %collective-permute-done.15.refs_5_ = bf16[400,128]{1,0:T(8,128)(2,1)S(1)} collective-permute-done((bf16[400,128]{1,0:T(8,128)(2,1)S(1)}, bf16[400,128]{1,0:T(8,128)(2,1)S(1)}, u32[]{:S(2)}, u32[]{:S(2)}) %collective-permute-start.15) | collective-permute-done | bytes 102432 | tf_op jit(solution)/shard_map/ppermute | solution.py:34
  108.4 0.9 copy-done.5
  109.3 0.8 mix.3
  110.2 1.3 collective-permute-start.16
  111.4 9.2 %all_to_all.38.a_ref = bf16[8,128,128]{2,1,0:T(8,128)(2,1)} all-to-all(bf16[8,128,128]{2,1,0:T(8,128)(2,1)S(1)} %get-tuple-element.91), channel_id=1, replica_groups=mesh['y'=4,'xl'=2,'xh'=2,'z'=4,'c'=2] {'y','xl'}, dimensions={0} | all-to-all | bytes 524288 | tf_op jit(solution)/shard_map/all_to_all | solution.py:38
  120.6 2.9 %project_out.3 = bf16[8,128,128]{2,1,0:T(8,128)(2,1)} custom-call(s32[4]{0:T(128)} %pad_add_fusion.c_ref.refs_0_.where_ref, bf16[8,128,128]{2,1,0:T(8,128)(2,1)} %all_to_all.38.a_ref, bf16[2,1024,512]{2,1,0:T(8,128)(2,1)} %bitcast.17, bf16[2,1024,512]{2,1,0:T(8,128)(2,1)} %collective-permute-done.10.w_oth), custom_call_target="tpu_custom_call" | custom-call | flops 268435456 | bytes 2621440 | tf_op jit(solution)/shard_map/project_out/pallas_call | solution.py:392
  123.5 11.2 %all_to_all.39.r_ref = bf16[8,128,128]{2,1,0:T(8,128)(2,1)S(1)} all-to-all(bf16[8,128,128]{2,1,0:T(8,128)(2,1)} %project_out.3), channel_id=1, replica_groups=mesh['y'=4,'xl'=2,'xh'=2,'z'=4,'c'=2] {'xh','z'}, dimensions={0} | all-to-all | bytes 524288 | tf_op jit(solution)/shard_map/all_to_all | solution.py:38
  134.8 0.7 last.1
  135.5 13.9 %collective-permute-start.17 = (bf16[2,128,128]{2,1,0:T(8,128)(2,1)S(1)}, bf16[2,128,128]{2,1,0:T(8,128)(2,1)S(1)}, u32[]{:S(2)}, u32[]{:S(2)}) collective-permute-start(bf16[2,128,128]{2,1,0:T(8,128)(2,1)S(1)} %get-tuple-element.97), channel_id=1, source_target_pairs={{0,1},{1,0},{2,3},{3,2},{4,5},{5,4},{6,7},{7,6},{8,9},{9,8},{10,11... | collective-permute-start | bytes 196616 | tf_op jit(solution)/shard_map/ppermute | solution.py:34
  149.5 0.9 collective-permute-done.17.got_ref
  150.4 1.2 arrange.1
  151.6 3.4 %all-to-all-start.6 = ((bf16[8,64,128]{2,1,0:T(8,128)(2,1)}), bf16[8,64,128]{2,1,0:T(8,128)(2,1)S(1)}, u32[]{:S(2)}, u32[]{:S(2)}) async-start(bf16[8,64,128]{2,1,0:T(8,128)(2,1)} %arrange.1), calls=%async_computation.6 | async-start | bytes 262144 | tf_op jit(solution)/shard_map/all_to_all | solution.py:38
  155.0 4.6 %reorder.1.fir_ref = bf16[127,16,512]{2,1,0:T(8,128)(2,1)} custom-call(s32[4]{0:T(128)} %pad_add_fusion.c_ref.refs_0_.where_ref, s32[2,128]{1,0:T(2,128)} %par_ref.5, bf16[127,16,512]{2,1,0:T(8,128)(2,1)} %bitcast.19, bf16[57,16,512]{2,1,0:T(8,128)(2,1)} %copy-done.15, bf16[22,16,512]{2,1,0:T(8,128)(2,1)} %collective-permute-done.9.refs_1_, ...), custom_call_target="tpu_custom_call" | custom-call | flops 536870912 | bytes 6291456 | tf_op jit(solution)/shard_map/reorder/pallas_call | solution.py:538
  159.7 0.9 all-to-all-done.6.r_ref
  160.6 2.2 %final.1 = (bf16[2,16,512]{2,1,0:T(8,128)(2,1)}, bf16[127,16,512]{2,1,0:T(8,128)(2,1)}, f32[16,16,512]{2,1,0:T(8,128)}) custom-call(s32[4]{0:T(128)S(1)} %copy-done.12, s32[2,128]{1,0:T(2,128)S(1)} %copy-done.14, bf16[8,64,128]{2,1,0:T(8,128)(2,1)S(1)} %all-to-all-done.6.r_ref, f32[16,512]{1,0:T(8,128)S(1)} %copy-done.7, ...), custom_call_target="tpu_custom_call", output_to_operand_aliasing={{1}: (6, {})} | custom-call | tf_op jit(solution)/shard_map/final/pallas_call | solution.py:578
  (52 shorter events, 2.0 us)
Async XLA Ops:
  0.6 6.1 %collective-permute-start = (bf16[512,512]{1,0:T(8,128)(2,1)}, bf16[512,512]{1,0:T(8,128)(2,1)S(1)}, u32[]{:S(2)}, u32[]{:S(2)}) collective-permute-start(bf16[512,512]{1,0:T(8,128)(2,1)} %own_ref.2), channel_id=1, source_target_pairs={{0,1},{1,0},{2,3},{3,2},{4,5},{5,4},{6,7},{7,6},{8,9},{9,8},{10,11... | collective-permute-start | bytes 1572872 | tf_op jit(solution)/shard_map/ppermute | solution.py:34
  2.1 4.6 %collective-permute-start.1 = (f32[2,512]{1,0:T(2,128)}, f32[2,512]{1,0:T(2,128)S(1)}, u32[]{:S(2)}, u32[]{:S(2)}) collective-permute-start(f32[2,512]{1,0:T(2,128)} %g_own.3), channel_id=1, source_target_pairs={{0,1},{1,0},{2,3},{3,2},{4,5},{5,4},{6,7},{7,6},{8,9},{9,8},{10,11... | collective-permute-start | bytes 12296 | tf_op jit(solution)/shard_map/ppermute | solution.py:34
  6.7 12.3 %copy-start.18 = (f32[2,512]{1,0:T(2,128)}, f32[2,512]{1,0:T(2,128)S(1)}, u32[]{:S(2)}) copy-start(f32[2,512]{1,0:T(2,128)S(1)} %collective-permute-done.1.g_oth) | copy-start | bytes 12292
  6.7 8.2 %copy-start.17 = (bf16[512,512]{1,0:T(8,128)(2,1)}, bf16[512,512]{1,0:T(8,128)(2,1)S(1)}, u32[]{:S(2)}) copy-start(bf16[512,512]{1,0:T(8,128)(2,1)S(1)} %collective-permute-done.oth_ref) | copy-start | bytes 1572868
  6.8 12.3 %collective-permute-start.2 = (bf16[2,3072,512]{2,1,0:T(8,128)(2,1)}, bf16[2,3072,512]{2,1,0:T(8,128)(2,1)}, u32[]{:S(2)}, u32[]{:S(2)}) collective-permute-start(bf16[2,3072,512]{2,1,0:T(8,128)(2,1)} %bitcast.12), channel_id=1, source_target_pairs={{0,1},{1,0},{2,3},{3,2},{4,5},{5,4},{6,7},{7,6},{8,9},{9,8},{10,11... | collective-permute-start | bytes 18874376 | tf_op jit(solution)/shard_map/ppermute | solution.py:34
  7.3 53.7 %collective-permute-start.10 = (bf16[2,1024,512]{2,1,0:T(8,128)(2,1)}, bf16[2,1024,512]{2,1,0:T(8,128)(2,1)}, u32[]{:S(2)}, u32[]{:S(2)}) collective-permute-start(bf16[2,1024,512]{2,1,0:T(8,128)(2,1)} %bitcast.15), channel_id=1, source_target_pairs={{0,1},{1,0},{2,3},{3,2},{4,5},{5,4},{6,7},{7,6},{8,9},{9,8},{10,11... | collective-permute-start | bytes 6291464 | tf_op jit(solution)/shard_map/ppermute | solution.py:34
  7.3 10.9 %all-to-all-start = ((bf16[8,80,128]{2,1,0:T(8,128)(2,1)}), bf16[8,80,128]{2,1,0:T(8,128)(2,1)S(1)}, u32[]{:S(2)}, u32[]{:S(2)}) async-start(bf16[8,80,128]{2,1,0:T(8,128)(2,1)} %get-tuple-element.59), calls=%async_computation | async-start | bytes 327680 | tf_op jit(solution)/shard_map/all_to_all | solution.py:38
  18.2 0.8 copy-start
  18.2 27.3 %copy-start.8 = (s32[4]{0:T(128)S(1)}, s32[4]{0:T(128)}, u32[]{:S(2)}) copy-start(s32[4]{0:T(128)} %pad_add_fusion.c_ref.refs_0_.where_ref) | copy-start | bytes 52
  18.2 27.3 %copy-start.13 = (s32[8,128]{1,0:T(8,128)S(1)}, s32[8,128]{1,0:T(8,128)}, u32[]{:S(2)}) copy-start(s32[8,128]{1,0:T(8,128)} %indices.1.refs_8_) | copy-start | bytes 12292
  18.2 20.6 %collective-permute-start.6 = (bf16[57,16,512]{2,1,0:T(8,128)(2,1)}, bf16[57,16,512]{2,1,0:T(8,128)(2,1)S(1)}, u32[]{:S(2)}, u32[]{:S(2)}) collective-permute-start(bf16[57,16,512]{2,1,0:T(8,128)(2,1)} %get-tuple-element.70), channel_id=1, source_target_pairs={{0,16},{16,0},{1,17},{17,1},{2,18},{18,2},{3,19},{19,3},{4,20},{20... | collective-permute-start | bytes 2801672 | tf_op jit(solution)/shard_map/ppermute | solution.py:34
  25.0 7.6 %collective-permute-start.3 = (bf16[2,400,128]{2,1,0:T(8,128)(2,1)}, bf16[2,400,128]{2,1,0:T(8,128)(2,1)S(1)}, u32[]{:S(2)}, u32[]{:S(2)}) collective-permute-start(bf16[2,400,128]{2,1,0:T(8,128)(2,1)} %get-tuple-element.67), channel_id=1, source_target_pairs={{0,2},{2,4},{4,6},{6,0},{1,3},{3,5},{5,7},{7,1},{8,10},{10,12},{12... | collective-permute-start | bytes 614408 | tf_op jit(solution)/shard_map/ppermute | solution.py:630
  26.7 10.9 %collective-permute-start.4 = (bf16[2,400,128]{2,1,0:T(8,128)(2,1)}, bf16[2,400,128]{2,1,0:T(8,128)(2,1)S(1)}, u32[]{:S(2)}, u32[]{:S(2)}) collective-permute-start(bf16[2,400,128]{2,1,0:T(8,128)(2,1)} %get-tuple-element.68), channel_id=1, source_target_pairs={{0,4},{2,6},{4,0},{6,2},{1,5},{3,7},{5,1},{7,3},{8,12},{10,14},{12... | collective-permute-start | bytes 614408 | tf_op jit(solution)/shard_map/ppermute | solution.py:630
  30.0 7.6 %collective-permute-start.5 = (bf16[2,400,128]{2,1,0:T(8,128)(2,1)}, bf16[2,400,128]{2,1,0:T(8,128)(2,1)S(1)}, u32[]{:S(2)}, u32[]{:S(2)}) collective-permute-start(bf16[2,400,128]{2,1,0:T(8,128)(2,1)} %get-tuple-element.69), channel_id=1, source_target_pairs={{0,6},{2,0},{4,2},{6,4},{1,7},{3,1},{5,3},{7,5},{8,14},{10,8},{12,... | collective-permute-start | bytes 614408 | tf_op jit(solution)/shard_map/ppermute | solution.py:630
  38.8 9.6 %copy-start.15 = (bf16[57,16,512]{2,1,0:T(8,128)(2,1)}, bf16[57,16,512]{2,1,0:T(8,128)(2,1)S(1)}, u32[]{:S(2)}) copy-start(bf16[57,16,512]{2,1,0:T(8,128)(2,1)S(1)} %collective-permute-done.6.refs_0_) | copy-start | bytes 2801668
  38.8 6.7 %collective-permute-start.7 = (bf16[400,128]{1,0:T(8,128)(2,1)S(1)}, bf16[400,128]{1,0:T(8,128)(2,1)S(1)}, u32[]{:S(2)}, u32[]{:S(2)}) collective-permute-start(bf16[400,128]{1,0:T(8,128)(2,1)S(1)} %fusion), channel_id=1, source_target_pairs={{0,8},{8,0},{1,9},{9,1},{2,10},{10,2},{3,11},{11,3},{4,12},{12,4},... | collective-permute-start | bytes 307208 | tf_op jit(solution)/shard_map/ppermute | solution.py:34
  41.3 4.3 %collective-permute-start.8 = (bf16[4,64,128]{2,1,0:T(8,128)(2,1)}, bf16[4,64,128]{2,1,0:T(8,128)(2,1)S(1)}, u32[]{:S(2)}, u32[]{:S(2)}) collective-permute-start(bf16[4,64,128]{2,1,0:T(8,128)(2,1)} %get-tuple-element.72), channel_id=1, source_target_pairs={{0,1},{1,0},{2,3},{3,2},{4,5},{5,4},{6,7},{7,6},{8,9},{9,8},{10,11... | collective-permute-start | bytes 196616 | tf_op jit(solution)/shard_map/ppermute | solution.py:34
  45.6 0.9 copy-start.1
  46.5 0.9 copy-start.4
  48.2 12.7 %collective-permute-start.9 = (bf16[22,16,512]{2,1,0:T(8,128)(2,1)}, bf16[22,16,512]{2,1,0:T(8,128)(2,1)}, u32[]{:S(2)}, u32[]{:S(2)}) collective-permute-start(bf16[22,16,512]{2,1,0:T(8,128)(2,1)} %get-tuple-element.77), channel_id=1, source_target_pairs={{0,16},{16,0},{1,17},{17,1},{2,18},{18,2},{3,19},{19,3},{4,20},{20... | collective-permute-start | bytes 1081352 | tf_op jit(solution)/shard_map/ppermute | solution.py:34
  61.0 16.5 %copy-start.6 = (bf16[2,512,128]{2,1,0:T(8,128)(2,1)S(1)}, bf16[2,512,128]{2,1,0:T(8,128)(2,1)}, u32[]{:S(2)}) copy-start(bf16[2,512,128]{2,1,0:T(8,128)(2,1)} %get-tuple-element.80.x_ref) | copy-start | bytes 786436
  61.0 16.5 %copy-start.9 = (s32[4]{0:T(128)S(1)}, s32[4]{0:T(128)}, u32[]{:S(2)}) copy-start(s32[4]{0:T(128)} %pad_add_fusion.c_ref.refs_0_.where_ref) | copy-start | bytes 52
  87.3 21.1 %copy-start.2 = (bf16[8,80,128]{2,1,0:T(8,128)(2,1)S(1)}, bf16[8,80,128]{2,1,0:T(8,128)(2,1)}, u32[]{:S(2)}) copy-start(bf16[8,80,128]{2,1,0:T(8,128)(2,1)} %copy-done) | copy-start | bytes 491524
  87.3 21.1 %copy-start.10 = (s32[4]{0:T(128)S(1)}, s32[4]{0:T(128)}, u32[]{:S(2)}) copy-start(s32[4]{0:T(128)} %pad_add_fusion.c_ref.refs_0_.where_ref) | copy-start | bytes 52
  87.3 16.0 %collective-permute-start.14 = (bf16[46,16,512]{2,1,0:T(8,128)(2,1)}, bf16[46,16,512]{2,1,0:T(8,128)(2,1)S(1)}, u32[]{:S(2)}, u32[]{:S(2)}) collective-permute-start(bf16[46,16,512]{2,1,0:T(8,128)(2,1)} %get-tuple-element.87), channel_id=1, source_target_pairs={{0,16},{16,0},{1,17},{17,1},{2,18},{18,2},{3,19},{19,3},{4,20},{20... | collective-permute-start | bytes 2261000 | tf_op jit(solution)/shard_map/ppermute | solution.py:34
  93.2 8.2 %collective-permute-start.11 = (bf16[2,400,128]{2,1,0:T(8,128)(2,1)}, bf16[2,400,128]{2,1,0:T(8,128)(2,1)S(1)}, u32[]{:S(2)}, u32[]{:S(2)}) collective-permute-start(bf16[2,400,128]{2,1,0:T(8,128)(2,1)} %get-tuple-element.84), channel_id=1, source_target_pairs={{0,2},{2,4},{4,6},{6,0},{1,3},{3,5},{5,7},{7,1},{8,10},{10,12},{12... | collective-permute-start | bytes 614408 | tf_op jit(solution)/shard_map/ppermute | solution.py:630
  93.2 8.2 %collective-permute-start.12 = (bf16[2,400,128]{2,1,0:T(8,128)(2,1)}, bf16[2,400,128]{2,1,0:T(8,128)(2,1)S(1)}, u32[]{:S(2)}, u32[]{:S(2)}) collective-permute-start(bf16[2,400,128]{2,1,0:T(8,128)(2,1)} %get-tuple-element.85), channel_id=1, source_target_pairs={{0,4},{2,6},{4,0},{6,2},{1,5},{3,7},{5,1},{7,3},{8,12},{10,14},{12... | collective-permute-start | bytes 614408 | tf_op jit(solution)/shard_map/ppermute | solution.py:630
  95.0 7.3 %collective-permute-start.13 = (bf16[2,400,128]{2,1,0:T(8,128)(2,1)}, bf16[2,400,128]{2,1,0:T(8,128)(2,1)S(1)}, u32[]{:S(2)}, u32[]{:S(2)}) collective-permute-start(bf16[2,400,128]{2,1,0:T(8,128)(2,1)} %get-tuple-element.86), channel_id=1, source_target_pairs={{0,6},{2,0},{4,2},{6,4},{1,7},{3,1},{5,3},{7,5},{8,14},{10,8},{12,... | collective-permute-start | bytes 614408 | tf_op jit(solution)/shard_map/ppermute | solution.py:630
  103.3 0.9 copy-start.16
  103.3 5.1 %collective-permute-start.15 = (bf16[400,128]{1,0:T(8,128)(2,1)S(1)}, bf16[400,128]{1,0:T(8,128)(2,1)S(1)}, u32[]{:S(2)}, u32[]{:S(2)}) collective-permute-start(bf16[400,128]{1,0:T(8,128)(2,1)S(1)} %fusion.1), channel_id=1, source_target_pairs={{0,8},{8,0},{1,9},{9,1},{2,10},{10,2},{3,11},{11,3},{4,12},{12,4},... | collective-permute-start | bytes 307208 | tf_op jit(solution)/shard_map/ppermute | solution.py:34
  108.4 0.9 copy-start.5
  110.2 10.5 %collective-permute-start.16 = (bf16[16,16,512]{2,1,0:T(8,128)(2,1)}, bf16[16,16,512]{2,1,0:T(8,128)(2,1)S(1)}, u32[]{:S(2)}, u32[]{:S(2)}) collective-permute-start(bf16[16,16,512]{2,1,0:T(8,128)(2,1)} %get-tuple-element.92), channel_id=1, source_target_pairs={{0,16},{16,0},{1,17},{17,1},{2,18},{18,2},{3,19},{19,3},{4,20},{20... | collective-permute-start | bytes 786440 | tf_op jit(solution)/shard_map/ppermute | solution.py:34
  120.6 14.2 %copy-start.11 = (s32[4]{0:T(128)S(1)}, s32[4]{0:T(128)}, u32[]{:S(2)}) copy-start(s32[4]{0:T(128)} %pad_add_fusion.c_ref.refs_0_.where_ref) | copy-start | bytes 52
  135.5 14.8 %collective-permute-start.17 = (bf16[2,128,128]{2,1,0:T(8,128)(2,1)S(1)}, bf16[2,128,128]{2,1,0:T(8,128)(2,1)S(1)}, u32[]{:S(2)}, u32[]{:S(2)}) collective-permute-start(bf16[2,128,128]{2,1,0:T(8,128)(2,1)S(1)} %get-tuple-element.97), channel_id=1, source_target_pairs={{0,1},{1,0},{2,3},{3,2},{4,5},{5,4},{6,7},{7,6},{8,9},{9,8},{10,11... | collective-permute-start | bytes 196616 | tf_op jit(solution)/shard_map/ppermute | solution.py:34
  151.6 8.9 %all-to-all-start.6 = ((bf16[8,64,128]{2,1,0:T(8,128)(2,1)}), bf16[8,64,128]{2,1,0:T(8,128)(2,1)S(1)}, u32[]{:S(2)}, u32[]{:S(2)}) async-start(bf16[8,64,128]{2,1,0:T(8,128)(2,1)} %arrange.1), calls=%async_computation.6 | async-start | bytes 262144 | tf_op jit(solution)/shard_map/all_to_all | solution.py:38
  155.0 5.6 %copy-start.3 = (f32[16,16,512]{2,1,0:T(8,128)S(1)}, f32[16,16,512]{2,1,0:T(8,128)}, u32[]{:S(2)}) copy-start(f32[16,16,512]{2,1,0:T(8,128)} %own_ref.3) | copy-start | bytes 1572868
  155.0 5.5 %copy-start.7 = (f32[16,512]{1,0:T(8,128)S(1)}, f32[16,512]{1,0:T(8,128)}, u32[]{:S(2)}) copy-start(f32[16,512]{1,0:T(8,128)} %poles_ref.3) | copy-start | bytes 98308
  155.0 5.5 %copy-start.12 = (s32[4]{0:T(128)S(1)}, s32[4]{0:T(128)}, u32[]{:S(2)}) copy-start(s32[4]{0:T(128)} %pad_add_fusion.c_ref.refs_0_.where_ref) | copy-start | bytes 52
  155.0 5.5 %copy-start.14 = (s32[2,128]{1,0:T(2,128)S(1)}, s32[2,128]{1,0:T(2,128)}, u32[]{:S(2)}) copy-start(s32[2,128]{1,0:T(2,128)} %par_ref.5) | copy-start | bytes 3076
